TPU v7x, 32 devices: a whole 2x2x4 slice. The times are simulated.
32 devices in a mesh: row: 8 (over z, x), col: 4 (over y, core).
Axes of the slice: x: 2, y: 2, z: 4, core: 2. Of those that a mesh axis runs over, the one named last changes fastest.
Arguments:
- front: float32 [9216, 9216], P('row', 'col')
- child_tiles: float32 [4096, 4096], P(('row', 'col')), may hold values from -0.4375 to 0.4375
- tile_target: int32 [4096], P(('row', 'col')), may hold values from 0 to 20735, as said below
- tile_count: int32 [128], P(('row', 'col')), may hold values from 24 to 32
- probe: float32 [9216, 512], P('col'), may hold values from -1.75 to 1.75
Outputs:
- panel_factor: float32 [9216, 1024], P('row', 'col')
- sketch: float32 [9216, 512], P('row', 'col')
Inputs may be any that keep to these rules, and one draw needn't show every extreme that they name: `tile_target`: among the 128 slots of one device, live or not, each counted once at its target tile and once at the mirrored tile, at most 8 placements fall inside the block of the front held by any one device.
All inputs are finite; a program needn't handle non-finite values.
Results may differ from a plain program's by a relative error of at most 0.00015.
Values sent between devices are 32-bit elements; how exact they have to be, the bound alone decides.
No kernel may reach another device: no remote copies, remote signals or barrier semaphores. Data moves between devices by JAX's collectives and lax.ppermute only.
A program may use at most 128 MiB of HBM per device.

v0:
```python
import jax
import jax.numpy as jnp
from jax import lax
from jax.sharding import PartitionSpec as P

NB = 512
PANELS = 2
TB = 64
SLOTS = 32


HIGH = lax.Precision.HIGHEST


def broadcast(value, axis, root):
    mine = lax.axis_index(axis) == root
    return lax.psum(jnp.where(mine, value, jnp.zeros_like(value)), axis)


def per_device(front, child_tiles, tile_target, tile_count, probe):
    row_count = lax.axis_size("row")
    col_count = lax.axis_size("col")
    devices = row_count * col_count
    local_rows, local_cols = front.shape
    tile_rows = local_rows // TB
    tile_cols = local_cols // TB
    grid = tile_cols * col_count
    local_tiles = tile_rows * tile_cols
    held = child_tiles.shape[0]
    capacity = 2 * max(1, (held + devices - 1) // devices)
    slot_index = jnp.arange(held, dtype=jnp.int32)
    live_once = slot_index % SLOTS < tile_count[slot_index // SLOTS]
    live = jnp.concatenate([live_once, live_once])
    mirrored = child_tiles.reshape(held, TB, TB).transpose(0, 2, 1).reshape(held, TB * TB)
    placements = jnp.concatenate([child_tiles, mirrored], axis=0)
    first_row = tile_target // grid
    first_col = tile_target % grid
    target_row = jnp.concatenate([first_row, first_col])
    target_col = jnp.concatenate([first_col, first_row])
    owner = target_row // tile_rows * col_count + target_col // tile_cols
    place = target_row % tile_rows * tile_cols + target_col % tile_cols
    onehot = (
        (owner[:, None] == jnp.arange(devices, dtype=jnp.int32)[None, :]) & live[:, None]
    ).astype(jnp.int32)
    earlier = jnp.cumsum(onehot, axis=0) - onehot
    rank = jnp.sum(earlier * onehot, axis=1)
    slot = jnp.where(live, owner * capacity + rank, devices * capacity)
    outgoing = (
        jnp.zeros((devices * capacity + 1, TB * TB), jnp.float32).at[slot].set(placements)[:-1]
    )
    where_to = jnp.full((devices * capacity + 1,), local_tiles, jnp.int32).at[slot].set(place)[:-1]
    incoming, landing = (
        lax.all_to_all(outgoing, ("row", "col"), split_axis=0, concat_axis=0, tiled=True),
        lax.all_to_all(where_to, ("row", "col"), split_axis=0, concat_axis=0, tiled=True),
    )
    extend = (
        jnp.zeros((local_tiles + 1, TB * TB), jnp.float32).at[landing].add(incoming)[:local_tiles]
    )
    extend = (
        extend.reshape(tile_rows, tile_cols, TB, TB)
        .transpose(0, 2, 1, 3)
        .reshape(local_rows, local_cols)
    )
    matrix = front + extend
    row_start = lax.axis_index("row") * local_rows
    col_start = lax.axis_index("col") * local_cols
    global_rows = row_start + jnp.arange(local_rows, dtype=jnp.int32)
    group = row_count // col_count
    margin = jnp.zeros((NB, NB), jnp.float32)
    factor_parts = []
    for k in range(PANELS):
        low = k * NB
        high = low + NB
        owner_col = low // local_cols
        offset = low % local_cols
        panel = broadcast(matrix[:, offset : offset + NB], "col", owner_col)
        padded = jnp.concatenate([margin, panel, margin], axis=0)
        begin = jnp.clip(low - row_start + NB, 0, local_rows + NB)
        piece = lax.dynamic_slice_in_dim(padded, begin, NB, 0)
        diag_block = lax.psum(piece, "row")
        chol = jnp.linalg.cholesky(0.5 * (diag_block + diag_block.T))
        solved = jax.scipy.linalg.solve_triangular(chol, panel.T, lower=True).T
        factor_parts.append(jnp.where((global_rows >= low)[:, None], solved, 0.0))
        trail = jnp.where((global_rows >= high)[:, None], solved, 0.0)
        column_owner = lax.axis_index("col") * group
        pieces = [broadcast(trail, "row", column_owner + member) for member in range(group)]
        across = jnp.concatenate(pieces, axis=0)
        matrix = matrix - jnp.dot(trail, across.T, precision=HIGH)
    start = PANELS * NB
    global_cols = col_start + jnp.arange(local_cols, dtype=jnp.int32)
    weighted = jnp.where((global_cols >= start)[:, None], probe, 0.0)
    shares = lax.psum_scatter(
        lax.dot_general(weighted, matrix, (((0,), (1,)), ((), ())), precision=HIGH),
        "col",
        scatter_dimension=0,
        tiled=True,
    )
    sketch = jnp.where((global_rows >= start)[:, None], shares.T, 0.0)
    all_panels = jnp.concatenate(factor_parts, axis=1)
    width = all_panels.shape[1] // col_count
    panel_factor = lax.dynamic_slice_in_dim(all_panels, lax.axis_index("col") * width, width, 1)
    return (panel_factor, sketch)


def solution(mesh):
    return jax.shard_map(
        per_device,
        mesh=mesh,
        in_specs=(
            P("row", "col"),
            P(("row", "col"), None),
            P(("row", "col")),
            P(("row", "col")),
            P("col", None),
        ),
        out_specs=(P("row", "col"), P("row", "col")),
        check_vma=False,
    )
```

profile of v0, /device:TPU:4, one launch (start us, length us, event | category | flops | bytes accessed | tf_op | source)
XLA Modules:
  0.0 1307.7 jit_solution(11080386746946422240)
XLA Ops:
  9.4 2.6 fusion.101
  11.9 2.6 fusion.129
  17.6 6.1 all-to-all-start
  23.7 1.9 copy.32
  26.9 2.2 pad_maximum_fusion
  29.1 5.7 copy.33
  34.7 6.8 scatter_custom_fusion.1
  41.5 4.6 slice_bitcast_fusion
  46.1 5.9 all-to-all-start.1
  53.8 91.6 %all-to-all-done.1 = f32[32,8,4096]{2,1,0:T(8,128)} async-done(((f32[32,8,4096]{2,1,0:T(8,128)}), f32[32,8,4096]{2,1,0:T(8,128)}, u32[]{:S(2)}, u32[]{:S(2)}) %all-to-all-start.1) | async-done | bytes 4194336 | tf_op jit(solution)/shard_map/all_to_all | solution.py:53
  145.4 12.6 scatter_custom_fusion.2
  158.1 9.2 slice.128
  167.3 17.6 %reshape.472 = f32[18,36,64,64]{3,2,1,0:T(8,128)} reshape(f32[648,4096]{1,0:T(8,128)} %slice.128) | data formatting | bytes 21233664 | tf_op jit(solution)/shard_map/reshape | solution.py:60
  184.8 22.4 %copy.34 = f32[18,64,36,64]{3,2,1,0:T(8,128)} copy(f32[18,64,36,64]{3,1,2,0:T(8,128)} %bitcast.181) | data formatting | bytes 21233664 | tf_op jit(solution)/shard_map/transpose | solution.py:61
  207.2 18.6 %reshape.473 = f32[1152,2304]{1,0:T(8,128)} reshape(f32[18,64,36,64]{3,2,1,0:T(8,128)} %copy.34) | data formatting | bytes 21233664 | tf_op jit(solution)/shard_map/reshape | solution.py:62
  225.8 7.8 add.250
  233.6 4.0 copy-done.1
  237.6 1.7 slice_select_fusion.1
  239.4 56.0 %all-reduce.10.cloned.1.call-done = f32[1152,512]{1,0:T(8,128)} async-done(((f32[1152,512]{1,0:T(8,128)}), f32[1152,512]{1,0:T(8,128)}) %all-reduce.10.cloned.1.call-update) | async-done | bytes 2359312 | tf_op jit(solution)/shard_map/psum | solution.py:17
  295.6 2.9 fusion.41
  298.8 79.9 %all-reduce.12.cloned.1.call-done = f32[512,512]{1,0:T(8,128)} async-done(((f32[512,512]{1,0:T(8,128)}), f32[512,512]{1,0:T(8,128)}) %all-reduce.12.cloned.1.call-update) | async-done | bytes 1048592 | tf_op jit(solution)/shard_map/psum | solution.py:80
  378.7 2.6 copy.35
  384.3 11.7 cholesky.286
  396.2 9.8 custom-call.27
  408.5 11.7 cholesky.305
  420.3 10.3 custom-call.28
  432.1 11.7 cholesky.326
  444.6 9.8 custom-call.29
  455.8 11.9 cholesky.343
  471.7 8.3 while.4
  480.0 39.3 %custom-call.30 = f32[4,128,128]{1,2,0:T(8,128)S(1)} custom-call(f32[4,128,128]{2,1,0:T(8,128)S(1)} %get-tuple-element.18), custom_call_target="InvertDiagBlocksLowerTriangular" | custom-call | tf_op jit(solution)/shard_map/jit(_solve_triangular)/triangular_solve | solution.py:82
  519.4 1.9 fusion.47
  521.2 2.2 convolution_subtract_fusion.7
  524.2 3.1 convolution_subtract_fusion.6
  528.0 4.3 convolution_subtract_fusion.3
  533.8 3.1 select_bitcast_fusion.4
  537.0 169.7 %all-reduce.20.cloned.1.call-done = (f32[1152,512]{0,1:T(8,128)}, f32[1152,512]{0,1:T(8,128)}) async-done(((f32[1152,512]{0,1:T(8,128)}, f32[1152,512]{0,1:T(8,128)}), (f32[1152,512]{0,1:T(8,128)}, f32[1152,512]{0,1:T(8,128)})) %all-reduce.20.cloned.1.call-update) | async-done | bytes 4718608 | tf_op jit(solution)/shard_map/psum | solution.py:17
  706.7 22.0 %convolution_subtract_fusion.1 = f32[1152,2304]{1,0:T(8,128)S(1)} fusion(f32[1152,2304]{1,0:T(8,128)} %copy-done.1, f32[1152,512]{0,1:T(8,128)} %get-tuple-element.46, f32[1152,512]{0,1:T(8,128)} %get-tuple-element.47, pred[1152]{0:T(1024)(128)(4,1)S(1)} %get-tuple-element.94, f32[128,1152]{1,0:T(8,128)S(1)} %fusion.71, f32[128,1152]{1,0:T(8,128)S(1)} %fusion.72, ...), kind=kOutput, calls=%fused_computation.8 | convolution fusion | flops 16313647104 | bytes 28312704 | tf_op jit(solution)/shard_map/dot_general | solution.py:88
  728.8 4.0 copy-done
  732.8 1.8 slice_select_fusion
  734.6 53.7 %all-reduce.14.cloned.1.call-done = f32[1152,512]{1,0:T(8,128)} async-done(((f32[1152,512]{1,0:T(8,128)}), f32[1152,512]{1,0:T(8,128)}) %all-reduce.14.cloned.1.call-update) | async-done | bytes 2359312 | tf_op jit(solution)/shard_map/psum | solution.py:17
  788.3 2.9 fusion.39
  791.7 80.2 %all-reduce.16.cloned.1.call-done = f32[512,512]{1,0:T(8,128)} async-done(((f32[512,512]{1,0:T(8,128)}), f32[512,512]{1,0:T(8,128)}) %all-reduce.16.cloned.1.call-update) | async-done | bytes 1048592 | tf_op jit(solution)/shard_map/psum | solution.py:80
  874.8 11.7 cholesky.358
  886.6 9.8 custom-call.31
  897.1 11.7 cholesky.377
  910.2 9.9 custom-call.32
  922.5 13.2 %cholesky.398 = f32[128,128]{1,0:T(8,128)} custom-call(f32[128,128]{1,0:T(8,128)} %cholesky.448), custom_call_target="Cholesky" | custom-call | tf_op jit(solution)/shard_map/jit(cholesky)/cholesky | solution.py:81
  937.8 11.3 custom-call.33
  951.4 11.9 cholesky.415
  967.6 11.3 while.5
  968.2 2.2 bitcast_dynamic-update-slice_fusion.5
  971.0 2.2 bitcast_dynamic-update-slice_fusion.5
  973.9 2.2 bitcast_dynamic-update-slice_fusion.5
  976.7 2.1 bitcast_dynamic-update-slice_fusion.5
  978.9 39.3 %custom-call.34 = f32[4,128,128]{1,2,0:T(8,128)S(1)} custom-call(f32[4,128,128]{2,1,0:T(8,128)S(1)} %get-tuple-element.19), custom_call_target="InvertDiagBlocksLowerTriangular" | custom-call | tf_op jit(solution)/shard_map/jit(_solve_triangular)/triangular_solve | solution.py:82
  1019.0 1.9 convolution_subtract_fusion.5
  1022.5 2.9 convolution_subtract_fusion.4
  1026.2 4.2 convolution_subtract_fusion.2
  1031.2 3.1 select_bitcast_fusion.1
  1034.4 169.7 %all-reduce.18.cloned.1.call-done = (f32[1152,512]{0,1:T(8,128)}, f32[1152,512]{0,1:T(8,128)}) async-done(((f32[1152,512]{0,1:T(8,128)}, f32[1152,512]{0,1:T(8,128)}), (f32[1152,512]{0,1:T(8,128)}, f32[1152,512]{0,1:T(8,128)})) %all-reduce.18.cloned.1.call-update) | async-done | bytes 4718608 | tf_op jit(solution)/shard_map/psum | solution.py:17
  1204.1 22.3 %convolution_subtract_fusion = f32[1152,2304]{1,0:T(8,128)S(1)} fusion(f32[1152,2304]{1,0:T(8,128)} %copy-done, f32[1152,512]{0,1:T(8,128)} %get-tuple-element.44, f32[1152,512]{0,1:T(8,128)} %get-tuple-element.45, pred[1152]{0:T(1024)(128)(4,1)S(1)} %fusion.89, f32[128,1152]{1,0:T(8,128)S(1)} %fusion.65, f32[128,1152]{1,0:T(8,128)S(1)} %copy-done.5, ...), kind=kOutput, calls=%fused_computation.7 | convolution fusion | flops 16313647104 | bytes 28312704 | tf_op jit(solution)/shard_map/dot_general | solution.py:88
  1226.4 41.0 %fusion.8 = f32[512,1152]{1,0:T(8,128)} fusion(f32[1152,2304]{1,0:T(8,128)S(1)} %convolution_subtract_fusion, f32[2304,512]{1,0:T(8,128)} %param.12, pred[2304]{0:T(1024)(128)(4,1)S(1)} %add_compare_fusion), kind=kOutput, calls=%fused_computation.23 | convolution fusion | flops 16308633600 | bytes 17697024 | tf_op jit(solution)/shard_map/dot_general | solution.py:93
  1272.0 26.5 %reduce-scatter.2.cloned.1.call-done = f32[128,1152]{1,0:T(8,128)} async-done(((f32[512,1152]{1,0:T(8,128)}), f32[128,1152]{1,0:T(8,128)}) %reduce-scatter.2.cloned.1.call-update) | async-done | bytes 589840 | tf_op jit(solution)/shard_map/reduce_scatter | solution.py:92
  (148 shorter events, 58.1 us)
Async XLA Ops:
  17.6 28.5 %all-to-all-start = ((s32[32,8,1]{1,2,0:T(1,128)}), s32[32,8,1]{1,2,0:T(1,128)S(1)}, u32[]{:S(2)}, u32[]{:S(2)}) async-start(s32[32,8,1]{1,2,0:T(1,128)} %bitcast.14), calls=%async_computation | async-start | bytes 32768 | tf_op jit(solution)/shard_map/all_to_all | solution.py:54
  46.1 99.3 %all-to-all-start.1 = ((f32[32,8,4096]{2,1,0:T(8,128)}), f32[32,8,4096]{2,1,0:T(8,128)}, u32[]{:S(2)}, u32[]{:S(2)}) async-start(f32[32,8,4096]{2,1,0:T(8,128)} %slice_bitcast_fusion), calls=%async_computation.1 | async-start | bytes 8388608 | tf_op jit(solution)/shard_map/all_to_all | solution.py:53
  52.0 243.4 %all-reduce.10.cloned.1.call-start = ((), (), s32[]{:S(2)}) async-start(), calls=%async_computation.3 | async-start | bytes 4718592 | tf_op jit(solution)/shard_map/psum | solution.py:17
  233.6 4.0 copy-start.1
  239.3 139.4 %all-reduce.12.cloned.1.call-start = ((), (), s32[]{:S(2)}) async-start(), calls=%async_computation.4 | async-start | bytes 2097152 | tf_op jit(solution)/shard_map/psum | solution.py:80
  298.5 408.2 %all-reduce.20.cloned.1.call-start = ((), (), s32[]{:S(2)}) async-start(), calls=%async_computation.9 | async-start | bytes 9437184 | tf_op jit(solution)/shard_map/psum | solution.py:17
  378.7 2.6 copy-start.6
  383.3 1.0 copy-start.10
  480.0 44.1 %copy-start.8 = (f32[512,512]{1,0:T(8,128)}, f32[512,512]{1,0:T(8,128)S(1)}, u32[]{:S(2)}) copy-start(f32[512,512]{1,0:T(8,128)S(1)} %get-tuple-element.220) | copy-start | bytes 3145732
  519.3 7.9 copy-start.11
  537.0 251.3 %all-reduce.14.cloned.1.call-start = ((), (), s32[]{:S(2)}) async-start(), calls=%async_computation.5 | async-start | bytes 4718592 | tf_op jit(solution)/shard_map/psum | solution.py:17
  728.8 4.0 copy-start
  734.6 137.3 %all-reduce.16.cloned.1.call-start = ((), (), s32[]{:S(2)}) async-start(), calls=%async_computation.6 | async-start | bytes 2097152 | tf_op jit(solution)/shard_map/psum | solution.py:80
  791.2 412.9 %all-reduce.18.cloned.1.call-start = ((), (), s32[]{:S(2)}) async-start(), calls=%async_computation.8 | async-start | bytes 9437184 | tf_op jit(solution)/shard_map/psum | solution.py:17
  871.8 1.7 copy-start.7
  874.7 45.5 %copy-start.9 = (f32[512,512]{1,0:T(8,128)}, f32[512,512]{1,0:T(8,128)S(1)}, u32[]{:S(2)}) copy-start(f32[512,512]{1,0:T(8,128)S(1)} %fusion.42) | copy-start | bytes 3145732
  920.5 97.7 %copy-start.3 = (f32[1152,512]{1,0:T(8,128)S(1)}, f32[1152,512]{1,0:T(8,128)}, u32[]{:S(2)}) copy-start(f32[1152,512]{1,0:T(8,128)} %all-reduce.14.cloned.1.call-done) | copy-start | bytes 7077892
  1018.2 0.8 copy-start.12
  1020.9 4.6 copy-start.13
  1026.2 8.1 copy-start.4
  1034.3 169.8 %copy-start.5 = (f32[128,1152]{1,0:T(8,128)S(1)}, f32[128,1152]{1,0:T(8,128)}, u32[]{:S(2)}) copy-start(f32[128,1152]{1,0:T(8,128)} %copy-done.4) | copy-start | bytes 1769476
  1034.4 264.1 %reduce-scatter.2.cloned.1.call-start = ((), (), s32[]{:S(2)}) async-start(), calls=%async_computation.7 | async-start | bytes 2949120 | tf_op jit(solution)/shard_map/reduce_scatter | solution.py:92
  1267.4 1.7 copy-start.2
Sparse Core Ops, SparseCore 0:
  239.4 55.9 all-reduce.9
  299.5 79.1 all-reduce.11
  537.1 169.5 all-reduce.19
  734.7 53.5 all-reduce.13
  792.6 79.1 all-reduce.15
  1034.5 169.5 all-reduce.17
  1267.5 30.8 reduce-scatter.1
where the time goes:
time: 1320 us; the launch traced here: 1310 us
  waiting for transfers between devices  727 us (55%)
  other arithmetic  293 us (22%)
  local copies, waits for them, and re-layouts  131 us (10%)
  matrix products  123 us (9%)
  between operations  20.1 us (2%)
  starting transfers between devices  13.4 us (1%)
    psum x4, waiting for transfers between devices, broadcast(): return lax.psum(jnp.where(mine, value, jnp.zeros_like(value)), axis)  449 us
    another operation x29, other arithmetic, per_device(): chol = jnp.linalg.cholesky(0.5 * (diag_block + diag_block.T))  163 us
    psum x2, waiting for transfers between devices, per_device(): diag_block = lax.psum(piece, 'row')  160 us
    all_to_all x1, waiting for transfers between devices, per_device(): lax.all_to_all(outgoing, ('row', 'col'), split_axis=0, concat_axis=0, til...  91.6 us
    another operation x5, other arithmetic, per_device(): solved = jax.scipy.linalg.solve_triangular(chol, panel.T, lower=True).T  79.9 us
    dot_general x2, matrix products, per_device(): matrix = matrix - jnp.dot(trail, across.T, precision=HIGH)  44.3 us
    dot_general x1, matrix products, per_device(): lax.dot_general(weighted, matrix, (((0,), (1,)), ((), ())), precision=HIGH)  41 us
    another operation x14, matrix products, per_device(): solved = jax.scipy.linalg.solve_triangular(chol, panel.T, lower=True).T  27.3 us
  transfers between devices with their start and end apart: 9, of which 8 were waited for; matrix products, arithmetic and copies ran while one was open for 2% of the time, Pallas kernels for 0%

commit v1 on v0

v1 whole, which is shorter than its diff:
```python
import functools

import jax
import jax.numpy as jnp
from jax import lax
from jax.experimental import pallas as pl
from jax.experimental.pallas import tpu as pltpu
from jax.sharding import PartitionSpec as P

NB = 512
PANELS = 2
PD = NB * PANELS
TB = 64
SLOTS = 32
LANES = 128
NBLK = PD // LANES
PACKED = NBLK * (NBLK + 1) // 2
AXES = ("row", "col")
HIGH = lax.Precision.HIGHEST
MIB = 1 << 20


def block_index(r, c):
    return r * NBLK - r * (r - 1) // 2 + (c - r)


def left_half(shape):
    return lax.broadcasted_iota(jnp.int32, shape, len(shape) - 1) < TB


def add_tile(ref, row, col, half, packed):
    turned = pltpu.roll(packed, TB, 1)
    mask = left_half(packed.shape) == (half == 0)
    top = jnp.where(mask, jnp.where(half == 0, packed, turned), 0.0)
    low = jnp.where(mask, jnp.where(half == 0, turned, packed), 0.0)
    cols = pl.ds(pl.multiple_of(col, LANES), LANES)
    upper = pl.ds(pl.multiple_of(row, TB), TB // 2)
    lower = pl.ds(pl.multiple_of(row + TB // 2, TB // 2), TB // 2)
    ref[upper, cols] += top
    ref[lower, cols] += low


def prepare_kernel(
    held, devices, capacity, local_rows,
    live_ref, row_ref, col_ref, owner_ref, place_ref, me_ref,
    tiles_ref, front_ref,
    out_ref, landing_ref, diag_ref,
    flat_ref, pair_ref, count_ref, slot_ref,
):
    half = TB // 2
    for d in range(devices):
        count_ref[d] = 0

    def clear(s, carry):
        landing_ref[s] = -1
        return carry

    lax.fori_loop(0, devices * capacity, clear, 0)

    def spread(g, carry):
        rows = tiles_ref[pl.ds(pl.multiple_of(g * 8, 8), 8), :]
        for k in range(half):
            flat_ref[pl.ds(g * 8 * half + k, 8, stride=half), :] = rows[:, k * LANES : (k + 1) * LANES]
        return carry

    lax.fori_loop(0, held // 8, spread, 0)

    def assign(t, carry):
        for m in range(2):
            owner = owner_ref[m * held + t]
            slot = owner * capacity + count_ref[owner]
            count_ref[owner] += 1
            slot_ref[m * held + t] = slot
            landing_ref[slot] = jnp.where(live_ref[t] == 1, place_ref[m * held + t], -1)
        return carry

    lax.fori_loop(0, held, assign, 0)

    def quad(q, carry):
        left = left_half((half, LANES))
        naturals = []
        for p in range(2):
            a = flat_ref[pl.ds(pl.multiple_of((4 * q + 2 * p) * half, half), half), :]
            b = flat_ref[pl.ds(pl.multiple_of((4 * q + 2 * p + 1) * half, half), half), :]
            pair_ref[p, pl.ds(0, half, stride=2), :] = jnp.where(left, a, pltpu.roll(b, TB, 1))
            pair_ref[p, pl.ds(1, half, stride=2), :] = jnp.where(left, pltpu.roll(a, TB, 1), b)
            naturals.append(pair_ref[p, :, :])
        turned = jnp.concatenate(naturals, axis=0).T
        for m, values, order in (
            (0, naturals[0], (0, 1)),
            (0, naturals[1], (2, 3)),
            (1, turned[:TB], (0, 2)),
            (1, turned[TB:], (1, 3)),
        ):
            up, low = values[:half], values[half:]
            out_ref[slot_ref[m * held + 4 * q + order[0]]] = jnp.where(left, up, pltpu.roll(low, TB, 1))
            out_ref[slot_ref[m * held + 4 * q + order[1]]] = jnp.where(left, pltpu.roll(up, TB, 1), low)
        return carry

    lax.fori_loop(0, held // 4, quad, 0)

    for r64 in range(PD // TB):
        home = (r64 * TB) // local_rows
        start = r64 * TB - home * local_rows
        mine = (me_ref[0] == home) & (me_ref[1] == 0)
        r = r64 // 2
        for c in range(r, NBLK):
            base = block_index(r, c) * LANES + (r64 % 2) * TB
            piece = front_ref[start : start + TB, c * LANES : (c + 1) * LANES]
            diag_ref[base : base + TB, :] = jnp.where(mine, piece, 0.0)

    def diagonal(t, carry):
        r, c = row_ref[t], col_ref[t]

        @pl.when((live_ref[t] == 1) & (r < PD // TB) & (c < PD // TB))
        def _():
            for m, (a, b) in enumerate(((r, c), (c, r))):
                big, wide = a // 2, b // 2

                @pl.when(wide >= big)
                def _():
                    base = block_index(big, wide) * LANES + (a % 2) * TB
                    add_tile(diag_ref, base, 0, b % 2, out_ref[slot_ref[m * held + t]])

        return carry

    lax.fori_loop(0, held, diagonal, 0)


def prepare(live, first_row, first_col, owner, place, me, child_tiles, front, devices, capacity):
    held = child_tiles.shape[0]
    local_rows, local_cols = front.shape
    half = TB // 2
    smem = pl.BlockSpec(memory_space=pltpu.SMEM)
    rows = min(PD, local_rows)
    return pl.pallas_call(
        functools.partial(prepare_kernel, held, devices, capacity, local_rows),
        grid=(1,),
        out_shape=(
            jax.ShapeDtypeStruct((devices * capacity, half, LANES), jnp.float32),
            jax.ShapeDtypeStruct((devices * capacity,), jnp.int32),
            jax.ShapeDtypeStruct((PACKED * LANES, LANES), jnp.float32),
        ),
        in_specs=[smem] * 6
        + [
            pl.BlockSpec((held, TB * TB), lambda i: (0, 0)),
            pl.BlockSpec((rows, PD), lambda i: (0, 0)),
        ],
        out_specs=(
            pl.BlockSpec((devices * capacity, half, LANES), lambda i: (0, 0, 0)),
            smem,
            pl.BlockSpec((PACKED * LANES, LANES), lambda i: (0, 0)),
        ),
        scratch_shapes=[
            pltpu.VMEM((held * half, LANES), jnp.float32),
            pltpu.VMEM((2, TB, LANES), jnp.float32),
            pltpu.SMEM((devices,), jnp.int32),
            pltpu.SMEM((2 * held,), jnp.int32),
        ],
        compiler_params=pltpu.CompilerParams(vmem_limit_bytes=40 * MIB),
        name="prepare",
    )(live, first_row, first_col, owner, place, me, child_tiles, front)


def lane_splat(x, lane):
    return jnp.broadcast_to(x[:, lane : lane + 1], x.shape)


def row_splat(x, row):
    return jnp.broadcast_to(x[row : row + 1, :], x.shape)


def inverse_factor(strips):
    strips = list(strips)
    lane = lax.broadcasted_iota(jnp.int32, (8, LANES), 1)
    sub = lax.broadcasted_iota(jnp.int32, (8, LANES), 0)
    result = []
    for k in range(LANES // 8):
        strip = strips[k]
        columns = [lane_splat(strip, 8 * k + t) for t in range(8)]
        e = [[row_splat(columns[t], s) if s <= t else None for t in range(8)] for s in range(8)]
        low = [[None] * 8 for _ in range(8)]
        inv = [None] * 8
        for s in range(8):
            x = e[s][s]
            y = lax.rsqrt(x)
            inv[s] = y * (1.5 - 0.5 * x * y * y)
            for t in range(s + 1, 8):
                low[t][s] = e[s][t] * inv[s]
            for t in range(s + 1, 8):
                for u in range(t, 8):
                    e[t][u] = e[t][u] - low[t][s] * low[u][s]
        li = [[None] * 8 for _ in range(8)]
        for s in range(8):
            li[s][s] = inv[s]
            for r in range(s + 1, 8):
                total = low[r][s] * li[s][s]
                for q in range(s + 1, r):
                    total = total + low[r][q] * li[q][s]
                li[r][s] = -inv[r] * total
        inside = (lane >= 8 * k) & (lane < 8 * k + 8)
        unit = jnp.where(lane - 8 * k == sub, 1.0, 0.0)
        strip = jnp.where(inside, unit, strip)
        rows = [row_splat(strip, s) for s in range(8)]
        u = []
        for r in range(8):
            total = li[r][0] * rows[0]
            for s in range(1, r + 1):
                total = total + li[r][s] * rows[s]
            u.append(total)
        mine = u[0]
        for r in range(1, 8):
            mine = jnp.where(sub == r, u[r], mine)
        result.append(jnp.where(lane < 8 * k + 8, mine, 0.0))
        if k + 1 == LANES // 8:
            break
        v = []
        for s in range(8):
            total = li[s][s] * u[s]
            for r in range(s + 1, 8):
                total = total + li[r][s] * u[r]
            v.append(total)
        for i in range(k + 1, LANES // 8):
            old = strips[i]
            total = lane_splat(old, 8 * k) * v[0]
            for s in range(1, 8):
                total = total + lane_splat(old, 8 * k + s) * v[s]
            strips[i] = jnp.where(inside, 0.0, old) - total
    return result


def factor_kernel(packed_ref, out_ref, top_ref, small_ref):
    out_ref[...] = jnp.zeros_like(out_ref)
    for r in range(NBLK):
        for c in range(r, NBLK):
            base = block_index(r, c) * LANES
            out_ref[r * LANES : (r + 1) * LANES, c * LANES : (c + 1) * LANES] = packed_ref[base : base + LANES, :]

    eye = jnp.where(
        lax.broadcasted_iota(jnp.int32, (LANES, LANES), 0) == lax.broadcasted_iota(jnp.int32, (LANES, LANES), 1), 1.0, 0.0
    )

    def outer(k, carry):
        at = pl.multiple_of(k * LANES, LANES)
        here = pl.ds(at, LANES)
        block = out_ref[here, here]
        block = 0.5 * (block + block.T)
        small_ref[...] = block
        strips = inverse_factor([small_ref[8 * i : 8 * i + 8, :] for i in range(LANES // 8)])
        for i, strip in enumerate(strips):
            small_ref[8 * i : 8 * i + 8, :] = strip
        out_ref[here, here] = eye
        top = jnp.dot(small_ref[...], out_ref[here, :], precision=HIGH, preferred_element_type=jnp.float32)
        top_ref[...] = top
        column = lax.broadcasted_iota(jnp.int32, (LANES, PD), 1)
        out_ref[here, :] = jnp.where(column < at + LANES, top, 0.0)

        def trailing(i, carry):
            there = pl.ds(pl.multiple_of(i * LANES, LANES), LANES)
            out_ref[there, here] = jnp.zeros((LANES, LANES), jnp.float32)
            out_ref[there, :] -= lax.dot_general(
                top_ref[:, there], top_ref[...], (((0,), (0,)), ((), ())), precision=HIGH, preferred_element_type=jnp.float32
            )
            return carry

        lax.fori_loop(k + 1, NBLK, trailing, 0)
        return carry

    lax.fori_loop(0, NBLK, outer, 0)


def inverse_of_factor(packed):
    return pl.pallas_call(
        factor_kernel,
        out_shape=jax.ShapeDtypeStruct((PD, PD), jnp.float32),
        in_specs=[pl.BlockSpec(memory_space=pltpu.VMEM)],
        out_specs=pl.BlockSpec(memory_space=pltpu.VMEM),
        scratch_shapes=[pltpu.VMEM((LANES, PD), jnp.float32), pltpu.VMEM((LANES, LANES), jnp.float32)],
        compiler_params=pltpu.CompilerParams(vmem_limit_bytes=24 * MIB),
        name="factor",
    )(packed)


def split(x):
    high = x.astype(jnp.bfloat16)
    return high, (x - high.astype(jnp.float32)).astype(jnp.bfloat16)


def assemble_kernel(
    slots, row_chunk, width,
    tile_row_ref, tile_col_ref, first_ref,
    front_ref, incoming_ref, probe_ref,
    product_ref, panel_ref,
    matrix_ref, high_ref, low_ref, semaphore,
):
    copy = pltpu.make_async_copy(front_ref, matrix_ref, semaphore)
    copy.start()
    depth = probe_ref.shape[0]
    step = 256
    first = first_ref[0]

    def cut(s, carry):
        rows = pl.ds(pl.multiple_of(s * step, step), step)
        index = lax.broadcasted_iota(jnp.int32, (step, probe_ref.shape[1]), 0) + s * step
        high, low = split(jnp.where(index >= first, probe_ref[rows, :], 0.0))
        high_ref[rows, :] = high
        low_ref[rows, :] = low
        return carry

    lax.fori_loop(0, depth // step, cut, 0)
    copy.wait()

    def place(s, carry):
        r, c = tile_row_ref[s], tile_col_ref[s]

        @pl.when(r >= 0)
        def _():
            add_tile(matrix_ref, r * TB, (c // 2) * LANES, c % 2, incoming_ref[s])

        return carry

    lax.fori_loop(0, slots, place, 0)

    def multiply(b, carry):
        rows = pl.ds(pl.multiple_of(b * row_chunk, row_chunk), row_chunk)
        panel_ref[rows, :] = matrix_ref[rows, :PD]
        high, low = split(matrix_ref[rows, :])
        dot = functools.partial(jnp.dot, preferred_element_type=jnp.float32)
        total = dot(high, high_ref[...]) + (dot(high, low_ref[...]) + dot(low, high_ref[...]))
        for j in range(probe_ref.shape[1] // width):
            product_ref[j, rows, :] = total[:, j * width : (j + 1) * width]
        return carry

    lax.fori_loop(0, matrix_ref.shape[0] // row_chunk, multiply, 0)


def assemble(tile_row, tile_col, first, front, incoming, probe, col_count):
    local_rows, local_cols = front.shape
    columns = probe.shape[1]
    width = columns // col_count
    smem = pl.BlockSpec(memory_space=pltpu.SMEM)
    vmem = pl.BlockSpec(memory_space=pltpu.VMEM)
    row_chunk = 192 if local_rows % 192 == 0 else 64
    return pl.pallas_call(
        functools.partial(assemble_kernel, tile_row.shape[0], row_chunk, width),
        out_shape=(
            jax.ShapeDtypeStruct((col_count, local_rows, width), jnp.float32),
            jax.ShapeDtypeStruct((local_rows, PD), jnp.float32),
        ),
        in_specs=[smem] * 3 + [pl.BlockSpec(memory_space=pl.ANY), vmem, vmem],
        out_specs=(vmem, vmem),
        scratch_shapes=[
            pltpu.VMEM((local_rows, local_cols), jnp.float32),
            pltpu.VMEM((local_cols, columns), jnp.bfloat16),
            pltpu.VMEM((local_cols, columns), jnp.bfloat16),
            pltpu.SemaphoreType.DMA,
        ],
        compiler_params=pltpu.CompilerParams(vmem_limit_bytes=56 * MIB),
        name="assemble",
    )(tile_row, tile_col, first, front, incoming, probe)


def masks(count):
    return [1 << b for b in range(count.bit_length() - 1)]


def exchange(x, axis, mask, count):
    return lax.ppermute(x, axis, [(d, d ^ mask) for d in range(count)])


def choose(bit, x):
    h = x.shape[0] // 2
    return jnp.where(bit, x[h:], x[:h]), jnp.where(bit, x[:h], x[h:])


def halve(x, axis, index, mask, count):
    keep, send = choose((index & mask) != 0, x)
    return keep + exchange(send, axis, mask, count)


def double(x, axis, index, mask, count):
    other = exchange(x, axis, mask, count)
    bit = (index & mask) != 0
    return jnp.concatenate([jnp.where(bit, other, x), jnp.where(bit, x, other)], axis=0)


def all_sum(x, axis, index, order, count):
    for mask in order:
        x = halve(x, axis, index, mask, count)
    for mask in order[::-1]:
        x = double(x, axis, index, mask, count)
    return x


def spread(x, axis, index, order, count):
    for mask in order:
        other = lax.ppermute(x, axis, [(d, d + mask) for d in range(0, count, 2 * mask)])
        x = jnp.where((index & (2 * mask - 1)) == mask, other, x)
    return x


def per_device(front, child_tiles, tile_target, tile_count, probe):
    row_count = lax.axis_size("row")
    col_count = lax.axis_size("col")
    devices = row_count * col_count
    local_rows, local_cols = front.shape
    tile_rows = local_rows // TB
    tile_cols = local_cols // TB
    grid = tile_cols * col_count
    held = child_tiles.shape[0]
    capacity = 2 * max(1, (held + devices - 1) // devices)
    row_index = lax.axis_index("row")
    col_index = lax.axis_index("col")
    device = row_index * col_count + col_index

    slot_index = jnp.arange(held, dtype=jnp.int32)
    live = (slot_index % SLOTS < tile_count[slot_index // SLOTS]).astype(jnp.int32)
    first_row = tile_target // grid
    first_col = tile_target % grid
    target_row = jnp.concatenate([first_row, first_col])
    target_col = jnp.concatenate([first_col, first_row])
    owner = target_row // tile_rows * col_count + target_col // tile_cols
    place = target_row % tile_rows * tile_cols + target_col % tile_cols
    me = jnp.stack([row_index, col_index])
    outgoing, landing, diagonal = prepare(
        live, first_row, first_col, owner, place, me, child_tiles, front, devices, capacity
    )

    packed = all_sum(diagonal, AXES, device, masks(devices), devices)

    places = lax.all_to_all(landing.reshape(devices, capacity), AXES, split_axis=0, concat_axis=0, tiled=True).reshape(-1)
    incoming = lax.all_to_all(
        outgoing.reshape(devices, capacity, TB // 2, LANES), AXES, split_axis=0, concat_axis=0, tiled=True
    ).reshape(devices * capacity, TB // 2, LANES)

    inverse = inverse_of_factor(packed)

    col_start = col_index * local_cols
    first = jnp.clip(PD - col_start, 0, local_cols).reshape(1)
    tile_row = jnp.where(places >= 0, places // tile_cols, -1)
    product, panel = assemble(tile_row, places % tile_cols, first, front, incoming, probe, col_count)

    share = product.reshape(-1, product.shape[2])
    order = masks(col_count)[::-1]
    for mask in order:
        share = halve(share, "col", col_index, mask, col_count)

    panel = spread(panel, "col", col_index, masks(col_count)[::-1], col_count)

    pieces = []
    for home in range((PD + local_rows - 1) // local_rows):
        rows = min(PD - home * local_rows, local_rows)
        pieces.append(jnp.where(row_index == home, share[:rows], 0.0))
    if len(pieces) == 1:
        top = spread(pieces[0], "row", row_index, masks(row_count)[::-1], row_count)
    else:
        top = all_sum(jnp.concatenate(pieces, axis=0), "row", row_index, masks(row_count), row_count)

    dot = functools.partial(jnp.dot, precision=lax.Precision.HIGH, preferred_element_type=jnp.float32)
    width = PD // col_count
    mine = lax.dynamic_slice_in_dim(inverse, col_index * width, width, 0)
    solved = lax.dot_general(
        panel, mine, (((1,), (1,)), ((), ())), precision=lax.Precision.HIGH, preferred_element_type=jnp.float32
    )
    global_rows = row_index * local_rows + jnp.arange(local_rows, dtype=jnp.int32)
    panel_of = (col_index * width + jnp.arange(width, dtype=jnp.int32)) // NB
    panel_factor = jnp.where(global_rows[:, None] >= panel_of[None, :] * NB, solved, 0.0)

    weights = lax.dot_general(
        inverse, dot(inverse, top), (((0,), (0,)), ((), ())), precision=lax.Precision.HIGH, preferred_element_type=jnp.float32
    )
    sketch = jnp.where((global_rows >= PD)[:, None], share - dot(panel, weights), 0.0)
    return (panel_factor, sketch)


def solution(mesh):
    return jax.shard_map(
        per_device,
        mesh=mesh,
        in_specs=(
            P("row", "col"),
            P(("row", "col"), None),
            P(("row", "col")),
            P(("row", "col")),
            P("col", None),
        ),
        out_specs=(P("row", "col"), P("row", "col")),
        check_vma=False,
    )
```

time: 1320 us -> 391 us (0.30)
  waiting for transfers between devices: 727 us -> 185 us
  other arithmetic: 293 us -> 15.4 us
  local copies, waits for them, and re-layouts: 131 us -> 5.5 us
  Pallas kernels: 0 us -> 123 us
  matrix products: 123 us -> 15.8 us
  between operations: 20.1 us -> 1 us
  starting transfers between devices: 13.4 us -> 30.6 us
    psum x6 -> x0, waiting for transfers between devices: 609 us -> none  [the longest x4 449 us: broadcast(): return lax.psum(jnp.where(mine, value, jnp.zeros_like(value)), axis)]
    another operation x36 -> x1, other arithmetic: 243 us -> 0.08 us  [per_device(): me = jnp.stack([row_index, col_index])]
    ppermute x0 -> x17, waiting for transfers between devices: none -> 146 us  [the longest x12 123 us: exchange(): return lax.ppermute(x, axis, [(d, d ^ mask) for d in range(count)])]
    pallas_call x0 -> x3, Pallas kernels: none -> 123 us  [the longest x1 69.4 us: inverse_of_factor(): pl.pallas_call(factor_kernel, out_shape=jax.ShapeDtypeStruct((PD, PD), jn...]
    dot_general x3 -> x4, matrix products: 85.3 us -> 15.8 us  [the longest x1 5.41 us: per_device(): lax.dot_general(panel, mine, (((1,), (1,)), ((), ())), precision=lax.Prec...]
    all_to_all x2 -> x1, waiting for transfers between devices: 91.6 us -> 39.1 us  [per_device(): lax.all_to_all(outgoing.reshape(devices, capacity, TB // 2, LANES), AXES,...]
    another operation x26 -> x0, matrix products: 37.4 us -> none  [the longest x14 27.3 us: per_device(): solved = jax.scipy.linalg.solve_triangular(chol, panel.T, lower=True).T]
    reshape x2 -> x0, local copies, waits for them, and re-layouts: 36.2 us -> none  [the longest x1 18.6 us: per_device(): extend = extend.reshape(tile_rows, tile_cols, TB, TB).transpose(0, 2, 1,...]
  transfers between devices with their start and end apart: 9 -> 18, of which waited for: 8 -> 11; matrix products, arithmetic and copies ran while one was open for 2% -> 5% of each run, Pallas kernels for 0% -> 27%
where the time goes in v1:
time: 391 us; the launch traced here: 388 us
  waiting for transfers between devices  185 us (47%)
  Pallas kernels  123 us (31%)
  starting transfers between devices  30.6 us (8%)
  matrix products  15.8 us (4%)
  other arithmetic  15.4 us (4%)
  blocking collectives  11.8 us (3%)
  local copies, waits for them, and re-layouts  5.5 us (1%)
    ppermute x12, waiting for transfers between devices, exchange(): return lax.ppermute(x, axis, [(d, d ^ mask) for d in range(count)])  123 us
    pallas_call x1, Pallas kernels, inverse_of_factor(): pl.pallas_call(factor_kernel, out_shape=jax.ShapeDtypeStruct((PD, PD), jn...  69.4 us
    all_to_all x1, waiting for transfers between devices, per_device(): lax.all_to_all(outgoing.reshape(devices, capacity, TB // 2, LANES), AXES,...  39.1 us
    pallas_call x1, Pallas kernels, assemble(): pl.pallas_call(functools.partial(assemble_kernel, tile_row.shape[0], row_...  35.7 us
    ppermute x5, waiting for transfers between devices, spread(): lax.ppermute(x, axis, [(d, d + mask) for d in range(0, count, 2 * mask)])  22.1 us
    pallas_call x1, Pallas kernels, prepare(): pl.pallas_call(functools.partial(prepare_kernel, held, devices, capacity,...  17.9 us
    ppermute x12, starting transfers between devices, exchange(): return lax.ppermute(x, axis, [(d, d ^ mask) for d in range(count)])  13.2 us
    ppermute x5, starting transfers between devices, spread(): lax.ppermute(x, axis, [(d, d + mask) for d in range(0, count, 2 * mask)])  12.8 us
  transfers between devices with their start and end apart: 18, of which 11 were waited for; matrix products, arithmetic and copies ran while one was open for 5% of the time, Pallas kernels for 27%

profile of v1, /device:TPU:4, one launch (start us, length us, event | category | flops | bytes accessed | tf_op | source)
XLA Modules:
  0.0 387.8 jit_solution(14557863869583349564)
XLA Ops:
  0.6 1.5 fusion.12
  2.1 0.7 and_select_fusion.6
  2.8 0.1 pad_add_fusion.2.me_ref
  2.9 2.6 compare_convert_fusion.live_ref
  5.5 1.6 copy-done.1
  7.1 17.9 %prepare.1 = (f32[256,32,128]{2,1,0:T(8,128)S(1)}, s32[256]{0:T(256)S(1)}, f32[4608,128]{1,0:T(8,128)S(1)}) custom-call(s32[128]{0:T(128)S(1)} %compare_convert_fusion.live_ref, s32[128]{0:T(128)S(1)} %get-tuple-element.33.row_ref, s32[128]{0:T(128)S(1)} %get-tuple-element.32.col_ref, s32[256]{0:T(256)S(1)} %get-tuple-element.31.owner_ref, ...), custom_call_target="tpu_custom_call" | custom-call | tf_op jit(solution)/shard_map/prepare/pallas_call | solution.py:136
  25.0 2.0 copy-done
  26.9 0.1 all_to_all.9
  27.0 11.8 %all_to_all.14 = s32[32,1,8]{2,1,0:T(1,128)S(1)} all-to-all(s32[32,1,8]{2,1,0:T(1,128)S(1)} %bitcast.22), channel_id=1, replica_groups=mesh['row'=8,'col'=4] {'row','col'}, dimensions={0} | all-to-all | bytes 2048 | tf_op jit(solution)/shard_map/all_to_all | solution.py:431
  38.9 4.6 %all-to-all-start.1 = ((f32[32,8,32,128]{3,2,1,0:T(8,128)}), f32[32,8,32,128]{3,2,1,0:T(8,128)}, u32[]{:S(2)}, u32[]{:S(2)}) async-start(f32[32,8,32,128]{3,2,1,0:T(8,128)} %bitcast.21), calls=%async_computation.1 | async-start | bytes 8388608 | tf_op jit(solution)/shard_map/all_to_all | solution.py:432
  43.5 0.1 slice_select_fusion.2
  43.6 0.2 collective-permute-start.2
  43.9 2.8 collective-permute-done.2
  46.7 1.4 select_add_fusion
  48.1 0.1 slice_select_fusion.4
  48.2 0.5 collective-permute-start.3
  48.7 0.1 remainder_reduce_fusion
  48.9 0.1 div.49
  48.9 0.1 rem.93
  49.0 47.8 %collective-permute-done.3 = f32[1152,128]{1,0:T(8,128)S(1)} collective-permute-done((f32[1152,128]{1,0:T(8,128)S(1)}, f32[1152,128]{1,0:T(8,128)S(1)}, u32[]{:S(2)}, u32[]{:S(2)}) %collective-permute-start.3) | collective-permute-done | bytes 589856 | tf_op jit(solution)/shard_map/ppermute | solution.py:368
  96.8 0.1 select_add_fusion.2
  97.0 0.1 collective-permute-start.4
  97.1 0.1 compare_reduce_fusion
  97.2 0.1 ge.34
  97.3 0.1 ne.154
  97.4 0.6 and_select_fusion
  98.0 39.1 %all-to-all-done.1 = f32[32,8,32,128]{3,2,1,0:T(8,128)} async-done(((f32[32,8,32,128]{3,2,1,0:T(8,128)}), f32[32,8,32,128]{3,2,1,0:T(8,128)}, u32[]{:S(2)}, u32[]{:S(2)}) %all-to-all-start.1) | async-done | bytes 4194336 | tf_op jit(solution)/shard_map/all_to_all | solution.py:432
  137.1 35.7 %assemble.1 = (f32[4,1152,128]{2,1,0:T(8,128)}, f32[1152,1024]{1,0:T(8,128)}) custom-call(s32[256]{0:T(256)} %get-tuple-element.29.tile_row_ref, s32[256]{0:T(256)} %get-tuple-element.28.tile_col_ref, s32[1]{0:T(128)} %bitcast.8.first_ref, f32[1152,2304]{1,0:T(8,128)} %front_ref.3, f32[256,32,128]{2,1,0:T(8,128)} %bitcast.10.incoming_ref, f32[2304,512]{1,0:T(8,128)} %probe_ref.1), custom_call_target="tpu_custom_call" | custom-call | tf_op jit(solution)/shard_map/assemble/pallas_call | solution.py:344
  172.8 1.3 collective-permute-start
  174.2 0.1 collective-permute-start.5
  174.3 5.1 %collective-permute-done.5 = f32[288,128]{1,0:T(8,128)S(1)} collective-permute-done((f32[288,128]{1,0:T(8,128)S(1)}, f32[288,128]{1,0:T(8,128)S(1)}, u32[]{:S(2)}, u32[]{:S(2)}) %collective-permute-start.5) | collective-permute-done | bytes 147488 | tf_op jit(solution)/shard_map/ppermute | solution.py:368
  179.5 1.5 collective-permute-start.6
  181.0 4.1 %collective-permute-done.6 = f32[144,128]{1,0:T(8,128)S(1)} collective-permute-done((f32[144,128]{1,0:T(8,128)S(1)}, f32[144,128]{1,0:T(8,128)S(1)}, u32[]{:S(2)}, u32[]{:S(2)}) %collective-permute-start.6) | collective-permute-done | bytes 73760 | tf_op jit(solution)/shard_map/ppermute | solution.py:368
  185.2 1.6 collective-permute-start.7
  186.7 6.0 %collective-permute-done.7 = f32[144,128]{1,0:T(8,128)S(1)} collective-permute-done((f32[144,128]{1,0:T(8,128)S(1)}, f32[144,128]{1,0:T(8,128)S(1)}, u32[]{:S(2)}, u32[]{:S(2)}) %collective-permute-start.7) | collective-permute-done | bytes 73760 | tf_op jit(solution)/shard_map/ppermute | solution.py:368
  192.8 0.1 collective-permute-start.8
  192.9 1.2 slice_select_fusion.1
  194.0 4.1 %collective-permute-start.12 = (f32[2304,128]{1,0:T(8,128)}, f32[2304,128]{1,0:T(8,128)S(1)}, u32[]{:S(2)}, u32[]{:S(2)}) collective-permute-start(f32[2304,128]{1,0:T(8,128)} %bitcast.12), channel_id=1, source_target_pairs={{0,2},{1,3},{2,0},{3,1},{4,6},{5,7},{6,4},{7,5},{8,10},{9,11},{10,... | collective-permute-start | bytes 3538952 | tf_op jit(solution)/shard_map/ppermute | solution.py:368
  198.1 0.6 collective-permute-done.8
  198.8 3.0 collective-permute-start.9
  201.8 5.4 %collective-permute-done.9 = f32[576,128]{1,0:T(8,128)S(1)} collective-permute-done((f32[576,128]{1,0:T(8,128)S(1)}, f32[576,128]{1,0:T(8,128)S(1)}, u32[]{:S(2)}, u32[]{:S(2)}) %collective-permute-start.9) | collective-permute-done | bytes 294944 | tf_op jit(solution)/shard_map/ppermute | solution.py:368
  207.2 1.9 collective-permute-start.10
  209.1 51.5 %collective-permute-done.12 = f32[2304,128]{1,0:T(8,128)S(1)} collective-permute-done((f32[2304,128]{1,0:T(8,128)}, f32[2304,128]{1,0:T(8,128)S(1)}, u32[]{:S(2)}, u32[]{:S(2)}) %collective-permute-start.12) | collective-permute-done | bytes 1179680 | tf_op jit(solution)/shard_map/ppermute | solution.py:368
  260.6 0.1 bitcast_add_fusion
  260.8 0.1 slice_select_fusion.3
  260.8 0.1 collective-permute-start.13
  260.9 6.1 %broadcast_select_fusion = f32[1152,1024]{1,0:T(8,128)} fusion(f32[1152,1024]{1,0:T(8,128)} %collective-permute-done, f32[1152,1024]{1,0:T(8,128)} %get-tuple-element.9, pred[]{:T(512)S(6)} %eq.26), kind=kLoop, calls=%fused_computation.4 | loop fusion | flops 1179648 | bytes 14155777 | tf_op jit(solution)/shard_map/jit(_where)/select_n | solution.py:398
  267.0 4.6 %collective-permute-start.1 = (f32[1152,1024]{1,0:T(8,128)}, f32[1152,1024]{1,0:T(8,128)}, u32[]{:S(2)}, u32[]{:S(2)}) collective-permute-start(f32[1152,1024]{1,0:T(8,128)} %broadcast_select_fusion), channel_id=1, source_target_pairs={{0,1},{2,3},{4,5},{6,7},{8,9},{10,11},{12,13},{14,15},{16,17},{18,... | collective-permute-start | bytes 14155784 | tf_op jit(solution)/shard_map/ppermute | solution.py:397
  271.5 0.1 broadcast_select_fusion.7
  271.6 1.1 pad_maximum_fusion.1
  272.7 0.1 select_add_fusion.1
  272.9 4.2 %collective-permute-start.14 = (f32[1024,128]{1,0:T(8,128)S(1)}, f32[1024,128]{1,0:T(8,128)}, u32[]{:S(2)}, u32[]{:S(2)}) collective-permute-start(f32[1024,128]{1,0:T(8,128)S(1)} %slice_select_fusion.5), channel_id=1, source_target_pairs={{0,16},{1,17},{2,18},{3,19}} | collective-permute-start | bytes 1572872 | tf_op jit(solution)/shard_map/ppermute | solution.py:397
  277.1 11.0 %collective-permute-done.14 = f32[1024,128]{1,0:T(8,128)} collective-permute-done((f32[1024,128]{1,0:T(8,128)S(1)}, f32[1024,128]{1,0:T(8,128)}, u32[]{:S(2)}, u32[]{:S(2)}) %collective-permute-start.14) | collective-permute-done | bytes 524320 | tf_op jit(solution)/shard_map/ppermute | solution.py:397
  288.1 0.1 broadcast_select_fusion.8
  288.1 1.3 collective-permute-start.15
  289.5 0.2 broadcast_select_fusion.5
  289.6 11.1 %collective-permute-done.15 = f32[1024,128]{1,0:T(8,128)S(1)} collective-permute-done((f32[1024,128]{1,0:T(8,128)S(1)}, f32[1024,128]{1,0:T(8,128)S(1)}, u32[]{:S(2)}, u32[]{:S(2)}) %collective-permute-start.15) | collective-permute-done | bytes 524320 | tf_op jit(solution)/shard_map/ppermute | solution.py:397
  300.8 1.5 collective-permute-start.16
  302.3 0.2 pad_maximum_fusion.packed_ref
  302.5 69.4 %factor.1 = f32[1024,1024]{1,0:T(8,128)S(1)} custom-call(f32[4608,128]{1,0:T(8,128)S(1)} %pad_maximum_fusion.packed_ref), custom_call_target="tpu_custom_call" | custom-call | tf_op jit(solution)/shard_map/factor/pallas_call | solution.py:273
  371.9 1.8 fusion.2
  373.8 3.4 fusion.13
  377.2 5.2 %fusion = f32[1152,128]{1,0:T(8,128)} fusion(f32[1152,128]{1,0:T(8,128)S(1)} %select_add_fusion.1, f32[1024,128]{1,0:T(8,128)S(1)} %fusion.13, f32[1152,1024]{1,0:T(8,128)} %collective-permute-done.1, f32[1152,1024]{1,0:T(8,128)} %broadcast_select_fusion, pred[]{:T(512)S(6)} %eq.25, pred[1152]{0:T(1024)(128)(4,1)S(1)} %broadcast_compare_fusion), kind=kOutput, calls=%fused_computation.2 | convolution fusion | flops 907444224 | bytes 11142273 | tf_op jit(solution)/shard_map/dot_general | solution.py:472
  382.4 5.4 %convolution_select_fusion = f32[1152,256]{1,0:T(8,128)} fusion(f32[1152,1024]{1,0:T(8,128)} %collective-permute-done.1, f32[1152,1024]{1,0:T(8,128)} %broadcast_select_fusion, pred[]{:T(512)S(6)} %eq.25, f32[1024,1024]{1,0:T(8,128)S(1)} %factor.1, s32[]{:T(128)S(6)} %select_n.293, s32[256]{0:T(256)S(1)} %fusion.9, s32[1152]{0:T(1024)S(1)} %iota_add_fusion), kind=kOutput, calls=%fused_computation | convolution fusion | flops 1813708800 | bytes 11674629 | tf_op jit(solution)/shard_map/dot_general | solution.py:462
  (30 shorter events, 0.5 us)
Async XLA Ops:
  5.5 1.6 copy-start.1
  25.0 2.0 copy-start
  38.9 98.2 %all-to-all-start.1 = ((f32[32,8,32,128]{3,2,1,0:T(8,128)}), f32[32,8,32,128]{3,2,1,0:T(8,128)}, u32[]{:S(2)}, u32[]{:S(2)}) async-start(f32[32,8,32,128]{3,2,1,0:T(8,128)} %bitcast.21), calls=%async_computation.1 | async-start | bytes 8388608 | tf_op jit(solution)/shard_map/all_to_all | solution.py:432
  43.6 3.0 collective-permute-start.2
  48.2 48.6 %collective-permute-start.3 = (f32[1152,128]{1,0:T(8,128)S(1)}, f32[1152,128]{1,0:T(8,128)S(1)}, u32[]{:S(2)}, u32[]{:S(2)}) collective-permute-start(f32[1152,128]{1,0:T(8,128)S(1)} %slice_select_fusion.4), channel_id=1, source_target_pairs={{0,2},{1,3},{2,0},{3,1},{4,6},{5,7},{6,4},{7,5},{8,10},{9,11},{10,... | collective-permute-start | bytes 1769480 | tf_op jit(solution)/shard_map/ppermute | solution.py:368
  97.0 77.1 %collective-permute-start.4 = (f32[576,128]{1,0:T(8,128)S(1)}, f32[576,128]{1,0:T(8,128)S(1)}, u32[]{:S(2)}, u32[]{:S(2)}) collective-permute-start(f32[576,128]{1,0:T(8,128)S(1)} %slice_select_fusion.6), channel_id=1, source_target_pairs={{0,4},{1,5},{2,6},{3,7},{4,0},{5,1},{6,2},{7,3},{8,12},{9,13},{10,... | collective-permute-start | bytes 884744 | tf_op jit(solution)/shard_map/ppermute | solution.py:368
  172.8 88.1 %collective-permute-start = (f32[1152,1024]{1,0:T(8,128)}, f32[1152,1024]{1,0:T(8,128)}, u32[]{:S(2)}, u32[]{:S(2)}) collective-permute-start(f32[1152,1024]{1,0:T(8,128)} %get-tuple-element.9), channel_id=1, source_target_pairs={{0,2},{4,6},{8,10},{12,14},{16,18},{20,22},{24,26},{28,30}} | collective-permute-start | bytes 14155784 | tf_op jit(solution)/shard_map/ppermute | solution.py:397
  174.1 18.7 %copy-start.2 = (f32[4,1152,128]{2,1,0:T(8,128)S(1)}, f32[4,1152,128]{2,1,0:T(8,128)}, u32[]{:S(2)}) copy-start(f32[4,1152,128]{2,1,0:T(8,128)} %get-tuple-element.11) | copy-start | bytes 7077892
  174.2 5.2 %collective-permute-start.5 = (f32[288,128]{1,0:T(8,128)S(1)}, f32[288,128]{1,0:T(8,128)S(1)}, u32[]{:S(2)}, u32[]{:S(2)}) collective-permute-start(f32[288,128]{1,0:T(8,128)S(1)} %slice_select_fusion.7), channel_id=1, source_target_pairs={{0,8},{1,9},{2,10},{3,11},{4,12},{5,13},{6,14},{7,15},{8,0},{9,1},... | collective-permute-start | bytes 442376 | tf_op jit(solution)/shard_map/ppermute | solution.py:368
  179.5 5.7 %collective-permute-start.6 = (f32[144,128]{1,0:T(8,128)S(1)}, f32[144,128]{1,0:T(8,128)S(1)}, u32[]{:S(2)}, u32[]{:S(2)}) collective-permute-start(f32[144,128]{1,0:T(8,128)S(1)} %slice_select_fusion.8), channel_id=1, source_target_pairs={{0,16},{1,17},{2,18},{3,19},{4,20},{5,21},{6,22},{7,23},{8,24},{9,... | collective-permute-start | bytes 221192 | tf_op jit(solution)/shard_map/ppermute | solution.py:368
  185.2 7.6 %collective-permute-start.7 = (f32[144,128]{1,0:T(8,128)S(1)}, f32[144,128]{1,0:T(8,128)S(1)}, u32[]{:S(2)}, u32[]{:S(2)}) collective-permute-start(f32[144,128]{1,0:T(8,128)S(1)} %select_add_fusion.5), channel_id=1, source_target_pairs={{0,16},{1,17},{2,18},{3,19},{4,20},{5,21},{6,22},{7,23},{8,24},{9,... | collective-permute-start | bytes 221192 | tf_op jit(solution)/shard_map/ppermute | solution.py:368
  192.8 5.9 %collective-permute-start.8 = (f32[288,128]{1,0:T(8,128)S(1)}, f32[288,128]{1,0:T(8,128)S(1)}, u32[]{:S(2)}, u32[]{:S(2)}) collective-permute-start(f32[288,128]{1,0:T(8,128)S(1)} %pad_maximum_fusion.4), channel_id=1, source_target_pairs={{0,8},{1,9},{2,10},{3,11},{4,12},{5,13},{6,14},{7,15},{8,0},{9,1},... | collective-permute-start | bytes 442376 | tf_op jit(solution)/shard_map/ppermute | solution.py:368
  194.0 66.6 %collective-permute-start.12 = (f32[2304,128]{1,0:T(8,128)}, f32[2304,128]{1,0:T(8,128)S(1)}, u32[]{:S(2)}, u32[]{:S(2)}) collective-permute-start(f32[2304,128]{1,0:T(8,128)} %bitcast.12), channel_id=1, source_target_pairs={{0,2},{1,3},{2,0},{3,1},{4,6},{5,7},{6,4},{7,5},{8,10},{9,11},{10,... | collective-permute-start | bytes 3538952 | tf_op jit(solution)/shard_map/ppermute | solution.py:368
  198.8 8.4 %collective-permute-start.9 = (f32[576,128]{1,0:T(8,128)S(1)}, f32[576,128]{1,0:T(8,128)S(1)}, u32[]{:S(2)}, u32[]{:S(2)}) collective-permute-start(f32[576,128]{1,0:T(8,128)S(1)} %pad_maximum_fusion.3), channel_id=1, source_target_pairs={{0,4},{1,5},{2,6},{3,7},{4,0},{5,1},{6,2},{7,3},{8,12},{9,13},{10,... | collective-permute-start | bytes 884744 | tf_op jit(solution)/shard_map/ppermute | solution.py:368
  207.2 64.3 %collective-permute-start.10 = (f32[1152,128]{1,0:T(8,128)S(1)}, f32[1152,128]{1,0:T(8,128)S(1)}, u32[]{:S(2)}, u32[]{:S(2)}) collective-permute-start(f32[1152,128]{1,0:T(8,128)S(1)} %pad_maximum_fusion.2), channel_id=1, source_target_pairs={{0,2},{1,3},{2,0},{3,1},{4,6},{5,7},{6,4},{7,5},{8,10},{9,11},{10,... | collective-permute-start | bytes 1769480 | tf_op jit(solution)/shard_map/ppermute | solution.py:368
  260.8 11.9 %collective-permute-start.13 = (f32[1152,128]{1,0:T(8,128)S(1)}, f32[1152,128]{1,0:T(8,128)S(1)}, u32[]{:S(2)}, u32[]{:S(2)}) collective-permute-start(f32[1152,128]{1,0:T(8,128)S(1)} %slice_select_fusion.3), channel_id=1, source_target_pairs={{0,1},{1,0},{2,3},{3,2},{4,5},{5,4},{6,7},{7,6},{8,9},{9,8},{10,11... | collective-permute-start | bytes 1769480 | tf_op jit(solution)/shard_map/ppermute | solution.py:368
  267.0 110.2 %collective-permute-start.1 = (f32[1152,1024]{1,0:T(8,128)}, f32[1152,1024]{1,0:T(8,128)}, u32[]{:S(2)}, u32[]{:S(2)}) collective-permute-start(f32[1152,1024]{1,0:T(8,128)} %broadcast_select_fusion), channel_id=1, source_target_pairs={{0,1},{2,3},{4,5},{6,7},{8,9},{10,11},{12,13},{14,15},{16,17},{18,... | collective-permute-start | bytes 14155784 | tf_op jit(solution)/shard_map/ppermute | solution.py:397
  272.7 16.8 %collective-permute-start.11 = (f32[2304,128]{1,0:T(8,128)}, f32[2304,128]{1,0:T(8,128)S(1)}, u32[]{:S(2)}, u32[]{:S(2)}) collective-permute-start(f32[2304,128]{1,0:T(8,128)} %pad_maximum_fusion.1), channel_id=1, source_target_pairs={{0,1},{1,0},{2,3},{3,2},{4,5},{5,4},{6,7},{7,6},{8,9},{9,8},{10,11... | collective-permute-start | bytes 3538952 | tf_op jit(solution)/shard_map/ppermute | solution.py:368
  272.9 15.2 %collective-permute-start.14 = (f32[1024,128]{1,0:T(8,128)S(1)}, f32[1024,128]{1,0:T(8,128)}, u32[]{:S(2)}, u32[]{:S(2)}) collective-permute-start(f32[1024,128]{1,0:T(8,128)S(1)} %slice_select_fusion.5), channel_id=1, source_target_pairs={{0,16},{1,17},{2,18},{3,19}} | collective-permute-start | bytes 1572872 | tf_op jit(solution)/shard_map/ppermute | solution.py:397
  288.1 12.6 %collective-permute-start.15 = (f32[1024,128]{1,0:T(8,128)S(1)}, f32[1024,128]{1,0:T(8,128)S(1)}, u32[]{:S(2)}, u32[]{:S(2)}) collective-permute-start(f32[1024,128]{1,0:T(8,128)S(1)} %broadcast_select_fusion.8), channel_id=1, source_target_pairs={{0,8},{16,24},{1,9},{17,25},{2,10},{18,26},{3,11},{19,27}} | collective-permute-start | bytes 1572872 | tf_op jit(solution)/shard_map/ppermute | solution.py:397
  300.8 71.1 %collective-permute-start.16 = (f32[1024,128]{1,0:T(8,128)S(1)}, f32[1024,128]{1,0:T(8,128)S(1)}, u32[]{:S(2)}, u32[]{:S(2)}) collective-permute-start(f32[1024,128]{1,0:T(8,128)S(1)} %broadcast_select_fusion.9), channel_id=1, source_target_pairs={{0,4},{8,12},{16,20},{24,28},{1,5},{9,13},{17,21},{25,29},{2,6},{1... | collective-permute-start | bytes 1572872 | tf_op jit(solution)/shard_map/ppermute | solution.py:397

commit v2 on v1

v2 whole, which is shorter than its diff:
```python
import functools

import jax
import jax.numpy as jnp
import numpy as np
from jax import lax
from jax.experimental import pallas as pl
from jax.experimental.pallas import tpu as pltpu
from jax.sharding import PartitionSpec as P

NB = 512
PANELS = 2
PD = NB * PANELS
TB = 64
SLOTS = 32
LANES = 128
NBLK = PD // LANES
PACKED = NBLK * (NBLK + 1) // 2
AXES = ("row", "col")
HIGH = lax.Precision.HIGHEST
MIB = 1 << 20
PIECES = 3


def block_index(r, c):
    return r * (r + 1) // 2 + c


def left_half(shape):
    return lax.broadcasted_iota(jnp.int32, shape, len(shape) - 1) < TB


def magic(divisor, limit):
    x = np.arange(limit, dtype=np.int64)
    for shift in range(8, 31):
        m = (1 << shift) // divisor + 1
        if m * limit < 1 << 31 and np.array_equal((x * m) >> shift, x // divisor):
            return m, shift
    raise ValueError("no multiplier")


def quotient(x, divisor, limit):
    m, shift = magic(divisor, limit)
    return (x * m) >> shift


def is_live(count_ref, t):
    return t % SLOTS < count_ref[t // SLOTS]


def pick_kernel(
    held, most, grid,
    target_ref, count_ref,
    tiles_ref,
    out_ref,
    flat_ref, pair_ref, label_ref, filled_ref,
):
    half = TB // 2
    side = PD // TB
    filled_ref[0] = 0
    for s in range(most):
        label_ref[s] = -1

    def look(t, carry):
        r = quotient(target_ref[t], grid, grid * grid)
        c = target_ref[t] - r * grid

        @pl.when(is_live(count_ref, t) & (r < side) & (c < side))
        def _():
            left = left_half((half, LANES))
            group = tiles_ref[pl.ds(pl.multiple_of(t // 8 * 8, 8), 8), :]
            row = lax.broadcasted_iota(jnp.int32, group.shape, 0)
            line = jnp.sum(jnp.where(row == t % 8, group, 0.0), axis=0, keepdims=True)
            for k in range(half):
                flat_ref[k : k + 1, :] = line[:, k * LANES : (k + 1) * LANES]
            flat = flat_ref[...]
            turned = pltpu.roll(flat, TB, 1)
            pair_ref[pl.ds(0, half, stride=2), :] = jnp.where(left, flat, turned)
            pair_ref[pl.ds(1, half, stride=2), :] = jnp.where(left, turned, flat)
            natural = pair_ref[...]
            mirrored = natural.T[:TB]
            mirrored = jnp.concatenate([mirrored, mirrored], axis=1)
            swap = r // 2 > c // 2
            value = jnp.where(swap, mirrored, natural) * jnp.where(r // 2 == c // 2, 2.0, 1.0)
            filled = filled_ref[0]
            out_ref[pl.ds(pl.multiple_of(filled * half, half), half), :] = jnp.where(left, value[:half], pltpu.roll(value[half:], TB, 1))
            label_ref[filled] = jnp.where(swap, c * side + r, r * side + c)
            filled_ref[0] = filled + 1

        return carry

    lax.fori_loop(0, held, look, 0)
    lane = lax.broadcasted_iota(jnp.int32, (8, LANES), 1)
    line = jnp.full((8, LANES), -1, jnp.int32)
    for s in range(most):
        line = jnp.where(lane == s, label_ref[s], line)
    out_ref[most * half : most * half + 8, :] = line.astype(jnp.float32)


def pick(target, count, child_tiles, most, grid):
    held = child_tiles.shape[0]
    smem = pl.BlockSpec(memory_space=pltpu.SMEM)
    rows = most * TB // 2 + 8
    return pl.pallas_call(
        functools.partial(pick_kernel, held, most, grid),
        grid=(1,),
        out_shape=jax.ShapeDtypeStruct((rows, LANES), jnp.float32),
        in_specs=[smem] * 2 + [pl.BlockSpec((held, TB * TB), lambda i: (0, 0))],
        out_specs=pl.BlockSpec((rows, LANES), lambda i: (0, 0)),
        scratch_shapes=[
            pltpu.VMEM((TB // 2, LANES), jnp.float32),
            pltpu.VMEM((TB, LANES), jnp.float32),
            pltpu.SMEM((most,), jnp.int32),
            pltpu.SMEM((1,), jnp.int32),
        ],
        compiler_params=pltpu.CompilerParams(vmem_limit_bytes=16 * MIB),
        name="pick",
    )(target, count, child_tiles)


def stage_kernel(
    held, devices, capacity, grid, tile_rows, tile_cols, col_count,
    target_ref, tally_ref,
    tiles_ref,
    out_ref,
    flat_ref, pair_ref, count_ref, slot_ref, landing_ref,
):
    half = TB // 2
    for d in range(devices):
        count_ref[d] = 0

    def clear(s, carry):
        landing_ref[s] = -1
        return carry

    lax.fori_loop(0, devices * capacity, clear, 0)

    def spread_out(g, carry):
        rows = tiles_ref[pl.ds(pl.multiple_of(g * 8, 8), 8), :]
        for k in range(half):
            flat_ref[pl.ds(g * 8 * half + k, 8, stride=half), :] = rows[:, k * LANES : (k + 1) * LANES]
        return carry

    lax.fori_loop(0, held // 8, spread_out, 0)

    def assign(t, carry):
        alive = is_live(tally_ref, t)
        r = quotient(target_ref[t], grid, grid * grid)
        c = target_ref[t] - r * grid
        for m, (a, b) in enumerate(((r, c), (c, r))):
            home = quotient(a, tile_rows, grid)
            side = quotient(b, tile_cols, grid)
            owner = home * col_count + side
            place = (a - home * tile_rows) * tile_cols + (b - side * tile_cols)
            filled = count_ref[owner]
            count_ref[owner] = filled + 1
            slot = owner * capacity + filled
            slot_ref[m * held + t] = owner * (capacity * half + 8) + filled * half
            landing_ref[slot] = jnp.where(alive, place, -1)
        return carry

    lax.fori_loop(0, held, assign, 0, unroll=4)

    def put(index, value):
        out_ref[pl.ds(pl.multiple_of(slot_ref[index], 8), half), :] = value

    def quad(q, carry):
        left = left_half((half, LANES))
        naturals = []
        for p in range(2):
            a = flat_ref[pl.ds(pl.multiple_of((4 * q + 2 * p) * half, half), half), :]
            b = flat_ref[pl.ds(pl.multiple_of((4 * q + 2 * p + 1) * half, half), half), :]
            pair_ref[p, pl.ds(0, half, stride=2), :] = jnp.where(left, a, pltpu.roll(b, TB, 1))
            pair_ref[p, pl.ds(1, half, stride=2), :] = jnp.where(left, pltpu.roll(a, TB, 1), b)
            naturals.append(pair_ref[p, :, :])
        turned = jnp.concatenate(naturals, axis=0).T
        for m, values, order in (
            (0, naturals[0], (0, 1)),
            (0, naturals[1], (2, 3)),
            (1, turned[:TB], (0, 2)),
            (1, turned[TB:], (1, 3)),
        ):
            up, low = values[:half], values[half:]
            put(m * held + 4 * q + order[0], jnp.where(left, up, pltpu.roll(low, TB, 1)))
            put(m * held + 4 * q + order[1], jnp.where(left, pltpu.roll(up, TB, 1), low))
        return carry

    lax.fori_loop(0, held // 4, quad, 0, unroll=2)

    lane = lax.broadcasted_iota(jnp.int32, (8, LANES), 1)

    def label(d, carry):
        line = jnp.full((8, LANES), -1, jnp.int32)
        for s in range(capacity):
            line = jnp.where(lane == s, landing_ref[d * capacity + s], line)
        at = d * (capacity * half + 8) + capacity * half
        out_ref[pl.ds(pl.multiple_of(at, 8), 8), :] = line.astype(jnp.float32)
        return carry

    lax.fori_loop(0, devices, label, 0)


def stage(target, tally, child_tiles, devices, capacity, grid, tile_rows, tile_cols, col_count):
    held = child_tiles.shape[0]
    half = TB // 2
    smem = pl.BlockSpec(memory_space=pltpu.SMEM)
    rows = devices * (capacity * half + 8)
    return pl.pallas_call(
        functools.partial(stage_kernel, held, devices, capacity, grid, tile_rows, tile_cols, col_count),
        grid=(1,),
        out_shape=jax.ShapeDtypeStruct((rows, LANES), jnp.float32),
        in_specs=[smem] * 2 + [pl.BlockSpec((held, TB * TB), lambda i: (0, 0))],
        out_specs=pl.BlockSpec((rows, LANES), lambda i: (0, 0)),
        scratch_shapes=[
            pltpu.VMEM((held * half, LANES), jnp.float32),
            pltpu.VMEM((2, TB, LANES), jnp.float32),
            pltpu.SMEM((devices,), jnp.int32),
            pltpu.SMEM((2 * held,), jnp.int32),
            pltpu.SMEM((devices * capacity,), jnp.int32),
        ],
        compiler_params=pltpu.CompilerParams(vmem_limit_bytes=24 * MIB),
        name="stage",
    )(target, tally, child_tiles)


def split(x):
    high = x.astype(jnp.bfloat16)
    return high, (x - high.astype(jnp.float32)).astype(jnp.bfloat16)


def dot3(left_high, left_low, right_high, right_low):
    dot = functools.partial(jnp.dot, preferred_element_type=jnp.float32)
    return dot(left_high, right_high) + (dot(left_high, right_low) + dot(left_low, right_high))


def lane_splat(x, lane):
    return jnp.broadcast_to(x[:, lane : lane + 1], x.shape)


def row_splat(ref, row):
    return jnp.broadcast_to(ref[row : row + 1, :], (8, LANES))


def inverse_factor(strips, splat_ref):
    strips = list(strips)
    lane = lax.broadcasted_iota(jnp.int32, (8, LANES), 1)
    sub = lax.broadcasted_iota(jnp.int32, (8, LANES), 0)
    result = []
    for k in range(LANES // 8):
        strip = strips[k]
        columns = [lane_splat(strip, 8 * k + t) for t in range(8)]
        for t in range(8):
            splat_ref[8 * t : 8 * t + 8, :] = columns[t]
        e = [[row_splat(splat_ref, 8 * t + s) if s <= t else None for t in range(8)] for s in range(8)]
        low = [[None] * 8 for _ in range(8)]
        inv = [None] * 8
        for s in range(8):
            inv[s] = lax.rsqrt(e[s][s])
            for t in range(s + 1, 8):
                low[t][s] = e[s][t] * inv[s]
            for t in range(s + 1, 8):
                for u in range(t, 8):
                    e[t][u] = e[t][u] - low[t][s] * low[u][s]
        li = [[None] * 8 for _ in range(8)]
        for s in range(8):
            li[s][s] = inv[s]
            for r in range(s + 1, 8):
                total = low[r][s] * li[s][s]
                for q in range(s + 1, r):
                    total = total + low[r][q] * li[q][s]
                li[r][s] = -inv[r] * total
        inside = (lane >= 8 * k) & (lane < 8 * k + 8)
        unit = jnp.where(lane - 8 * k == sub, 1.0, 0.0)
        strip = jnp.where(inside, unit, strip)
        splat_ref[64:72, :] = strip
        rows = [row_splat(splat_ref, 64 + s) for s in range(8)]
        u = []
        for r in range(8):
            total = li[r][0] * rows[0]
            for s in range(1, r + 1):
                total = total + li[r][s] * rows[s]
            u.append(total)
        mine = u[0]
        for r in range(1, 8):
            mine = jnp.where(sub == r, u[r], mine)
        result.append(jnp.where(lane < 8 * k + 8, mine, 0.0))
        if k + 1 == LANES // 8:
            break
        v = []
        for s in range(8):
            total = li[s][s] * u[s]
            for r in range(s + 1, 8):
                total = total + li[r][s] * u[r]
            v.append(total)
        for i in range(k + 1, LANES // 8):
            old = strips[i]
            total = lane_splat(old, 8 * k) * v[0]
            for s in range(1, 8):
                total = total + lane_splat(old, 8 * k + s) * v[s]
            strips[i] = jnp.where(inside, 0.0, old) - total
    return result


def factor_kernel(
    most, senders,
    label_ref, me_ref,
    front_ref, tiles_ref,
    packed_ref,
    out_ref, top_ref, small_ref, high_ref, low_ref, splat_ref, semaphore,
):
    @pl.when(me_ref[0] == 0)
    def _():
        copy = pltpu.make_async_copy(front_ref.at[:PD, :PD], out_ref, semaphore)
        copy.start()
        copy.wait()
        factor(most, senders, label_ref, front_ref, tiles_ref, packed_ref, out_ref, top_ref, small_ref, high_ref, low_ref, splat_ref)


def factor(most, senders, label_ref, front_ref, tiles_ref, packed_ref, out_ref, top_ref, small_ref, high_ref, low_ref, splat_ref):
    half = TB // 2
    side = PD // TB
    for r in range(NBLK):
        rows = slice(r * LANES, (r + 1) * LANES)
        if r > 0:
            out_ref[rows, : r * LANES] = jnp.zeros((LANES, r * LANES), jnp.float32)
    left = left_half((half, LANES))
    group = 8 if most * senders % 8 == 0 else 2

    def place(g, carry):
        parts = []
        for e in range(group):
            s = g * group + e
            p = label_ref[s]
            alive = p >= 0
            p = jnp.clip(p, 0, side * side - 1)
            r, c = p // side, p % side
            even = c % 2 == 0
            source = s // most * (most * half + 8) + s % most * half
            packed = tiles_ref[pl.ds(pl.multiple_of(source, 8), half), :]
            turned = pltpu.roll(packed, TB, 1)
            mask = (left == even) & alive
            top = jnp.where(mask, jnp.where(even, packed, turned), 0.0)
            low = jnp.where(mask, jnp.where(even, turned, packed), 0.0)
            parts.append((r, c // 2, top, low))
        for r, c, top, low in parts:
            cols = pl.ds(pl.multiple_of(c * LANES, LANES), LANES)
            out_ref[pl.ds(pl.multiple_of(r * TB, TB), half), cols] += top
            out_ref[pl.ds(pl.multiple_of(r * TB + half, half), half), cols] += low
        return carry

    lax.fori_loop(0, most * senders // group, place, 0)

    eye = jnp.where(
        lax.broadcasted_iota(jnp.int32, (LANES, LANES), 0) == lax.broadcasted_iota(jnp.int32, (LANES, LANES), 1), 1.0, 0.0
    )

    def outer(k, carry):
        at = pl.multiple_of(k * LANES, LANES)
        here = pl.ds(at, LANES)
        block = out_ref[here, here]
        block = 0.5 * (block + block.T)
        small_ref[...] = block
        strips = inverse_factor([small_ref[8 * i : 8 * i + 8, :] for i in range(LANES // 8)], splat_ref)
        for i, strip in enumerate(strips):
            small_ref[8 * i : 8 * i + 8, :] = strip
        out_ref[here, here] = eye
        top = dot3(*split(small_ref[...]), *split(out_ref[here, :]))
        top_ref[...] = top
        column = lax.broadcasted_iota(jnp.int32, (LANES, PD), 1)
        out_ref[here, :] = jnp.where(column < at + LANES, top, 0.0)
        high_ref[...], low_ref[...] = split(top)
        for step in range(NBLK - 1):

            @pl.when(k == step)
            def _():
                edge = (step + 1) * LANES
                for start in range(edge, PD, LANES):
                    there = slice(start, start + LANES)
                    across = split(top_ref[:, there].T)
                    out_ref[there, :edge] = jnp.where(
                        lax.broadcasted_iota(jnp.int32, (LANES, edge), 1) < edge - LANES, out_ref[there, :edge], 0.0
                    ) - dot3(*across, high_ref[:, :edge], low_ref[:, :edge])
                    out_ref[there, start:] -= dot3(*across, high_ref[:, start:], low_ref[:, start:])

        return carry

    lax.fori_loop(0, NBLK, outer, 0)
    for r in range(NBLK):
        for c in range(r + 1):
            base = block_index(r, c) * LANES
            packed_ref[base : base + LANES, :] = out_ref[r * LANES : (r + 1) * LANES, c * LANES : (c + 1) * LANES]


def inverse_of_factor(label, me, front, tiles, most, senders):
    smem = pl.BlockSpec(memory_space=pltpu.SMEM)
    return pl.pallas_call(
        functools.partial(factor_kernel, most, senders),
        grid=(1,),
        out_shape=jax.ShapeDtypeStruct((PACKED * LANES, LANES), jnp.float32),
        in_specs=[smem, smem, pl.BlockSpec(memory_space=pl.ANY), pl.BlockSpec(tiles.shape, lambda i: (0, 0))],
        out_specs=pl.BlockSpec((PACKED * LANES, LANES), lambda i: (0, 0)),
        scratch_shapes=[
            pltpu.VMEM((PD, PD), jnp.float32),
            pltpu.VMEM((LANES, PD), jnp.float32),
            pltpu.VMEM((LANES, LANES), jnp.float32),
            pltpu.VMEM((LANES, PD), jnp.bfloat16),
            pltpu.VMEM((LANES, PD), jnp.bfloat16),
            pltpu.VMEM((72, LANES), jnp.float32),
            pltpu.SemaphoreType.DMA,
        ],
        compiler_params=pltpu.CompilerParams(vmem_limit_bytes=56 * MIB),
        name="factor",
    )(label, me, front, tiles)


def unpack_kernel(packed_ref, out_ref):
    for r in range(NBLK):
        for c in range(NBLK):
            rows, cols = slice(r * LANES, (r + 1) * LANES), slice(c * LANES, (c + 1) * LANES)
            if c > r:
                out_ref[rows, cols] = jnp.zeros((LANES, LANES), jnp.float32)
            else:
                base = block_index(r, c) * LANES
                out_ref[rows, cols] = packed_ref[base : base + LANES, :]


def unpack(packed):
    vmem = pl.BlockSpec(memory_space=pltpu.VMEM)
    return pl.pallas_call(
        unpack_kernel,
        out_shape=jax.ShapeDtypeStruct((PD, PD), jnp.float32),
        in_specs=[vmem],
        out_specs=vmem,
        compiler_params=pltpu.CompilerParams(vmem_limit_bytes=16 * MIB),
        name="unpack",
    )(packed)


def assemble_kernel(
    slots, capacity, tile_cols, limit, row_chunk, width, order,
    landing_ref, first_ref,
    front_ref, incoming_ref, probe_ref,
    product_ref, *rest,
):
    panels, (matrix_ref, high_ref, low_ref, semaphore) = rest[:-4], rest[-4:]
    copy = pltpu.make_async_copy(front_ref, matrix_ref, semaphore)
    copy.start()
    step = 256 if probe_ref.shape[0] % 256 == 0 else 128
    half = TB // 2

    def cut(s, carry):
        rows = pl.ds(pl.multiple_of(s * step, step), step)
        index = lax.broadcasted_iota(jnp.int32, (step, probe_ref.shape[1]), 0) + s * step
        high, low = split(jnp.where(index >= first_ref[0], probe_ref[rows, :], 0.0))
        high_ref[rows, :] = high
        low_ref[rows, :] = low
        return carry

    lax.fori_loop(0, probe_ref.shape[0] // step, cut, 0)
    copy.wait()
    block = capacity * half + 8
    group = 8 if slots % 8 == 0 else 2
    left = left_half((half, LANES))

    def place(g, carry):
        parts = []
        for e in range(group):
            s = g * group + e
            p = landing_ref[s]
            alive = p >= 0
            p = jnp.maximum(p, 0)
            r = quotient(p, tile_cols, limit)
            c = p - r * tile_cols
            even = c % 2 == 0
            source = s // capacity * block + s % capacity * half
            packed = incoming_ref[pl.ds(pl.multiple_of(source, 8), half), :]
            turned = pltpu.roll(packed, TB, 1)
            mask = (left == even) & alive
            top = jnp.where(mask, jnp.where(even, packed, turned), 0.0)
            low = jnp.where(mask, jnp.where(even, turned, packed), 0.0)
            parts.append((r, c // 2, top, low))
        for r, c, top, low in parts:
            cols = pl.ds(pl.multiple_of(c * LANES, LANES), LANES)
            matrix_ref[pl.ds(pl.multiple_of(r * TB, TB), half), cols] += top
            matrix_ref[pl.ds(pl.multiple_of(r * TB + half, half), half), cols] += low
        return carry

    lax.fori_loop(0, slots // group, place, 0)
    rows = matrix_ref.shape[0] // len(panels)
    for i, panel_ref in enumerate(panels):
        panel_ref[...] = matrix_ref[i * rows : (i + 1) * rows, :PD]

    def multiply(b, carry):
        rows = pl.ds(pl.multiple_of(b * row_chunk, row_chunk), row_chunk)
        high, low = split(matrix_ref[rows, :])
        dot = functools.partial(jnp.dot, preferred_element_type=jnp.float32)
        total = dot(high, high_ref[...]) + (dot(high, low_ref[...]) + dot(low, high_ref[...]))
        for j, at in enumerate(order):
            product_ref[at, rows, :] = total[:, j * width : (j + 1) * width]
        return carry

    lax.fori_loop(0, matrix_ref.shape[0] // row_chunk, multiply, 0)


def assemble(landing, first, front, incoming, probe, capacity, tile_rows, tile_cols, order):
    local_rows, local_cols = front.shape
    columns = probe.shape[1]
    width = columns // len(order)
    smem = pl.BlockSpec(memory_space=pltpu.SMEM)
    vmem = pl.BlockSpec(memory_space=pltpu.VMEM)
    row_chunk = 192 if local_rows % 192 == 0 else 64
    return pl.pallas_call(
        functools.partial(
            assemble_kernel, landing.shape[0], capacity, tile_cols, tile_rows * tile_cols, row_chunk, width, order
        ),
        out_shape=(jax.ShapeDtypeStruct((len(order), local_rows, width), jnp.float32),)
        + (jax.ShapeDtypeStruct((local_rows // PIECES, PD), jnp.float32),) * PIECES,
        in_specs=[smem] * 2 + [pl.BlockSpec(memory_space=pl.ANY), vmem, vmem],
        out_specs=(vmem,) * (1 + PIECES),
        scratch_shapes=[
            pltpu.VMEM((local_rows, local_cols), jnp.float32),
            pltpu.VMEM((local_cols, columns), jnp.bfloat16),
            pltpu.VMEM((local_cols, columns), jnp.bfloat16),
            pltpu.SemaphoreType.DMA,
        ],
        compiler_params=pltpu.CompilerParams(vmem_limit_bytes=56 * MIB),
        name="assemble",
    )(landing, first, front, incoming, probe)


def finish_kernel(
    sources, width,
    where_ref, *refs,
):
    panels = refs[: sources * PIECES]
    inverse_ref, weights_ref, share_ref, solved_ref, sketch_ref, panel_ref, semaphore = refs[sources * PIECES :]
    col, row_start = where_ref[0], where_ref[1]
    piece = panel_ref.shape[0] // PIECES
    for j in range(sources):

        @pl.when(col == j)
        def _():
            moves = [
                pltpu.make_async_copy(panels[j * PIECES + i], panel_ref.at[i * piece : (i + 1) * piece], semaphore.at[i])
                for i in range(PIECES)
            ]
            for move in moves:
                move.start()
            for move in moves:
                move.wait()

    right_high, right_low = split(jnp.concatenate([inverse_ref[...].T, weights_ref[...]], axis=1))
    dot = functools.partial(jnp.dot, preferred_element_type=jnp.float32)
    step = 192 if panel_ref.shape[0] % 192 == 0 else 64

    def body(b, carry):
        rows = pl.ds(pl.multiple_of(b * step, step), step)
        high, low = split(panel_ref[rows, :])
        total = dot(high, right_high) + (dot(high, right_low) + dot(low, right_high))
        index = row_start + b * step + lax.broadcasted_iota(jnp.int32, (step, width), 0)
        column = col * width + lax.broadcasted_iota(jnp.int32, (step, width), 1)
        solved_ref[rows, :] = jnp.where(index >= (column // NB) * NB, total[:, :width], 0.0)
        rest = share_ref[rows, :] - total[:, width:]
        index = row_start + b * step + lax.broadcasted_iota(jnp.int32, rest.shape, 0)
        sketch_ref[rows, :] = jnp.where(index >= PD, rest, 0.0)
        return carry

    lax.fori_loop(0, panel_ref.shape[0] // step, body, 0)


def finish(where, panels, inverse, weights, share):
    local_rows = share.shape[0]
    width = inverse.shape[0]
    vmem = pl.BlockSpec(memory_space=pltpu.VMEM)
    return pl.pallas_call(
        functools.partial(finish_kernel, len(panels), width),
        out_shape=(
            jax.ShapeDtypeStruct((local_rows, width), jnp.float32),
            jax.ShapeDtypeStruct(share.shape, jnp.float32),
        ),
        in_specs=[pl.BlockSpec(memory_space=pltpu.SMEM)] + [pl.BlockSpec(memory_space=pl.ANY)] * (len(panels) * PIECES) + [vmem] * 3,
        out_specs=(vmem, vmem),
        scratch_shapes=[pltpu.VMEM((local_rows, PD), jnp.float32), pltpu.SemaphoreType.DMA((PIECES,))],
        compiler_params=pltpu.CompilerParams(vmem_limit_bytes=28 * MIB),
        name="finish",
    )(where, *sum(panels, []), inverse, weights, share)


def masks(count):
    return [1 << b for b in range(count.bit_length() - 1)]


def exchange(x, axis, mask, count):
    return lax.ppermute(x, axis, [(d, d ^ mask) for d in range(count)])


def choose(bit, x):
    h = x.shape[0] // 2
    return jnp.where(bit, x[h:], x[:h]), jnp.where(bit, x[:h], x[h:])


def halve(x, axis, index, mask, count):
    keep, send = choose((index & mask) != 0, x)
    return keep + exchange(send, axis, mask, count)


def double(x, axis, index, mask, count):
    other = exchange(x, axis, mask, count)
    bit = (index & mask) != 0
    return jnp.concatenate([jnp.where(bit, other, x), jnp.where(bit, x, other)], axis=0)


def all_sum(x, axis, index, order, count):
    for mask in order:
        x = halve(x, axis, index, mask, count)
    for mask in order[::-1]:
        x = double(x, axis, index, mask, count)
    return x


def spread(x, axis, index, order, count):
    for mask in order:
        other = lax.ppermute(x, axis, [(d, d + mask) for d in range(0, count, 2 * mask)])
        x = jnp.where((index & (2 * mask - 1)) == mask, other, x)
    return x


def collect(x, count, inner):
    return [x] + [
        lax.ppermute(x, AXES, [(d + e, e) for e in range(inner)]) for d in range(inner, count, inner)
    ]


def collect_last(x, inner):
    return [x] + [lax.ppermute(x, AXES, [(e, 0)]) for e in range(1, inner)]


def scatter(x, axis, index, order, count):
    done = 0
    for mask in order:
        pairs = [(d, d + mask) for d in range(count) if d & done == d]
        h = x.shape[0] // 2
        x = jnp.where((index & mask) != 0, lax.ppermute(x[h:], axis, pairs), x[:h])
        done |= mask
    return x


def bits_reversed(count):
    width = count.bit_length() - 1
    return [sum(((j >> b) & 1) << (width - 1 - b) for b in range(width)) for j in range(count)]


def per_device(front, child_tiles, tile_target, tile_count, probe):
    row_count = lax.axis_size("row")
    col_count = lax.axis_size("col")
    devices = row_count * col_count
    local_rows, local_cols = front.shape
    tile_rows = local_rows // TB
    tile_cols = local_cols // TB
    grid = tile_cols * col_count
    held = child_tiles.shape[0]
    capacity = 2 * max(1, (held + devices - 1) // devices)
    row_index = lax.axis_index("row")
    col_index = lax.axis_index("col")
    device = row_index * col_count + col_index
    half = TB // 2

    homes = (PD + local_rows - 1) // local_rows
    most = max(1, homes * capacity // 2)
    picked = pick(tile_target, tile_count, child_tiles, most, grid)
    inner = min(2, row_count) * col_count
    gathered = jnp.concatenate(collect(picked, devices, inner), axis=0)
    gathered, tile_target = lax.optimization_barrier((gathered, tile_target))
    outgoing = stage(tile_target, tile_count, child_tiles, devices, capacity, grid, tile_rows, tile_cols, col_count)
    gathered = jnp.concatenate(collect_last(gathered, inner), axis=0)
    gathered, outgoing = lax.optimization_barrier((gathered, outgoing))
    label = gathered.reshape(devices, -1, LANES)[:, most * half, :most].astype(jnp.int32).reshape(-1)
    corner = front
    if homes > 1:
        corner = [front[:, :PD]] + [lax.ppermute(front[:, :PD], "row", [(home, 0)]) for home in range(1, homes)]
        corner = jnp.concatenate(corner, axis=0)

    incoming = lax.all_to_all(
        outgoing.reshape(devices, capacity * half + 8, LANES), AXES, split_axis=0, concat_axis=0, tiled=True
    )

    packed = inverse_of_factor(label, device.reshape(1), corner, gathered, most, devices)
    order = masks(devices)
    order = order[:1] + [m for m in order[1:] if m >= col_count] + [m for m in order[1:] if m < col_count]
    part = scatter(packed, AXES, device, order, devices)
    part, incoming = lax.optimization_barrier((part, incoming))
    first = jnp.clip(PD - col_index * local_cols, 0, local_cols).reshape(1)
    landing = incoming[:, capacity * half, :capacity].astype(jnp.int32).reshape(-1)
    product, *panel = assemble(
        landing, first, front, incoming.reshape(-1, LANES), probe, capacity, tile_rows, tile_cols, bits_reversed(col_count)
    )

    share = product.reshape(-1, product.shape[2])
    order = order[::-1]
    sums = masks(col_count)
    panel_order = sums[::-1]
    held = {0: panel}
    ahead = lax.ppermute(panel[0], "col", [(0, panel_order[0])])
    for mask in sums[:-1]:
        share = halve(share, "col", col_index, mask, col_count)
    part = double(part, AXES, device, order[0], devices)
    share, part = lax.optimization_barrier((share, part))
    share = halve(share, "col", col_index, sums[-1], col_count)
    for mask in order[1:-2]:
        part = double(part, AXES, device, mask, devices)
    share, part, *later = lax.optimization_barrier((share, part, *panel[1:]))
    part = double(part, AXES, device, order[-2], devices)
    held[panel_order[0]] = [ahead] + [lax.ppermute(piece, "col", [(0, panel_order[0])]) for piece in later]

    top_order = masks(row_count)[::-1]
    if homes == 1:
        top = spread(share[:PD], "row", row_index, top_order[:1], row_count)
        part = double(part, AXES, device, order[-1], devices)
        top = spread(top, "row", row_index, top_order[1:], row_count)
    else:
        pieces = []
        for home in range(homes):
            rows = min(PD - home * local_rows, local_rows)
            pieces.append(jnp.where(row_index == home, share[:rows], 0.0))
        top = all_sum(jnp.concatenate(pieces, axis=0), "row", row_index, masks(row_count), row_count)
        part = double(part, AXES, device, order[-1], devices)
    inverse = unpack(part)

    for mask in panel_order:
        for d in range(0, col_count, 2 * mask):
            if d + mask not in held:
                held[d + mask] = [lax.ppermute(piece, "col", [(d, d + mask)]) for piece in held[d]]
    panels = [held[d] for d in range(col_count)]

    dot = functools.partial(jnp.dot, precision=lax.Precision.HIGH, preferred_element_type=jnp.float32)
    weights = lax.dot_general(
        inverse, dot(inverse, top), (((0,), (0,)), ((), ())), precision=lax.Precision.HIGH, preferred_element_type=jnp.float32
    )
    width = PD // col_count
    mine = lax.dynamic_slice_in_dim(inverse, col_index * width, width, 0)
    return finish(jnp.stack([col_index, row_index * local_rows]), panels, mine, weights, share)


def solution(mesh):
    return jax.shard_map(
        per_device,
        mesh=mesh,
        in_specs=(
            P("row", "col"),
            P(("row", "col"), None),
            P(("row", "col")),
            P(("row", "col")),
            P("col", None),
        ),
        out_specs=(P("row", "col"), P("row", "col")),
        check_vma=False,
    )
```

time: 391 us -> 299 us (0.76)
  Pallas kernels: 123 us -> 53.5 us
  waiting for transfers between devices: 185 us -> 151 us
  starting transfers between devices: 30.6 us -> 63.9 us
  blocking collectives: 11.8 us -> 0 us
  matrix products: 15.8 us -> 6.34 us
  other arithmetic: 15.4 us -> 10.3 us
  local copies, waits for them, and re-layouts: 5.5 us -> 10.5 us
    ppermute x0 -> x24, waiting for transfers between devices: none -> 118 us  [the longest x5 84.2 us: scatter(): x = jnp.where(index & mask != 0, lax.ppermute(x[h:], axis, pairs), x[:h])]
    ppermute x12 -> x7, waiting for transfers between devices: 123 us -> 22.1 us  [exchange(): return lax.ppermute(x, axis, [(d, d ^ mask) for d in range(count)])]
    pallas_call x3 -> x6, Pallas kernels: 123 us -> 53.5 us  [the longest x1 24 us: assemble(): pl.pallas_call(functools.partial(assemble_kernel, landing.shape[0], capac...]
    all_to_all x1, waiting for transfers between devices: 39.1 us -> 1.26 us  [per_device(): lax.all_to_all(outgoing.reshape(devices, capacity * half + 8, LANES), AXE...]
    ppermute x0 -> x24, starting transfers between devices: none -> 26.6 us  [the longest x6 7.5 us: per_device(): lax.ppermute(piece, 'col', [(d, d + mask)])]
    all_to_all x1 -> x0, blocking collectives: 11.8 us -> none  [per_device(): lax.all_to_all(landing.reshape(devices, capacity), AXES, split_axis=0, co...]
    ppermute x5 -> x3, waiting for transfers between devices: 22.1 us -> 10.3 us  [spread(): lax.ppermute(x, axis, [(d, d + mask) for d in range(0, count, 2 * mask)])]
    dot_general x2 -> x0, matrix products: 10.6 us -> none  [the longest x1 5.41 us: per_device(): lax.dot_general(panel, mine, (((1,), (1,)), ((), ())), precision=lax.Prec...]
  transfers between devices with their start and end apart: 18 -> 35, of which waited for: 11 -> 14; matrix products, arithmetic and copies ran while one was open for 5% -> 5% of each run, Pallas kernels for 27% -> 5%
where the time goes in v2:
time: 299 us; the launch traced here: 298 us
  waiting for transfers between devices  151 us (51%)
  starting transfers between devices  63.9 us (21%)
  Pallas kernels  53.5 us (18%)
  local copies, waits for them, and re-layouts  10.5 us (4%)
  other arithmetic  10.3 us (3%)
  matrix products  6.34 us (2%)
    ppermute x5, waiting for transfers between devices, scatter(): x = jnp.where(index & mask != 0, lax.ppermute(x[h:], axis, pairs), x[:h])  84.2 us
    ppermute x2, waiting for transfers between devices, per_device(): lax.ppermute(piece, 'col', [(0, panel_order[0])])  26.9 us
    pallas_call x1, Pallas kernels, assemble(): pl.pallas_call(functools.partial(assemble_kernel, landing.shape[0], capac...  24 us
    ppermute x7, waiting for transfers between devices, exchange(): return lax.ppermute(x, axis, [(d, d ^ mask) for d in range(count)])  22.1 us
    all_to_all x1, starting transfers between devices, per_device(): lax.all_to_all(outgoing.reshape(devices, capacity * half + 8, LANES), AXE...  15.2 us
    ppermute x7, starting transfers between devices, exchange(): return lax.ppermute(x, axis, [(d, d ^ mask) for d in range(count)])  14.5 us
    pallas_call x1, Pallas kernels, stage(): pl.pallas_call(functools.partial(stage_kernel, held, devices, capacity, g...  12.9 us
    ppermute x3, waiting for transfers between devices, spread(): lax.ppermute(x, axis, [(d, d + mask) for d in range(0, count, 2 * mask)])  10.3 us
  transfers between devices with their start and end apart: 35, of which 14 were waited for; matrix products, arithmetic and copies ran while one was open for 5% of the time, Pallas kernels for 5%

profile of v2, /device:TPU:4, one launch (start us, length us, event | category | flops | bytes accessed | tf_op | source)
XLA Modules:
  0.0 297.6 jit_solution(16352709875382733133)
XLA Ops:
  0.6 1.6 copy-done.1
  3.5 3.9 %pick.1 = f32[136,128]{1,0:T(8,128)S(1)} custom-call(s32[128]{0:T(128)S(1)} %copy-done.6, s32[4]{0:T(128)S(1)} %copy-done.8, f32[128,4096]{1,0:T(8,128)S(1)} %copy-done.1), custom_call_target="tpu_custom_call" | custom-call | tf_op jit(solution)/shard_map/pick/pallas_call | solution.py:104
  7.4 1.3 collective-permute-start
  8.7 1.3 collective-permute-start.1
  10.0 1.3 collective-permute-start.2
  11.3 2.3 collective-permute-done
  13.6 2.2 collective-permute-done.1
  15.8 2.2 collective-permute-done.2
  18.0 0.7 collective-permute-start.3
  18.7 2.1 collective-permute-start.4
  20.8 0.7 collective-permute-start.5
  21.5 0.7 collective-permute-start.6
  22.2 0.7 collective-permute-start.7
  22.9 12.9 %stage.1 = f32[8448,128]{1,0:T(8,128)S(1)} custom-call(s32[128]{0:T(128)S(1)} %copy-done.7, s32[4]{0:T(128)S(1)} %copy-done.9, f32[128,4096]{1,0:T(8,128)S(1)} %copy-done.2), custom_call_target="tpu_custom_call" | custom-call | tf_op jit(solution)/shard_map/stage/pallas_call | solution.py:208
  35.8 2.0 copy-done
  38.6 0.7 collective-permute-start.9
  39.5 15.2 %all-to-all-start = ((f32[32,264,128]{2,1,0:T(8,128)}), f32[32,264,128]{2,1,0:T(8,128)}, u32[]{:S(2)}, u32[]{:S(2)}) async-start(f32[32,264,128]{2,1,0:T(8,128)} %bitcast.16), calls=%async_computation | async-start | bytes 8650752 | tf_op jit(solution)/shard_map/all_to_all | solution.py:683
  55.3 3.0 %factor.1 = f32[4608,128]{1,0:T(8,128)} custom-call(s32[128]{0:T(128)} %convert_element_type.15.label_ref, s32[1]{0:T(128)} %bitcast.3.me_ref, f32[1152,2304]{1,0:T(8,128)} %front_ref.3, f32[4352,128]{1,0:T(8,128)} %copy-done.11), custom_call_target="tpu_custom_call" | custom-call | tf_op jit(solution)/shard_map/factor/pallas_call | solution.py:396
  58.4 1.5 slice.75
  59.9 1.7 collective-permute-start.10
  61.8 0.7 collective-permute-start.11
  62.6 0.7 collective-permute-start.12
  63.4 0.7 collective-permute-start.13
  64.1 1.5 collective-permute-start.14
  65.6 84.2 %collective-permute-done.14 = f32[144,128]{1,0:T(8,128)S(1)} collective-permute-done((f32[144,128]{1,0:T(8,128)S(1)}, f32[144,128]{1,0:T(8,128)S(1)}, u32[]{:S(2)}, u32[]{:S(2)}) %collective-permute-start.14) | collective-permute-done | bytes 73760 | tf_op jit(solution)/shard_map/ppermute | solution.py:643
  149.8 1.3 all-to-all-done
  151.1 1.0 convert_reduce_fusion
  152.7 24.0 %assemble.1 = (f32[4,1152,128]{2,1,0:T(8,128)}, f32[384,1024]{1,0:T(8,128)}, f32[384,1024]{1,0:T(8,128)}, f32[384,1024]{1,0:T(8,128)}) custom-call(s32[256]{0:T(256)} %convert_element_type.17.landing_ref, s32[1]{0:T(128)} %bitcast.5.first_ref, f32[1152,2304]{1,0:T(8,128)} %front_ref.3, f32[8448,128]{1,0:T(8,128)} %bitcast.6.incoming_ref, f32[2304,512]{1,0:T(8,128)} %probe_ref.1), custom_call_target="tpu_custom_call" | custom-call | tf_op jit(solution)/shard_map/assemble/pallas_call | solution.py:512
  176.7 1.8 slice_select_fusion.2
  178.6 1.6 collective-permute-start.20
  180.1 3.1 %collective-permute-done.20 = f32[144,128]{1,0:T(8,128)S(1)} collective-permute-done((f32[144,128]{1,0:T(8,128)S(1)}, f32[144,128]{1,0:T(8,128)S(1)}, u32[]{:S(2)}, u32[]{:S(2)}) %collective-permute-start.20) | collective-permute-done | bytes 73760 | tf_op jit(solution)/shard_map/ppermute | solution.py:594
  183.4 2.3 collective-permute-start.22
  185.8 4.1 %collective-permute-done.22 = f32[288,128]{1,0:T(8,128)S(1)} collective-permute-done((f32[288,128]{1,0:T(8,128)S(1)}, f32[288,128]{1,0:T(8,128)S(1)}, u32[]{:S(2)}, u32[]{:S(2)}) %collective-permute-start.22) | collective-permute-done | bytes 147488 | tf_op jit(solution)/shard_map/ppermute | solution.py:594
  189.9 10.0 %collective-permute-start.23 = (f32[576,128]{1,0:T(8,128)S(1)}, f32[576,128]{1,0:T(8,128)S(1)}, u32[]{:S(2)}, u32[]{:S(2)}) collective-permute-start(f32[576,128]{1,0:T(8,128)S(1)} %pad_maximum_fusion.3), channel_id=1, source_target_pairs={{0,8},{1,9},{2,10},{3,11},{4,12},{5,13},{6,14},{7,15},{8,0},{9,1},... | collective-permute-start | bytes 884744 | tf_op jit(solution)/shard_map/ppermute | solution.py:594
  200.4 5.7 %collective-permute-done.23 = f32[576,128]{1,0:T(8,128)S(1)} collective-permute-done((f32[576,128]{1,0:T(8,128)S(1)}, f32[576,128]{1,0:T(8,128)S(1)}, u32[]{:S(2)}, u32[]{:S(2)}) %collective-permute-start.23) | collective-permute-done | bytes 294944 | tf_op jit(solution)/shard_map/ppermute | solution.py:594
  206.1 0.9 pad_maximum_fusion.2
  207.0 7.0 %collective-permute-done.21 = f32[1152,128]{1,0:T(8,128)S(1)} collective-permute-done((f32[1152,128]{1,0:T(8,128)S(1)}, f32[1152,128]{1,0:T(8,128)S(1)}, u32[]{:S(2)}, u32[]{:S(2)}) %collective-permute-start.21) | collective-permute-done | bytes 589856 | tf_op jit(solution)/shard_map/ppermute | solution.py:594
  214.1 0.8 slice.73
  214.9 4.2 %collective-permute-start.31 = (f32[1024,128]{1,0:T(8,128)}, f32[1024,128]{1,0:T(8,128)S(1)}, u32[]{:S(2)}, u32[]{:S(2)}) collective-permute-start(f32[1024,128]{1,0:T(8,128)} %slice.73), channel_id=1, source_target_pairs={{0,16},{1,17},{2,18},{3,19}} | collective-permute-start | bytes 1572872 | tf_op jit(solution)/shard_map/ppermute | solution.py:623
  219.3 1.3 collective-permute-start.18
  220.6 1.8 collective-permute-start.15
  222.4 1.3 collective-permute-start.24
  223.7 4.7 %collective-permute-done.31 = f32[1024,128]{1,0:T(8,128)S(1)} collective-permute-done((f32[1024,128]{1,0:T(8,128)}, f32[1024,128]{1,0:T(8,128)S(1)}, u32[]{:S(2)}, u32[]{:S(2)}) %collective-permute-start.31) | collective-permute-done | bytes 524320 | tf_op jit(solution)/shard_map/ppermute | solution.py:623
  228.3 1.3 collective-permute-start.25
  229.7 2.3 collective-permute-done.29
  232.0 0.8 copy-done.13
  232.8 1.3 collective-permute-start.32
  234.1 1.3 broadcast_select_fusion.3
  235.4 1.1 pad_maximum_fusion.1
  236.5 5.6 %collective-permute-done.32 = f32[1024,128]{1,0:T(8,128)S(1)} collective-permute-done((f32[1024,128]{1,0:T(8,128)S(1)}, f32[1024,128]{1,0:T(8,128)S(1)}, u32[]{:S(2)}, u32[]{:S(2)}) %collective-permute-start.32) | collective-permute-done | bytes 524320 | tf_op jit(solution)/shard_map/ppermute | solution.py:623
  242.1 0.8 copy-done.14
  242.9 1.9 broadcast_select_fusion.5
  244.8 2.1 collective-permute-start.33
  247.0 0.8 collective-permute-start.16
  247.7 10.8 %collective-permute-done.24.refs_7_ = f32[384,1024]{1,0:T(8,128)} collective-permute-done((f32[384,1024]{1,0:T(8,128)}, f32[384,1024]{1,0:T(8,128)}, u32[]{:S(2)}, u32[]{:S(2)}) %collective-permute-start.24) | collective-permute-done | bytes 1572896 | tf_op jit(solution)/shard_map/ppermute | solution.py:713
  258.5 0.8 collective-permute-start.17
  259.3 16.1 %collective-permute-done.25.refs_8_ = f32[384,1024]{1,0:T(8,128)} collective-permute-done((f32[384,1024]{1,0:T(8,128)}, f32[384,1024]{1,0:T(8,128)}, u32[]{:S(2)}, u32[]{:S(2)}) %collective-permute-start.25) | collective-permute-done | bytes 1572896 | tf_op jit(solution)/shard_map/ppermute | solution.py:713
  275.4 1.4 collective-permute-start.26
  276.8 1.4 collective-permute-start.27
  278.2 1.4 collective-permute-start.28
  279.6 1.4 broadcast_select_fusion.1
  281.7 2.9 fusion
  284.6 3.5 %fusion.3.refs_13_ = f32[1024,128]{1,0:T(8,128)S(1)} fusion(f32[1024,1024]{1,0:T(8,128)S(1)} %unpack.1, f32[1024,128]{1,0:T(8,128)S(1)} %fusion), kind=kOutput, calls=%fused_computation.42 | convolution fusion | flops 805306368 | bytes 5242880 | tf_op jit(solution)/shard_map/dot_general | solution.py:736
  288.2 9.3 %finish.1 = (f32[1152,256]{1,0:T(8,128)}, f32[1152,128]{1,0:T(8,128)}) custom-call(s32[2]{0:T(128)S(1)} %pad_add_fusion.where_ref, f32[384,1024]{1,0:T(8,128)S(1)} %copy-done.3, f32[384,1024]{1,0:T(8,128)S(1)} %copy-done.4, f32[384,1024]{1,0:T(8,128)S(1)} %copy-done.5, f32[384,1024]{1,0:T(8,128)} %collective-permute-done.15.refs_3_, ...), custom_call_target="tpu_custom_call" | custom-call | tf_op jit(solution)/shard_map/finish/pallas_call | solution.py:575
  (87 shorter events, 5.7 us)
Async XLA Ops:
  0.6 1.6 copy-start.1
  2.2 0.7 copy-start.6
  2.9 0.7 copy-start.8
  3.5 19.4 %copy-start.2 = (f32[128,4096]{1,0:T(8,128)S(1)}, f32[128,4096]{1,0:T(8,128)}, u32[]{:S(2)}) copy-start(f32[128,4096]{1,0:T(8,128)} %tiles_ref.3) | copy-start | bytes 6291460
  3.5 19.4 %copy-start.7 = (s32[128]{0:T(128)S(1)}, s32[128]{0:T(128)}, u32[]{:S(2)}) copy-start(s32[128]{0:T(128)} %target_ref.2) | copy-start | bytes 1540
  3.5 19.4 %copy-start.9 = (s32[4]{0:T(128)S(1)}, s32[4]{0:T(128)}, u32[]{:S(2)}) copy-start(s32[4]{0:T(128)} %tally_ref.1) | copy-start | bytes 52
  7.4 6.2 %collective-permute-start = (f32[136,128]{1,0:T(8,128)S(1)}, f32[136,128]{1,0:T(8,128)S(1)}, u32[]{:S(2)}, u32[]{:S(2)}) collective-permute-start(f32[136,128]{1,0:T(8,128)S(1)} %pick.1), channel_id=1, source_target_pairs={{8,0},{9,1},{10,2},{11,3},{12,4},{13,5},{14,6},{15,7}} | collective-permute-start | bytes 208904 | tf_op jit(solution)/shard_map/ppermute | solution.py:630
  8.7 7.1 %collective-permute-start.1 = (f32[136,128]{1,0:T(8,128)S(1)}, f32[136,128]{1,0:T(8,128)S(1)}, u32[]{:S(2)}, u32[]{:S(2)}) collective-permute-start(f32[136,128]{1,0:T(8,128)S(1)} %pick.1), channel_id=1, source_target_pairs={{16,0},{17,1},{18,2},{19,3},{20,4},{21,5},{22,6},{23,7}} | collective-permute-start | bytes 208904 | tf_op jit(solution)/shard_map/ppermute | solution.py:630
  10.0 8.0 %collective-permute-start.2 = (f32[136,128]{1,0:T(8,128)S(1)}, f32[136,128]{1,0:T(8,128)S(1)}, u32[]{:S(2)}, u32[]{:S(2)}) collective-permute-start(f32[136,128]{1,0:T(8,128)S(1)} %pick.1), channel_id=1, source_target_pairs={{24,0},{25,1},{26,2},{27,3},{28,4},{29,5},{30,6},{31,7}} | collective-permute-start | bytes 208904 | tf_op jit(solution)/shard_map/ppermute | solution.py:630
  18.0 19.8 %collective-permute-start.3 = (f32[544,128]{1,0:T(8,128)S(1)}, f32[544,128]{1,0:T(8,128)S(1)}, u32[]{:S(2)}, u32[]{:S(2)}) collective-permute-start(f32[544,128]{1,0:T(8,128)S(1)} %pad_maximum_fusion.4), channel_id=1, source_target_pairs={{1,0}} | collective-permute-start | bytes 835592 | tf_op jit(solution)/shard_map/ppermute | solution.py:635
  18.7 19.8 %collective-permute-start.4 = (f32[544,128]{1,0:T(8,128)S(1)}, f32[544,128]{1,0:T(8,128)S(1)}, u32[]{:S(2)}, u32[]{:S(2)}) collective-permute-start(f32[544,128]{1,0:T(8,128)S(1)} %pad_maximum_fusion.4), channel_id=1, source_target_pairs={{2,0}} | collective-permute-start | bytes 835592 | tf_op jit(solution)/shard_map/ppermute | solution.py:635
  20.8 18.5 %collective-permute-start.5 = (f32[544,128]{1,0:T(8,128)S(1)}, f32[544,128]{1,0:T(8,128)S(1)}, u32[]{:S(2)}, u32[]{:S(2)}) collective-permute-start(f32[544,128]{1,0:T(8,128)S(1)} %pad_maximum_fusion.4), channel_id=1, source_target_pairs={{3,0}} | collective-permute-start | bytes 835592 | tf_op jit(solution)/shard_map/ppermute | solution.py:635
  21.5 17.8 %collective-permute-start.6 = (f32[544,128]{1,0:T(8,128)S(1)}, f32[544,128]{1,0:T(8,128)S(1)}, u32[]{:S(2)}, u32[]{:S(2)}) collective-permute-start(f32[544,128]{1,0:T(8,128)S(1)} %pad_maximum_fusion.4), channel_id=1, source_target_pairs={{4,0}} | collective-permute-start | bytes 835592 | tf_op jit(solution)/shard_map/ppermute | solution.py:635
  22.2 17.1 %collective-permute-start.7 = (f32[544,128]{1,0:T(8,128)S(1)}, f32[544,128]{1,0:T(8,128)S(1)}, u32[]{:S(2)}, u32[]{:S(2)}) collective-permute-start(f32[544,128]{1,0:T(8,128)S(1)} %pad_maximum_fusion.4), channel_id=1, source_target_pairs={{5,0}} | collective-permute-start | bytes 835592 | tf_op jit(solution)/shard_map/ppermute | solution.py:635
  35.8 2.0 copy-start
  37.8 1.6 collective-permute-start.8
  38.6 0.9 collective-permute-start.9
  39.5 15.2 %copy-start.11 = (f32[4352,128]{1,0:T(8,128)}, f32[4352,128]{1,0:T(8,128)S(1)}, u32[]{:S(2)}) copy-start(f32[4352,128]{1,0:T(8,128)S(1)} %constant_dynamic-update-slice_fusion.tiles_ref) | copy-start | bytes 6684676
  39.5 111.6 %all-to-all-start = ((f32[32,264,128]{2,1,0:T(8,128)}), f32[32,264,128]{2,1,0:T(8,128)}, u32[]{:S(2)}, u32[]{:S(2)}) async-start(f32[32,264,128]{2,1,0:T(8,128)} %bitcast.16), calls=%async_computation | async-start | bytes 8650752 | tf_op jit(solution)/shard_map/all_to_all | solution.py:683
  58.4 3.2 %copy-start.10 = (f32[4608,128]{1,0:T(8,128)S(1)}, f32[4608,128]{1,0:T(8,128)}, u32[]{:S(2)}) copy-start(f32[4608,128]{1,0:T(8,128)} %factor.1) | copy-start | bytes 7077892
  59.9 1.7 collective-permute-start.10
  61.8 0.7 collective-permute-start.11
  62.6 0.7 collective-permute-start.12
  63.4 0.7 collective-permute-start.13
  64.1 85.7 %collective-permute-start.14 = (f32[144,128]{1,0:T(8,128)S(1)}, f32[144,128]{1,0:T(8,128)S(1)}, u32[]{:S(2)}, u32[]{:S(2)}) collective-permute-start(f32[144,128]{1,0:T(8,128)S(1)} %slice.83), channel_id=1, source_target_pairs={{0,2},{1,3},{4,6},{5,7},{8,10},{9,11},{12,14},{13,15},{16,18},{17,... | collective-permute-start | bytes 221192 | tf_op jit(solution)/shard_map/ppermute | solution.py:643
  178.5 4.8 %collective-permute-start.19 = (f32[2304,128]{1,0:T(8,128)S(1)}, f32[2304,128]{1,0:T(8,128)S(1)}, u32[]{:S(2)}, u32[]{:S(2)}) collective-permute-start(f32[2304,128]{1,0:T(8,128)S(1)} %bitcast.18), channel_id=1, source_target_pairs={{0,1},{1,0},{2,3},{3,2},{4,5},{5,4},{6,7},{7,6},{8,9},{9,8},{10,11... | collective-permute-start | bytes 3538952 | tf_op jit(solution)/shard_map/ppermute | solution.py:594
  178.6 4.7 %collective-permute-start.20 = (f32[144,128]{1,0:T(8,128)S(1)}, f32[144,128]{1,0:T(8,128)S(1)}, u32[]{:S(2)}, u32[]{:S(2)}) collective-permute-start(f32[144,128]{1,0:T(8,128)S(1)} %slice_select_fusion.7), channel_id=1, source_target_pairs={{0,2},{1,3},{2,0},{3,1},{4,6},{5,7},{6,4},{7,5},{8,10},{9,11},{10,... | collective-permute-start | bytes 221192 | tf_op jit(solution)/shard_map/ppermute | solution.py:594
  183.4 6.4 %collective-permute-start.22 = (f32[288,128]{1,0:T(8,128)S(1)}, f32[288,128]{1,0:T(8,128)S(1)}, u32[]{:S(2)}, u32[]{:S(2)}) collective-permute-start(f32[288,128]{1,0:T(8,128)S(1)} %pad_maximum_fusion.5), channel_id=1, source_target_pairs={{0,16},{1,17},{2,18},{3,19},{4,20},{5,21},{6,22},{7,23},{8,24},{9,... | collective-permute-start | bytes 442376 | tf_op jit(solution)/shard_map/ppermute | solution.py:594
  189.9 16.2 %collective-permute-start.23 = (f32[576,128]{1,0:T(8,128)S(1)}, f32[576,128]{1,0:T(8,128)S(1)}, u32[]{:S(2)}, u32[]{:S(2)}) collective-permute-start(f32[576,128]{1,0:T(8,128)S(1)} %pad_maximum_fusion.3), channel_id=1, source_target_pairs={{0,8},{1,9},{2,10},{3,11},{4,12},{5,13},{6,14},{7,15},{8,0},{9,1},... | collective-permute-start | bytes 884744 | tf_op jit(solution)/shard_map/ppermute | solution.py:594
  199.9 14.1 %collective-permute-start.21 = (f32[1152,128]{1,0:T(8,128)S(1)}, f32[1152,128]{1,0:T(8,128)S(1)}, u32[]{:S(2)}, u32[]{:S(2)}) collective-permute-start(f32[1152,128]{1,0:T(8,128)S(1)} %slice_select_fusion.4), channel_id=1, source_target_pairs={{0,2},{1,3},{2,0},{3,1},{4,6},{5,7},{6,4},{7,5},{8,10},{9,11},{10,... | collective-permute-start | bytes 1769480 | tf_op jit(solution)/shard_map/ppermute | solution.py:594
  207.0 12.3 %copy-start.3 = (f32[384,1024]{1,0:T(8,128)S(1)}, f32[384,1024]{1,0:T(8,128)}, u32[]{:S(2)}) copy-start(f32[384,1024]{1,0:T(8,128)} %get-tuple-element.23.refs_0_) | copy-start | bytes 4718596
  214.9 13.4 %collective-permute-start.31 = (f32[1024,128]{1,0:T(8,128)}, f32[1024,128]{1,0:T(8,128)S(1)}, u32[]{:S(2)}, u32[]{:S(2)}) collective-permute-start(f32[1024,128]{1,0:T(8,128)} %slice.73), channel_id=1, source_target_pairs={{0,16},{1,17},{2,18},{3,19}} | collective-permute-start | bytes 1572872 | tf_op jit(solution)/shard_map/ppermute | solution.py:623
  219.2 12.8 %collective-permute-start.29 = (f32[1152,128]{1,0:T(8,128)}, f32[1152,128]{1,0:T(8,128)S(1)}, u32[]{:S(2)}, u32[]{:S(2)}) collective-permute-start(f32[1152,128]{1,0:T(8,128)} %pad_maximum_fusion.2), channel_id=1, source_target_pairs={{0,4},{1,5},{2,6},{3,7},{4,0},{5,1},{6,2},{7,3},{8,12},{9,13},{10,... | collective-permute-start | bytes 1769480 | tf_op jit(solution)/shard_map/ppermute | solution.py:594
  219.3 25.6 %collective-permute-start.18 = (f32[384,1024]{1,0:T(8,128)S(1)}, f32[384,1024]{1,0:T(8,128)}, u32[]{:S(2)}, u32[]{:S(2)}) collective-permute-start(f32[384,1024]{1,0:T(8,128)S(1)} %copy-done.3), channel_id=1, source_target_pairs={{0,2},{4,6},{8,10},{12,14},{16,18},{20,22},{24,26},{28,30}} | collective-permute-start | bytes 4718600 | tf_op jit(solution)/shard_map/ppermute | solution.py:703
  220.6 26.4 %collective-permute-start.15 = (f32[384,1024]{1,0:T(8,128)S(1)}, f32[384,1024]{1,0:T(8,128)}, u32[]{:S(2)}, u32[]{:S(2)}) collective-permute-start(f32[384,1024]{1,0:T(8,128)S(1)} %copy-done.3), channel_id=1, source_target_pairs={{0,1},{4,5},{8,9},{12,13},{16,17},{20,21},{24,25},{28,29}} | collective-permute-start | bytes 4718600 | tf_op jit(solution)/shard_map/ppermute | solution.py:732
  222.4 36.1 %collective-permute-start.24 = (f32[384,1024]{1,0:T(8,128)}, f32[384,1024]{1,0:T(8,128)}, u32[]{:S(2)}, u32[]{:S(2)}) collective-permute-start(f32[384,1024]{1,0:T(8,128)} %get-tuple-element.30.refs_1_), channel_id=1, source_target_pairs={{0,2},{4,6},{8,10},{12,14},{16,18},{20,22},{24,26},{28,30}} | collective-permute-start | bytes 4718600 | tf_op jit(solution)/shard_map/ppermute | solution.py:713
  228.3 47.0 %collective-permute-start.25 = (f32[384,1024]{1,0:T(8,128)}, f32[384,1024]{1,0:T(8,128)}, u32[]{:S(2)}, u32[]{:S(2)}) collective-permute-start(f32[384,1024]{1,0:T(8,128)} %get-tuple-element.31.refs_2_), channel_id=1, source_target_pairs={{0,2},{4,6},{8,10},{12,14},{16,18},{20,22},{24,26},{28,30}} | collective-permute-start | bytes 4718600 | tf_op jit(solution)/shard_map/ppermute | solution.py:713
  229.7 6.8 %copy-start.12 = (f32[1024,128]{1,0:T(8,128)}, f32[1024,128]{1,0:T(8,128)S(1)}, u32[]{:S(2)}) copy-start(f32[1024,128]{1,0:T(8,128)S(1)} %broadcast_select_fusion.4) | copy-start | bytes 1572868
  232.0 0.8 copy-start.13
  232.8 9.4 %collective-permute-start.32 = (f32[1024,128]{1,0:T(8,128)S(1)}, f32[1024,128]{1,0:T(8,128)S(1)}, u32[]{:S(2)}, u32[]{:S(2)}) collective-permute-start(f32[1024,128]{1,0:T(8,128)S(1)} %broadcast_select_fusion.4), channel_id=1, source_target_pairs={{0,8},{16,24},{1,9},{17,25},{2,10},{18,26},{3,11},{19,27}} | collective-permute-start | bytes 1572872 | tf_op jit(solution)/shard_map/ppermute | solution.py:623
  242.1 0.8 copy-start.14
  242.9 35.2 %collective-permute-start.30 = (f32[2304,128]{1,0:T(8,128)}, f32[2304,128]{1,0:T(8,128)}, u32[]{:S(2)}, u32[]{:S(2)}) collective-permute-start(f32[2304,128]{1,0:T(8,128)} %pad_maximum_fusion.1), channel_id=1, source_target_pairs={{0,1},{1,0},{2,3},{3,2},{4,5},{5,4},{6,7},{7,6},{8,9},{9,8},{10,11... | collective-permute-start | bytes 3538952 | tf_op jit(solution)/shard_map/ppermute | solution.py:594
  244.8 31.9 %collective-permute-start.33 = (f32[1024,128]{1,0:T(8,128)}, f32[1024,128]{1,0:T(8,128)}, u32[]{:S(2)}, u32[]{:S(2)}) collective-permute-start(f32[1024,128]{1,0:T(8,128)} %broadcast_select_fusion.5), channel_id=1, source_target_pairs={{0,4},{8,12},{16,20},{24,28},{1,5},{9,13},{17,21},{25,29},{2,6},{1... | collective-permute-start | bytes 1572872 | tf_op jit(solution)/shard_map/ppermute | solution.py:623
  247.0 41.1 %collective-permute-start.16 = (f32[384,1024]{1,0:T(8,128)}, f32[384,1024]{1,0:T(8,128)S(1)}, u32[]{:S(2)}, u32[]{:S(2)}) collective-permute-start(f32[384,1024]{1,0:T(8,128)} %get-tuple-element.30.refs_1_), channel_id=1, source_target_pairs={{0,1},{4,5},{8,9},{12,13},{16,17},{20,21},{24,25},{28,29}} | collective-permute-start | bytes 4718600 | tf_op jit(solution)/shard_map/ppermute | solution.py:732
  258.5 29.6 %collective-permute-start.17 = (f32[384,1024]{1,0:T(8,128)}, f32[384,1024]{1,0:T(8,128)S(1)}, u32[]{:S(2)}, u32[]{:S(2)}) collective-permute-start(f32[384,1024]{1,0:T(8,128)} %get-tuple-element.31.refs_2_), channel_id=1, source_target_pairs={{0,1},{4,5},{8,9},{12,13},{16,17},{20,21},{24,25},{28,29}} | collective-permute-start | bytes 4718600 | tf_op jit(solution)/shard_map/ppermute | solution.py:732
  275.4 12.7 %collective-permute-start.26 = (f32[384,1024]{1,0:T(8,128)}, f32[384,1024]{1,0:T(8,128)S(1)}, u32[]{:S(2)}, u32[]{:S(2)}) collective-permute-start(f32[384,1024]{1,0:T(8,128)} %collective-permute-done.18.refs_6_), channel_id=1, source_target_pairs={{2,3},{6,7},{10,11},{14,15},{18,19},{22,23},{26,27},{30,31}} | collective-permute-start | bytes 4718600 | tf_op jit(solution)/shard_map/ppermute | solution.py:732
  276.8 11.3 %collective-permute-start.27 = (f32[384,1024]{1,0:T(8,128)}, f32[384,1024]{1,0:T(8,128)S(1)}, u32[]{:S(2)}, u32[]{:S(2)}) collective-permute-start(f32[384,1024]{1,0:T(8,128)} %collective-permute-done.24.refs_7_), channel_id=1, source_target_pairs={{2,3},{6,7},{10,11},{14,15},{18,19},{22,23},{26,27},{30,31}} | collective-permute-start | bytes 4718600 | tf_op jit(solution)/shard_map/ppermute | solution.py:732
  278.2 9.9 %collective-permute-start.28 = (f32[384,1024]{1,0:T(8,128)}, f32[384,1024]{1,0:T(8,128)S(1)}, u32[]{:S(2)}, u32[]{:S(2)}) collective-permute-start(f32[384,1024]{1,0:T(8,128)} %collective-permute-done.25.refs_8_), channel_id=1, source_target_pairs={{2,3},{6,7},{10,11},{14,15},{18,19},{22,23},{26,27},{30,31}} | collective-permute-start | bytes 4718600 | tf_op jit(solution)/shard_map/ppermute | solution.py:732
  284.6 3.6 %copy-start.4 = (f32[384,1024]{1,0:T(8,128)S(1)}, f32[384,1024]{1,0:T(8,128)}, u32[]{:S(2)}) copy-start(f32[384,1024]{1,0:T(8,128)} %get-tuple-element.30.refs_1_) | copy-start | bytes 4718596
  284.6 3.6 %copy-start.5 = (f32[384,1024]{1,0:T(8,128)S(1)}, f32[384,1024]{1,0:T(8,128)}, u32[]{:S(2)}) copy-start(f32[384,1024]{1,0:T(8,128)} %get-tuple-element.31.refs_2_) | copy-start | bytes 4718596

commit v3 on v2

--- a/solution.py
+++ b/solution.py
@@ -19,7 +19,8 @@
 AXES = ("row", "col")
 HIGH = lax.Precision.HIGHEST
 MIB = 1 << 20
-PIECES = 3
+MIDDLE = 3
+PIECES = 4
 
 
 def block_index(r, c):
@@ -625,14 +626,14 @@
     return x
 
 
-def collect(x, count, inner):
-    return [x] + [
-        lax.ppermute(x, AXES, [(d + e, e) for e in range(inner)]) for d in range(inner, count, inner)
-    ]
-
-
-def collect_last(x, inner):
-    return [x] + [lax.ppermute(x, AXES, [(e, 0)]) for e in range(1, inner)]
+def collect(x, count, inner, pair):
+    heads = range(0, inner, pair)
+    offsets = [far + near for far in range(0, count, inner) for near in range(pair) if far + near > 0]
+    return [x] + [lax.ppermute(x, AXES, [(e + offset, e) for e in heads]) for offset in offsets]
+
+
+def collect_last(x, inner, pair):
+    return [x] + [lax.ppermute(x, AXES, [(e, 0)]) for e in range(pair, inner, pair)]
 
 
 def scatter(x, axis, index, order, count):
@@ -668,11 +669,11 @@
     homes = (PD + local_rows - 1) // local_rows
     most = max(1, homes * capacity // 2)
     picked = pick(tile_target, tile_count, child_tiles, most, grid)
-    inner = min(2, row_count) * col_count
-    gathered = jnp.concatenate(collect(picked, devices, inner), axis=0)
+    inner, pair = min(2, row_count) * col_count, min(2, col_count)
+    gathered = jnp.concatenate(collect(picked, devices, inner, pair), axis=0)
     gathered, tile_target = lax.optimization_barrier((gathered, tile_target))
     outgoing = stage(tile_target, tile_count, child_tiles, devices, capacity, grid, tile_rows, tile_cols, col_count)
-    gathered = jnp.concatenate(collect_last(gathered, inner), axis=0)
+    gathered = jnp.concatenate(collect_last(gathered, inner, pair), axis=0)
     gathered, outgoing = lax.optimization_barrier((gathered, outgoing))
     label = gathered.reshape(devices, -1, LANES)[:, most * half, :most].astype(jnp.int32).reshape(-1)
     corner = front
@@ -699,18 +700,20 @@
     order = order[::-1]
     sums = masks(col_count)
     panel_order = sums[::-1]
-    held = {0: panel}
-    ahead = lax.ppermute(panel[0], "col", [(0, panel_order[0])])
+    far = [(0, panel_order[0])]
+    sent = [lax.ppermute(panel[0], "col", far)]
     for mask in sums[:-1]:
         share = halve(share, "col", col_index, mask, col_count)
     part = double(part, AXES, device, order[0], devices)
-    share, part = lax.optimization_barrier((share, part))
+    share, part, *panel[1:] = lax.optimization_barrier((share, part, *panel[1:]))
+    sent += [lax.ppermute(piece, "col", far) for piece in panel[1:MIDDLE]]
     share = halve(share, "col", col_index, sums[-1], col_count)
     for mask in order[1:-2]:
         part = double(part, AXES, device, mask, devices)
-    share, part, *later = lax.optimization_barrier((share, part, *panel[1:]))
+    share, part, *panel[MIDDLE:] = lax.optimization_barrier((share, part, *panel[MIDDLE:]))
+    sent += [lax.ppermute(piece, "col", far) for piece in panel[MIDDLE:]]
     part = double(part, AXES, device, order[-2], devices)
-    held[panel_order[0]] = [ahead] + [lax.ppermute(piece, "col", [(0, panel_order[0])]) for piece in later]
+    held = {0: panel, panel_order[0]: sent}
 
     top_order = masks(row_count)[::-1]
     if homes == 1:

time: 299 us -> 281 us (0.940)
  waiting for transfers between devices: 151 us -> 140 us
    all_to_all x1, starting transfers between devices: 15.2 us -> 3.95 us  [per_device(): lax.all_to_all(outgoing.reshape(devices, capacity * half + 8, LANES), AXE...]
    ppermute x13 -> x14, waiting for transfers between devices: 33.6 us -> 25.6 us  [the longest x2 10.4 us: per_device(): sent += [lax.ppermute(piece, 'col', far) for piece in panel[1:MIDDLE]]]
    ppermute x6 -> x8, starting transfers between devices: 7.5 us -> 11.3 us  [per_device(): lax.ppermute(piece, 'col', [(d, d + mask)])]
    ppermute x13 -> x14, starting transfers between devices: 13.9 us -> 16.9 us  [the longest x7 9.04 us: collect(): lax.ppermute(x, AXES, [(e + offset, e) for e in heads])]
    unnamed x37 -> x41, local copies, waits for them, and re-layouts: 6.72 us -> 5.87 us
  transfers between devices with their start and end apart: 35 -> 38, of which waited for: 14 -> 15; matrix products, arithmetic and copies ran while one was open for 5% -> 5% of each run, Pallas kernels for 5% -> 6%
where the time goes in v3:
time: 281 us; the launch traced here: 280 us
  waiting for transfers between devices  140 us (50%)
  starting transfers between devices  62.1 us (22%)
  Pallas kernels  53.7 us (19%)
  local copies, waits for them, and re-layouts  9.65 us (3%)
  other arithmetic  7.68 us (3%)
  matrix products  5.28 us (2%)
    ppermute x5, waiting for transfers between devices, scatter(): x = jnp.where(index & mask != 0, lax.ppermute(x[h:], axis, pairs), x[:h])  84.1 us
    pallas_call x1, Pallas kernels, assemble(): pl.pallas_call(functools.partial(assemble_kernel, landing.shape[0], capac...  24 us
    ppermute x7, waiting for transfers between devices, exchange(): return lax.ppermute(x, axis, [(d, d ^ mask) for d in range(count)])  22.1 us
    ppermute x7, starting transfers between devices, exchange(): return lax.ppermute(x, axis, [(d, d ^ mask) for d in range(count)])  16.2 us
    pallas_call x1, Pallas kernels, stage(): pl.pallas_call(functools.partial(stage_kernel, held, devices, capacity, g...  12.9 us
    ppermute x8, starting transfers between devices, per_device(): lax.ppermute(piece, 'col', [(d, d + mask)])  11.3 us
    ppermute x2, waiting for transfers between devices, per_device(): sent += [lax.ppermute(piece, 'col', far) for piece in panel[1:MIDDLE]]  10.4 us
    pallas_call x1, Pallas kernels, finish(): pl.pallas_call(functools.partial(finish_kernel, len(panels), width), out_...  9.25 us
  transfers between devices with their start and end apart: 38, of which 15 were waited for; matrix products, arithmetic and copies ran while one was open for 5% of the time, Pallas kernels for 6%

profile of v3, /device:TPU:4, one launch (start us, length us, event | category | flops | bytes accessed | tf_op | source)
XLA Modules:
  0.0 280.4 jit_solution(460127495831495086)
XLA Ops:
  0.6 1.6 copy-done.1
  3.5 4.1 %pick.1 = f32[136,128]{1,0:T(8,128)S(1)} custom-call(s32[128]{0:T(128)S(1)} %copy-done.5, s32[4]{0:T(128)S(1)} %copy-done.7, f32[128,4096]{1,0:T(8,128)S(1)} %copy-done.1), custom_call_target="tpu_custom_call" | custom-call | tf_op jit(solution)/shard_map/pick/pallas_call | solution.py:105
  7.7 1.3 collective-permute-start
  9.0 1.3 collective-permute-start.1
  10.3 1.3 collective-permute-start.2
  11.6 1.3 collective-permute-start.3
  12.9 1.3 collective-permute-start.4
  14.2 1.3 collective-permute-start.5
  15.5 1.3 collective-permute-start.6
  16.9 1.9 collective-permute-done.3
  19.4 2.8 collective-permute-done.5
  22.2 0.7 collective-permute-done.6
  23.0 1.3 collective-permute-start.7
  24.3 0.7 collective-permute-start.8
  25.0 0.7 collective-permute-start.9
  25.7 12.9 %stage.1 = f32[8448,128]{1,0:T(8,128)S(1)} custom-call(s32[128]{0:T(128)S(1)} %copy-done.6, s32[4]{0:T(128)S(1)} %copy-done.8, f32[128,4096]{1,0:T(8,128)S(1)} %copy-done.2), custom_call_target="tpu_custom_call" | custom-call | tf_op jit(solution)/shard_map/stage/pallas_call | solution.py:209
  38.6 2.1 copy-done
  40.8 4.0 %all-to-all-start = ((f32[32,264,128]{2,1,0:T(8,128)}), f32[32,264,128]{2,1,0:T(8,128)}, u32[]{:S(2)}, u32[]{:S(2)}) async-start(f32[32,264,128]{2,1,0:T(8,128)} %bitcast.16), calls=%async_computation | async-start | bytes 8650752 | tf_op jit(solution)/shard_map/all_to_all | solution.py:684
  45.4 3.0 %factor.1 = f32[4608,128]{1,0:T(8,128)} custom-call(s32[128]{0:T(128)} %convert_element_type.15.label_ref, s32[1]{0:T(128)} %bitcast.3.me_ref, f32[1152,2304]{1,0:T(8,128)} %front_ref.3, f32[4352,128]{1,0:T(8,128)} %copy-done.12), custom_call_target="tpu_custom_call" | custom-call | tf_op jit(solution)/shard_map/factor/pallas_call | solution.py:397
  48.5 1.5 slice.75
  50.0 1.7 collective-permute-start.10
  51.9 0.7 collective-permute-start.11
  54.2 1.5 collective-permute-start.14
  55.7 84.1 %collective-permute-done.14 = f32[144,128]{1,0:T(8,128)S(1)} collective-permute-done((f32[144,128]{1,0:T(8,128)S(1)}, f32[144,128]{1,0:T(8,128)S(1)}, u32[]{:S(2)}, u32[]{:S(2)}) %collective-permute-start.14) | collective-permute-done | bytes 73760 | tf_op jit(solution)/shard_map/ppermute | solution.py:644
  139.8 1.2 all-to-all-done
  141.0 1.0 convert_reduce_fusion
  142.7 24.0 %assemble.1 = (f32[4,1152,128]{2,1,0:T(8,128)}, f32[288,1024]{1,0:T(8,128)}, f32[288,1024]{1,0:T(8,128)}, f32[288,1024]{1,0:T(8,128)}, f32[288,1024]{1,0:T(8,128)}) custom-call(s32[256]{0:T(256)} %convert_element_type.17.landing_ref, s32[1]{0:T(128)} %bitcast.5.first_ref, f32[1152,2304]{1,0:T(8,128)} %front_ref.3, f32[8448,128]{1,0:T(8,128)} %bitcast.6.incoming_ref, ...), custom_call_target="tpu_custom_call" | custom-call | tf_op jit(solution)/shard_map/assemble/pallas_call | solution.py:513
  166.7 1.8 slice_select_fusion.2
  168.6 1.3 collective-permute-start.16
  169.9 3.3 %collective-permute-done.16 = f32[144,128]{1,0:T(8,128)S(1)} collective-permute-done((f32[144,128]{1,0:T(8,128)S(1)}, f32[144,128]{1,0:T(8,128)S(1)}, u32[]{:S(2)}, u32[]{:S(2)}) %collective-permute-start.16) | collective-permute-done | bytes 73760 | tf_op jit(solution)/shard_map/ppermute | solution.py:595
  173.4 2.3 collective-permute-start.18
  175.8 4.1 %collective-permute-done.18 = f32[288,128]{1,0:T(8,128)S(1)} collective-permute-done((f32[288,128]{1,0:T(8,128)S(1)}, f32[288,128]{1,0:T(8,128)S(1)}, u32[]{:S(2)}, u32[]{:S(2)}) %collective-permute-start.18) | collective-permute-done | bytes 147488 | tf_op jit(solution)/shard_map/ppermute | solution.py:595
  179.9 10.1 %collective-permute-start.19 = (f32[576,128]{1,0:T(8,128)S(1)}, f32[576,128]{1,0:T(8,128)S(1)}, u32[]{:S(2)}, u32[]{:S(2)}) collective-permute-start(f32[576,128]{1,0:T(8,128)S(1)} %pad_maximum_fusion.4), channel_id=1, source_target_pairs={{0,8},{1,9},{2,10},{3,11},{4,12},{5,13},{6,14},{7,15},{8,0},{9,1},... | collective-permute-start | bytes 884744 | tf_op jit(solution)/shard_map/ppermute | solution.py:595
  190.6 5.7 %collective-permute-done.19 = f32[576,128]{1,0:T(8,128)S(1)} collective-permute-done((f32[576,128]{1,0:T(8,128)S(1)}, f32[576,128]{1,0:T(8,128)S(1)}, u32[]{:S(2)}, u32[]{:S(2)}) %collective-permute-start.19) | collective-permute-done | bytes 294944 | tf_op jit(solution)/shard_map/ppermute | solution.py:595
  196.3 7.8 %collective-permute-done.17 = f32[1152,128]{1,0:T(8,128)S(1)} collective-permute-done((f32[1152,128]{1,0:T(8,128)S(1)}, f32[1152,128]{1,0:T(8,128)S(1)}, u32[]{:S(2)}, u32[]{:S(2)}) %collective-permute-start.17) | collective-permute-done | bytes 589856 | tf_op jit(solution)/shard_map/ppermute | solution.py:595
  204.2 1.9 collective-permute-start.32
  206.1 1.3 collective-permute-start.24
  207.4 1.7 collective-permute-start.20
  209.1 1.3 collective-permute-start.25
  210.4 0.8 slice.73
  211.2 5.0 %collective-permute-start.34 = (f32[1024,128]{1,0:T(8,128)}, f32[1024,128]{1,0:T(8,128)}, u32[]{:S(2)}, u32[]{:S(2)}) collective-permute-start(f32[1024,128]{1,0:T(8,128)} %slice.73), channel_id=1, source_target_pairs={{0,16},{1,17},{2,18},{3,19}} | collective-permute-start | bytes 1572872 | tf_op jit(solution)/shard_map/ppermute | solution.py:624
  216.2 1.2 collective-permute-done.32
  217.6 1.2 pad_maximum_fusion.2
  218.8 7.3 %collective-permute-done.34 = f32[1024,128]{1,0:T(8,128)} collective-permute-done((f32[1024,128]{1,0:T(8,128)}, f32[1024,128]{1,0:T(8,128)}, u32[]{:S(2)}, u32[]{:S(2)}) %collective-permute-start.34) | collective-permute-done | bytes 524320 | tf_op jit(solution)/shard_map/ppermute | solution.py:624
  226.2 1.3 collective-permute-start.35
  227.5 1.3 collective-permute-start.26
  228.8 1.7 collective-permute-start.21
  230.5 6.4 %collective-permute-done.25.refs_9_ = f32[288,1024]{1,0:T(8,128)} collective-permute-done((f32[288,1024]{1,0:T(8,128)S(1)}, f32[288,1024]{1,0:T(8,128)}, u32[]{:S(2)}, u32[]{:S(2)}) %collective-permute-start.25) | collective-permute-done | bytes 1179680 | tf_op jit(solution)/shard_map/ppermute | solution.py:709
  236.9 1.7 collective-permute-start.22
  238.6 0.8 copy-done.16
  239.4 1.3 collective-permute-start.27
  240.8 1.1 broadcast_select_fusion.5
  242.0 2.2 collective-permute-start.36
  244.2 1.4 broadcast_select_fusion.1
  245.6 4.0 %collective-permute-done.26.refs_10_ = f32[288,1024]{1,0:T(8,128)} collective-permute-done((f32[288,1024]{1,0:T(8,128)}, f32[288,1024]{1,0:T(8,128)}, u32[]{:S(2)}, u32[]{:S(2)}) %collective-permute-start.26) | collective-permute-done | bytes 1179680 | tf_op jit(solution)/shard_map/ppermute | solution.py:709
  249.6 1.4 collective-permute-start.28
  250.9 0.7 collective-permute-start.23
  251.7 1.4 collective-permute-start.29
  253.1 9.1 %collective-permute-done.27.refs_11_ = f32[288,1024]{1,0:T(8,128)} collective-permute-done((f32[288,1024]{1,0:T(8,128)}, f32[288,1024]{1,0:T(8,128)}, u32[]{:S(2)}, u32[]{:S(2)}) %collective-permute-start.27) | collective-permute-done | bytes 1179680 | tf_op jit(solution)/shard_map/ppermute | solution.py:714
  262.2 1.4 collective-permute-start.30
  263.6 1.4 collective-permute-start.31
  265.7 1.8 fusion
  267.5 3.5 %fusion.3.refs_17_ = f32[1024,128]{1,0:T(8,128)S(1)} fusion(f32[1024,1024]{1,0:T(8,128)S(1)} %unpack.1, f32[1024,128]{1,0:T(8,128)S(1)} %fusion), kind=kOutput, calls=%fused_computation.42 | convolution fusion | flops 805306368 | bytes 5242880 | tf_op jit(solution)/shard_map/dot_general | solution.py:739
  271.0 9.3 %finish.1 = (f32[1152,256]{1,0:T(8,128)}, f32[1152,128]{1,0:T(8,128)}) custom-call(s32[2]{0:T(128)S(1)} %pad_add_fusion.where_ref, f32[288,1024]{1,0:T(8,128)S(1)} %copy-done.3, f32[288,1024]{1,0:T(8,128)S(1)} %copy-done.4, f32[288,1024]{1,0:T(8,128)} %get-tuple-element.33.refs_2_, f32[288,1024]{1,0:T(8,128)} %get-tuple-element.37.refs_3_, ...), custom_call_target="tpu_custom_call" | custom-call | tf_op jit(solution)/shard_map/finish/pallas_call | solution.py:576
  (97 shorter events, 7.2 us)
Async XLA Ops:
  0.6 1.6 copy-start.1
  2.2 0.7 copy-start.5
  2.9 0.7 copy-start.7
  3.5 22.2 %copy-start.2 = (f32[128,4096]{1,0:T(8,128)S(1)}, f32[128,4096]{1,0:T(8,128)}, u32[]{:S(2)}) copy-start(f32[128,4096]{1,0:T(8,128)} %tiles_ref.3) | copy-start | bytes 6291460
  3.5 22.2 %copy-start.6 = (s32[128]{0:T(128)S(1)}, s32[128]{0:T(128)}, u32[]{:S(2)}) copy-start(s32[128]{0:T(128)} %target_ref.2) | copy-start | bytes 1540
  3.5 22.2 %copy-start.8 = (s32[4]{0:T(128)S(1)}, s32[4]{0:T(128)}, u32[]{:S(2)}) copy-start(s32[4]{0:T(128)} %tally_ref.1) | copy-start | bytes 52
  7.7 6.5 %collective-permute-start = (f32[136,128]{1,0:T(8,128)S(1)}, f32[136,128]{1,0:T(8,128)S(1)}, u32[]{:S(2)}, u32[]{:S(2)}) collective-permute-start(f32[136,128]{1,0:T(8,128)S(1)} %pick.1), channel_id=1, source_target_pairs={{1,0},{3,2},{5,4},{7,6}} | collective-permute-start | bytes 208904 | tf_op jit(solution)/shard_map/ppermute | solution.py:632
  9.0 6.5 %collective-permute-start.1 = (f32[136,128]{1,0:T(8,128)S(1)}, f32[136,128]{1,0:T(8,128)S(1)}, u32[]{:S(2)}, u32[]{:S(2)}) collective-permute-start(f32[136,128]{1,0:T(8,128)S(1)} %pick.1), channel_id=1, source_target_pairs={{8,0},{10,2},{12,4},{14,6}} | collective-permute-start | bytes 208904 | tf_op jit(solution)/shard_map/ppermute | solution.py:632
  10.3 6.6 %collective-permute-start.2 = (f32[136,128]{1,0:T(8,128)S(1)}, f32[136,128]{1,0:T(8,128)S(1)}, u32[]{:S(2)}, u32[]{:S(2)}) collective-permute-start(f32[136,128]{1,0:T(8,128)S(1)} %pick.1), channel_id=1, source_target_pairs={{9,0},{11,2},{13,4},{15,6}} | collective-permute-start | bytes 208904 | tf_op jit(solution)/shard_map/ppermute | solution.py:632
  11.6 7.2 %collective-permute-start.3 = (f32[136,128]{1,0:T(8,128)S(1)}, f32[136,128]{1,0:T(8,128)S(1)}, u32[]{:S(2)}, u32[]{:S(2)}) collective-permute-start(f32[136,128]{1,0:T(8,128)S(1)} %pick.1), channel_id=1, source_target_pairs={{16,0},{18,2},{20,4},{22,6}} | collective-permute-start | bytes 208904 | tf_op jit(solution)/shard_map/ppermute | solution.py:632
  12.9 6.5 %collective-permute-start.4 = (f32[136,128]{1,0:T(8,128)S(1)}, f32[136,128]{1,0:T(8,128)S(1)}, u32[]{:S(2)}, u32[]{:S(2)}) collective-permute-start(f32[136,128]{1,0:T(8,128)S(1)} %pick.1), channel_id=1, source_target_pairs={{17,0},{19,2},{21,4},{23,6}} | collective-permute-start | bytes 208904 | tf_op jit(solution)/shard_map/ppermute | solution.py:632
  14.2 8.0 %collective-permute-start.5 = (f32[136,128]{1,0:T(8,128)S(1)}, f32[136,128]{1,0:T(8,128)S(1)}, u32[]{:S(2)}, u32[]{:S(2)}) collective-permute-start(f32[136,128]{1,0:T(8,128)S(1)} %pick.1), channel_id=1, source_target_pairs={{24,0},{26,2},{28,4},{30,6}} | collective-permute-start | bytes 208904 | tf_op jit(solution)/shard_map/ppermute | solution.py:632
  15.5 7.4 %collective-permute-start.6 = (f32[136,128]{1,0:T(8,128)S(1)}, f32[136,128]{1,0:T(8,128)S(1)}, u32[]{:S(2)}, u32[]{:S(2)}) collective-permute-start(f32[136,128]{1,0:T(8,128)S(1)} %pick.1), channel_id=1, source_target_pairs={{25,0},{27,2},{29,4},{31,6}} | collective-permute-start | bytes 208904 | tf_op jit(solution)/shard_map/ppermute | solution.py:632
  23.0 17.7 %collective-permute-start.7 = (f32[1088,128]{1,0:T(8,128)S(1)}, f32[1088,128]{1,0:T(8,128)S(1)}, u32[]{:S(2)}, u32[]{:S(2)}) collective-permute-start(f32[1088,128]{1,0:T(8,128)S(1)} %constant_dynamic-update-slice_fusion), channel_id=1, source_target_pairs={{2,0}} | collective-permute-start | bytes 1671176 | tf_op jit(solution)/shard_map/ppermute | solution.py:636
  24.3 16.4 %collective-permute-start.8 = (f32[1088,128]{1,0:T(8,128)S(1)}, f32[1088,128]{1,0:T(8,128)S(1)}, u32[]{:S(2)}, u32[]{:S(2)}) collective-permute-start(f32[1088,128]{1,0:T(8,128)S(1)} %constant_dynamic-update-slice_fusion), channel_id=1, source_target_pairs={{4,0}} | collective-permute-start | bytes 1671176 | tf_op jit(solution)/shard_map/ppermute | solution.py:636
  25.0 15.7 %collective-permute-start.9 = (f32[1088,128]{1,0:T(8,128)S(1)}, f32[1088,128]{1,0:T(8,128)S(1)}, u32[]{:S(2)}, u32[]{:S(2)}) collective-permute-start(f32[1088,128]{1,0:T(8,128)S(1)} %constant_dynamic-update-slice_fusion), channel_id=1, source_target_pairs={{6,0}} | collective-permute-start | bytes 1671176 | tf_op jit(solution)/shard_map/ppermute | solution.py:636
  38.6 2.1 copy-start
  40.8 4.0 %copy-start.12 = (f32[4352,128]{1,0:T(8,128)}, f32[4352,128]{1,0:T(8,128)S(1)}, u32[]{:S(2)}) copy-start(f32[4352,128]{1,0:T(8,128)S(1)} %pad_maximum_fusion.1.tiles_ref) | copy-start | bytes 6684676
  40.8 100.2 %all-to-all-start = ((f32[32,264,128]{2,1,0:T(8,128)}), f32[32,264,128]{2,1,0:T(8,128)}, u32[]{:S(2)}, u32[]{:S(2)}) async-start(f32[32,264,128]{2,1,0:T(8,128)} %bitcast.16), calls=%async_computation | async-start | bytes 8650752 | tf_op jit(solution)/shard_map/all_to_all | solution.py:684
  48.5 3.2 %copy-start.11 = (f32[4608,128]{1,0:T(8,128)S(1)}, f32[4608,128]{1,0:T(8,128)}, u32[]{:S(2)}) copy-start(f32[4608,128]{1,0:T(8,128)} %factor.1) | copy-start | bytes 7077892
  50.0 1.7 collective-permute-start.10
  51.9 0.7 collective-permute-start.11
  52.7 0.7 collective-permute-start.12
  53.5 0.7 collective-permute-start.13
  54.2 85.6 %collective-permute-start.14 = (f32[144,128]{1,0:T(8,128)S(1)}, f32[144,128]{1,0:T(8,128)S(1)}, u32[]{:S(2)}, u32[]{:S(2)}) collective-permute-start(f32[144,128]{1,0:T(8,128)S(1)} %slice.83), channel_id=1, source_target_pairs={{0,2},{1,3},{4,6},{5,7},{8,10},{9,11},{12,14},{13,15},{16,18},{17,... | collective-permute-start | bytes 221192 | tf_op jit(solution)/shard_map/ppermute | solution.py:644
  168.5 4.8 %collective-permute-start.15 = (f32[2304,128]{1,0:T(8,128)S(1)}, f32[2304,128]{1,0:T(8,128)S(1)}, u32[]{:S(2)}, u32[]{:S(2)}) collective-permute-start(f32[2304,128]{1,0:T(8,128)S(1)} %bitcast.18), channel_id=1, source_target_pairs={{0,1},{1,0},{2,3},{3,2},{4,5},{5,4},{6,7},{7,6},{8,9},{9,8},{10,11... | collective-permute-start | bytes 3538952 | tf_op jit(solution)/shard_map/ppermute | solution.py:595
  168.6 4.7 %collective-permute-start.16 = (f32[144,128]{1,0:T(8,128)S(1)}, f32[144,128]{1,0:T(8,128)S(1)}, u32[]{:S(2)}, u32[]{:S(2)}) collective-permute-start(f32[144,128]{1,0:T(8,128)S(1)} %slice_select_fusion.7), channel_id=1, source_target_pairs={{0,2},{1,3},{2,0},{3,1},{4,6},{5,7},{6,4},{7,5},{8,10},{9,11},{10,... | collective-permute-start | bytes 221192 | tf_op jit(solution)/shard_map/ppermute | solution.py:595
  173.4 16.6 %copy-start.9 = (f32[2304,128]{1,0:T(8,128)}, f32[2304,128]{1,0:T(8,128)S(1)}, u32[]{:S(2)}) copy-start(f32[2304,128]{1,0:T(8,128)S(1)} %bitcast_add_fusion) | copy-start | bytes 3538948
  173.4 6.4 %collective-permute-start.18 = (f32[288,128]{1,0:T(8,128)S(1)}, f32[288,128]{1,0:T(8,128)S(1)}, u32[]{:S(2)}, u32[]{:S(2)}) collective-permute-start(f32[288,128]{1,0:T(8,128)S(1)} %pad_maximum_fusion.5), channel_id=1, source_target_pairs={{0,16},{1,17},{2,18},{3,19},{4,20},{5,21},{6,22},{7,23},{8,24},{9,... | collective-permute-start | bytes 442376 | tf_op jit(solution)/shard_map/ppermute | solution.py:595
  179.9 16.4 %collective-permute-start.19 = (f32[576,128]{1,0:T(8,128)S(1)}, f32[576,128]{1,0:T(8,128)S(1)}, u32[]{:S(2)}, u32[]{:S(2)}) collective-permute-start(f32[576,128]{1,0:T(8,128)S(1)} %pad_maximum_fusion.4), channel_id=1, source_target_pairs={{0,8},{1,9},{2,10},{3,11},{4,12},{5,13},{6,14},{7,15},{8,0},{9,1},... | collective-permute-start | bytes 884744 | tf_op jit(solution)/shard_map/ppermute | solution.py:595
  190.0 14.1 %collective-permute-start.17 = (f32[1152,128]{1,0:T(8,128)S(1)}, f32[1152,128]{1,0:T(8,128)S(1)}, u32[]{:S(2)}, u32[]{:S(2)}) collective-permute-start(f32[1152,128]{1,0:T(8,128)S(1)} %slice_select_fusion.4), channel_id=1, source_target_pairs={{0,2},{1,3},{2,0},{3,1},{4,6},{5,7},{6,4},{7,5},{8,10},{9,11},{10,... | collective-permute-start | bytes 1769480 | tf_op jit(solution)/shard_map/ppermute | solution.py:595
  190.6 13.6 %copy-start.10 = (f32[2304,128]{1,0:T(8,128)S(1)}, f32[2304,128]{1,0:T(8,128)}, u32[]{:S(2)}) copy-start(f32[2304,128]{1,0:T(8,128)} %copy-done.9) | copy-start | bytes 3538948
  196.3 9.8 %copy-start.3 = (f32[288,1024]{1,0:T(8,128)S(1)}, f32[288,1024]{1,0:T(8,128)}, u32[]{:S(2)}) copy-start(f32[288,1024]{1,0:T(8,128)} %get-tuple-element.26.refs_0_) | copy-start | bytes 3538948
  196.3 12.8 %copy-start.4 = (f32[288,1024]{1,0:T(8,128)S(1)}, f32[288,1024]{1,0:T(8,128)}, u32[]{:S(2)}) copy-start(f32[288,1024]{1,0:T(8,128)} %get-tuple-element.32.refs_1_) | copy-start | bytes 3538948
  204.2 13.2 %collective-permute-start.32 = (f32[1152,128]{1,0:T(8,128)S(1)}, f32[1152,128]{1,0:T(8,128)S(1)}, u32[]{:S(2)}, u32[]{:S(2)}) collective-permute-start(f32[1152,128]{1,0:T(8,128)S(1)} %pad_maximum_fusion.3), channel_id=1, source_target_pairs={{0,4},{1,5},{2,6},{3,7},{4,0},{5,1},{6,2},{7,3},{8,12},{9,13},{10,... | collective-permute-start | bytes 1769480 | tf_op jit(solution)/shard_map/ppermute | solution.py:595
  206.1 21.4 %collective-permute-start.24 = (f32[288,1024]{1,0:T(8,128)S(1)}, f32[288,1024]{1,0:T(8,128)}, u32[]{:S(2)}, u32[]{:S(2)}) collective-permute-start(f32[288,1024]{1,0:T(8,128)S(1)} %copy-done.3), channel_id=1, source_target_pairs={{0,2},{4,6},{8,10},{12,14},{16,18},{20,22},{24,26},{28,30}} | collective-permute-start | bytes 3538952 | tf_op jit(solution)/shard_map/ppermute | solution.py:704
  207.4 21.4 %collective-permute-start.20 = (f32[288,1024]{1,0:T(8,128)S(1)}, f32[288,1024]{1,0:T(8,128)}, u32[]{:S(2)}, u32[]{:S(2)}) collective-permute-start(f32[288,1024]{1,0:T(8,128)S(1)} %copy-done.3), channel_id=1, source_target_pairs={{0,1},{4,5},{8,9},{12,13},{16,17},{20,21},{24,25},{28,29}} | collective-permute-start | bytes 3538952 | tf_op jit(solution)/shard_map/ppermute | solution.py:735
  209.1 27.8 %collective-permute-start.25 = (f32[288,1024]{1,0:T(8,128)S(1)}, f32[288,1024]{1,0:T(8,128)}, u32[]{:S(2)}, u32[]{:S(2)}) collective-permute-start(f32[288,1024]{1,0:T(8,128)S(1)} %copy-done.4), channel_id=1, source_target_pairs={{0,2},{4,6},{8,10},{12,14},{16,18},{20,22},{24,26},{28,30}} | collective-permute-start | bytes 3538952 | tf_op jit(solution)/shard_map/ppermute | solution.py:709
  211.2 14.9 %collective-permute-start.34 = (f32[1024,128]{1,0:T(8,128)}, f32[1024,128]{1,0:T(8,128)}, u32[]{:S(2)}, u32[]{:S(2)}) collective-permute-start(f32[1024,128]{1,0:T(8,128)} %slice.73), channel_id=1, source_target_pairs={{0,16},{1,17},{2,18},{3,19}} | collective-permute-start | bytes 1572872 | tf_op jit(solution)/shard_map/ppermute | solution.py:624
  217.6 1.2 copy-start.13
  218.8 23.2 %collective-permute-start.33 = (f32[2304,128]{1,0:T(8,128)}, f32[2304,128]{1,0:T(8,128)}, u32[]{:S(2)}, u32[]{:S(2)}) collective-permute-start(f32[2304,128]{1,0:T(8,128)} %pad_maximum_fusion.2), channel_id=1, source_target_pairs={{0,1},{1,0},{2,3},{3,2},{4,5},{5,4},{6,7},{7,6},{8,9},{9,8},{10,11... | collective-permute-start | bytes 3538952 | tf_op jit(solution)/shard_map/ppermute | solution.py:595
  226.1 10.8 %copy-start.15 = (f32[1024,128]{1,0:T(8,128)}, f32[1024,128]{1,0:T(8,128)S(1)}, u32[]{:S(2)}) copy-start(f32[1024,128]{1,0:T(8,128)S(1)} %broadcast_select_fusion.4) | copy-start | bytes 1572868
  226.2 12.5 %collective-permute-start.35 = (f32[1024,128]{1,0:T(8,128)S(1)}, f32[1024,128]{1,0:T(8,128)S(1)}, u32[]{:S(2)}, u32[]{:S(2)}) collective-permute-start(f32[1024,128]{1,0:T(8,128)S(1)} %broadcast_select_fusion.4), channel_id=1, source_target_pairs={{0,8},{16,24},{1,9},{17,25},{2,10},{18,26},{3,11},{19,27}} | collective-permute-start | bytes 1572872 | tf_op jit(solution)/shard_map/ppermute | solution.py:624
  227.5 22.1 %collective-permute-start.26 = (f32[288,1024]{1,0:T(8,128)}, f32[288,1024]{1,0:T(8,128)}, u32[]{:S(2)}, u32[]{:S(2)}) collective-permute-start(f32[288,1024]{1,0:T(8,128)} %get-tuple-element.33.refs_2_), channel_id=1, source_target_pairs={{0,2},{4,6},{8,10},{12,14},{16,18},{20,22},{24,26},{28,30}} | collective-permute-start | bytes 3538952 | tf_op jit(solution)/shard_map/ppermute | solution.py:709
  228.8 22.1 %collective-permute-start.21 = (f32[288,1024]{1,0:T(8,128)S(1)}, f32[288,1024]{1,0:T(8,128)}, u32[]{:S(2)}, u32[]{:S(2)}) collective-permute-start(f32[288,1024]{1,0:T(8,128)S(1)} %copy-done.4), channel_id=1, source_target_pairs={{0,1},{4,5},{8,9},{12,13},{16,17},{20,21},{24,25},{28,29}} | collective-permute-start | bytes 3538952 | tf_op jit(solution)/shard_map/ppermute | solution.py:735
  236.9 14.8 %collective-permute-start.22 = (f32[288,1024]{1,0:T(8,128)}, f32[288,1024]{1,0:T(8,128)}, u32[]{:S(2)}, u32[]{:S(2)}) collective-permute-start(f32[288,1024]{1,0:T(8,128)} %get-tuple-element.33.refs_2_), channel_id=1, source_target_pairs={{0,1},{4,5},{8,9},{12,13},{16,17},{20,21},{24,25},{28,29}} | collective-permute-start | bytes 3538952 | tf_op jit(solution)/shard_map/ppermute | solution.py:735
  238.6 0.8 copy-start.16
  239.4 22.8 %collective-permute-start.27 = (f32[288,1024]{1,0:T(8,128)}, f32[288,1024]{1,0:T(8,128)}, u32[]{:S(2)}, u32[]{:S(2)}) collective-permute-start(f32[288,1024]{1,0:T(8,128)} %get-tuple-element.37.refs_3_), channel_id=1, source_target_pairs={{0,2},{4,6},{8,10},{12,14},{16,18},{20,22},{24,26},{28,30}} | collective-permute-start | bytes 3538952 | tf_op jit(solution)/shard_map/ppermute | solution.py:714
  240.7 3.4 %copy-start.14 = (f32[1152,128]{1,0:T(8,128)S(1)}, f32[1152,128]{1,0:T(8,128)}, u32[]{:S(2)}) copy-start(f32[1152,128]{1,0:T(8,128)} %copy-done.13) | copy-start | bytes 1769476
  242.0 21.6 %collective-permute-start.36 = (f32[1024,128]{1,0:T(8,128)S(1)}, f32[1024,128]{1,0:T(8,128)S(1)}, u32[]{:S(2)}, u32[]{:S(2)}) collective-permute-start(f32[1024,128]{1,0:T(8,128)S(1)} %broadcast_select_fusion.5), channel_id=1, source_target_pairs={{0,4},{8,12},{16,20},{24,28},{1,5},{9,13},{17,21},{25,29},{2,6},{1... | collective-permute-start | bytes 1572872 | tf_op jit(solution)/shard_map/ppermute | solution.py:624
  249.6 21.4 %collective-permute-start.28 = (f32[288,1024]{1,0:T(8,128)}, f32[288,1024]{1,0:T(8,128)S(1)}, u32[]{:S(2)}, u32[]{:S(2)}) collective-permute-start(f32[288,1024]{1,0:T(8,128)} %collective-permute-done.24.refs_8_), channel_id=1, source_target_pairs={{2,3},{6,7},{10,11},{14,15},{18,19},{22,23},{26,27},{30,31}} | collective-permute-start | bytes 3538952 | tf_op jit(solution)/shard_map/ppermute | solution.py:735
  250.9 20.0 %collective-permute-start.23 = (f32[288,1024]{1,0:T(8,128)}, f32[288,1024]{1,0:T(8,128)S(1)}, u32[]{:S(2)}, u32[]{:S(2)}) collective-permute-start(f32[288,1024]{1,0:T(8,128)} %get-tuple-element.37.refs_3_), channel_id=1, source_target_pairs={{0,1},{4,5},{8,9},{12,13},{16,17},{20,21},{24,25},{28,29}} | collective-permute-start | bytes 3538952 | tf_op jit(solution)/shard_map/ppermute | solution.py:735
  251.7 19.3 %collective-permute-start.29 = (f32[288,1024]{1,0:T(8,128)}, f32[288,1024]{1,0:T(8,128)S(1)}, u32[]{:S(2)}, u32[]{:S(2)}) collective-permute-start(f32[288,1024]{1,0:T(8,128)} %collective-permute-done.25.refs_9_), channel_id=1, source_target_pairs={{2,3},{6,7},{10,11},{14,15},{18,19},{22,23},{26,27},{30,31}} | collective-permute-start | bytes 3538952 | tf_op jit(solution)/shard_map/ppermute | solution.py:735
  262.2 8.8 %collective-permute-start.30 = (f32[288,1024]{1,0:T(8,128)}, f32[288,1024]{1,0:T(8,128)S(1)}, u32[]{:S(2)}, u32[]{:S(2)}) collective-permute-start(f32[288,1024]{1,0:T(8,128)} %collective-permute-done.26.refs_10_), channel_id=1, source_target_pairs={{2,3},{6,7},{10,11},{14,15},{18,19},{22,23},{26,27},{30,31}} | collective-permute-start | bytes 3538952 | tf_op jit(solution)/shard_map/ppermute | solution.py:735
  263.6 7.4 %collective-permute-start.31 = (f32[288,1024]{1,0:T(8,128)}, f32[288,1024]{1,0:T(8,128)S(1)}, u32[]{:S(2)}, u32[]{:S(2)}) collective-permute-start(f32[288,1024]{1,0:T(8,128)} %collective-permute-done.27.refs_11_), channel_id=1, source_target_pairs={{2,3},{6,7},{10,11},{14,15},{18,19},{22,23},{26,27},{30,31}} | collective-permute-start | bytes 3538952 | tf_op jit(solution)/shard_map/ppermute | solution.py:735

commit v4 on v3

--- a/solution.py
+++ b/solution.py
@@ -90,7 +90,7 @@
 
         return carry
 
-    lax.fori_loop(0, held, look, 0)
+    lax.fori_loop(0, held, look, 0, unroll=4)
     lane = lax.broadcasted_iota(jnp.int32, (8, LANES), 1)
     line = jnp.full((8, LANES), -1, jnp.int32)
     for s in range(most):
@@ -142,7 +142,7 @@
             flat_ref[pl.ds(g * 8 * half + k, 8, stride=half), :] = rows[:, k * LANES : (k + 1) * LANES]
         return carry
 
-    lax.fori_loop(0, held // 8, spread_out, 0)
+    lax.fori_loop(0, held // 8, spread_out, 0, unroll=2)
 
     def assign(t, carry):
         alive = is_live(tally_ref, t)
@@ -186,7 +186,7 @@
             put(m * held + 4 * q + order[1], jnp.where(left, pltpu.roll(up, TB, 1), low))
         return carry
 
-    lax.fori_loop(0, held // 4, quad, 0, unroll=2)
+    lax.fori_loop(0, held // 4, quad, 0, unroll=4)
 
     lane = lax.broadcasted_iota(jnp.int32, (8, LANES), 1)
 

time: 281 us -> 279 us (level)
  transfers between devices with their start and end apart: 38 -> 38, of which waited for: 15 -> 15; matrix products, arithmetic and copies ran while one was open for 5% -> 5% of each run, Pallas kernels for 6% -> 5%
where the time goes in v4:
time: 279 us; the launch traced here: 278 us
  waiting for transfers between devices  140 us (50%)
  starting transfers between devices  62.7 us (22%)
  Pallas kernels  51.5 us (18%)
  local copies, waits for them, and re-layouts  9.65 us (3%)
  other arithmetic  7.68 us (3%)
  matrix products  5.28 us (2%)
    ppermute x5, waiting for transfers between devices, scatter(): x = jnp.where(index & mask != 0, lax.ppermute(x[h:], axis, pairs), x[:h])  84.3 us
    pallas_call x1, Pallas kernels, assemble(): pl.pallas_call(functools.partial(assemble_kernel, landing.shape[0], capac...  24 us
    ppermute x7, waiting for transfers between devices, exchange(): return lax.ppermute(x, axis, [(d, d ^ mask) for d in range(count)])  21.7 us
    ppermute x7, starting transfers between devices, exchange(): return lax.ppermute(x, axis, [(d, d ^ mask) for d in range(count)])  16.6 us
    ppermute x8, starting transfers between devices, per_device(): lax.ppermute(piece, 'col', [(d, d + mask)])  11.3 us
    pallas_call x1, Pallas kernels, stage(): pl.pallas_call(functools.partial(stage_kernel, held, devices, capacity, g...  11.1 us
    ppermute x2, waiting for transfers between devices, per_device(): sent += [lax.ppermute(piece, 'col', far) for piece in panel[1:MIDDLE]]  10.3 us
    pallas_call x1, Pallas kernels, finish(): pl.pallas_call(functools.partial(finish_kernel, len(panels), width), out_...  9.21 us
  transfers between devices with their start and end apart: 38, of which 15 were waited for; matrix products, arithmetic and copies ran while one was open for 5% of the time, Pallas kernels for 5%

profile of v4, /device:TPU:4, one launch (start us, length us, event | category | flops | bytes accessed | tf_op | source)
XLA Modules:
  0.0 278.4 jit_solution(12958053946534758491)
XLA Ops:
  0.6 1.6 copy-done.1
  3.5 3.6 %pick.1 = f32[136,128]{1,0:T(8,128)S(1)} custom-call(s32[128]{0:T(128)S(1)} %copy-done.5, s32[4]{0:T(128)S(1)} %copy-done.7, f32[128,4096]{1,0:T(8,128)S(1)} %copy-done.1), custom_call_target="tpu_custom_call" | custom-call | tf_op jit(solution)/shard_map/pick/pallas_call | solution.py:105
  7.2 1.3 collective-permute-start
  8.5 1.3 collective-permute-start.1
  9.8 1.3 collective-permute-start.2
  11.1 1.3 collective-permute-start.3
  12.4 1.3 collective-permute-start.4
  13.7 1.3 collective-permute-start.5
  15.0 1.3 collective-permute-start.6
  16.4 1.9 collective-permute-done.3
  18.9 2.8 collective-permute-done.5
  21.7 0.7 collective-permute-done.6
  22.5 1.3 collective-permute-start.7
  23.8 0.7 collective-permute-start.8
  24.5 0.7 collective-permute-start.9
  25.2 11.1 %stage.1 = f32[8448,128]{1,0:T(8,128)S(1)} custom-call(s32[128]{0:T(128)S(1)} %copy-done.6, s32[4]{0:T(128)S(1)} %copy-done.8, f32[128,4096]{1,0:T(8,128)S(1)} %copy-done.2), custom_call_target="tpu_custom_call" | custom-call | tf_op jit(solution)/shard_map/stage/pallas_call | solution.py:209
  36.4 2.1 copy-done
  38.6 4.1 %all-to-all-start = ((f32[32,264,128]{2,1,0:T(8,128)}), f32[32,264,128]{2,1,0:T(8,128)}, u32[]{:S(2)}, u32[]{:S(2)}) async-start(f32[32,264,128]{2,1,0:T(8,128)} %bitcast.16), calls=%async_computation | async-start | bytes 8650752 | tf_op jit(solution)/shard_map/all_to_all | solution.py:684
  43.3 3.0 %factor.1 = f32[4608,128]{1,0:T(8,128)} custom-call(s32[128]{0:T(128)} %convert_element_type.15.label_ref, s32[1]{0:T(128)} %bitcast.3.me_ref, f32[1152,2304]{1,0:T(8,128)} %front_ref.3, f32[4352,128]{1,0:T(8,128)} %copy-done.12), custom_call_target="tpu_custom_call" | custom-call | tf_op jit(solution)/shard_map/factor/pallas_call | solution.py:397
  46.4 1.5 slice.75
  47.9 1.7 collective-permute-start.10
  49.8 0.7 collective-permute-start.11
  52.1 1.5 collective-permute-start.14
  53.6 84.3 %collective-permute-done.14 = f32[144,128]{1,0:T(8,128)S(1)} collective-permute-done((f32[144,128]{1,0:T(8,128)S(1)}, f32[144,128]{1,0:T(8,128)S(1)}, u32[]{:S(2)}, u32[]{:S(2)}) %collective-permute-start.14) | collective-permute-done | bytes 73760 | tf_op jit(solution)/shard_map/ppermute | solution.py:644
  137.9 1.1 all-to-all-done
  139.0 1.0 convert_reduce_fusion
  140.7 24.0 %assemble.1 = (f32[4,1152,128]{2,1,0:T(8,128)}, f32[288,1024]{1,0:T(8,128)}, f32[288,1024]{1,0:T(8,128)}, f32[288,1024]{1,0:T(8,128)}, f32[288,1024]{1,0:T(8,128)}) custom-call(s32[256]{0:T(256)} %convert_element_type.17.landing_ref, s32[1]{0:T(128)} %bitcast.5.first_ref, f32[1152,2304]{1,0:T(8,128)} %front_ref.3, f32[8448,128]{1,0:T(8,128)} %bitcast.6.incoming_ref, ...), custom_call_target="tpu_custom_call" | custom-call | tf_op jit(solution)/shard_map/assemble/pallas_call | solution.py:513
  164.7 1.8 slice_select_fusion.2
  166.6 1.6 collective-permute-start.16
  168.1 3.1 %collective-permute-done.16 = f32[144,128]{1,0:T(8,128)S(1)} collective-permute-done((f32[144,128]{1,0:T(8,128)S(1)}, f32[144,128]{1,0:T(8,128)S(1)}, u32[]{:S(2)}, u32[]{:S(2)}) %collective-permute-start.16) | collective-permute-done | bytes 73760 | tf_op jit(solution)/shard_map/ppermute | solution.py:595
  171.4 2.5 collective-permute-start.18
  173.9 3.9 %collective-permute-done.18 = f32[288,128]{1,0:T(8,128)S(1)} collective-permute-done((f32[288,128]{1,0:T(8,128)S(1)}, f32[288,128]{1,0:T(8,128)S(1)}, u32[]{:S(2)}, u32[]{:S(2)}) %collective-permute-start.18) | collective-permute-done | bytes 147488 | tf_op jit(solution)/shard_map/ppermute | solution.py:595
  177.9 10.1 %collective-permute-start.19 = (f32[576,128]{1,0:T(8,128)S(1)}, f32[576,128]{1,0:T(8,128)S(1)}, u32[]{:S(2)}, u32[]{:S(2)}) collective-permute-start(f32[576,128]{1,0:T(8,128)S(1)} %pad_maximum_fusion.4), channel_id=1, source_target_pairs={{0,8},{1,9},{2,10},{3,11},{4,12},{5,13},{6,14},{7,15},{8,0},{9,1},... | collective-permute-start | bytes 884744 | tf_op jit(solution)/shard_map/ppermute | solution.py:595
  188.6 5.7 %collective-permute-done.19 = f32[576,128]{1,0:T(8,128)S(1)} collective-permute-done((f32[576,128]{1,0:T(8,128)S(1)}, f32[576,128]{1,0:T(8,128)S(1)}, u32[]{:S(2)}, u32[]{:S(2)}) %collective-permute-start.19) | collective-permute-done | bytes 294944 | tf_op jit(solution)/shard_map/ppermute | solution.py:595
  194.4 7.8 %collective-permute-done.17 = f32[1152,128]{1,0:T(8,128)S(1)} collective-permute-done((f32[1152,128]{1,0:T(8,128)S(1)}, f32[1152,128]{1,0:T(8,128)S(1)}, u32[]{:S(2)}, u32[]{:S(2)}) %collective-permute-start.17) | collective-permute-done | bytes 589856 | tf_op jit(solution)/shard_map/ppermute | solution.py:595
  202.3 1.8 collective-permute-start.32
  204.1 1.3 collective-permute-start.24
  205.4 1.7 collective-permute-start.20
  207.1 1.3 collective-permute-start.25
  208.4 0.8 slice.73
  209.2 5.0 %collective-permute-start.34 = (f32[1024,128]{1,0:T(8,128)}, f32[1024,128]{1,0:T(8,128)}, u32[]{:S(2)}, u32[]{:S(2)}) collective-permute-start(f32[1024,128]{1,0:T(8,128)} %slice.73), channel_id=1, source_target_pairs={{0,16},{1,17},{2,18},{3,19}} | collective-permute-start | bytes 1572872 | tf_op jit(solution)/shard_map/ppermute | solution.py:624
  214.2 1.2 collective-permute-done.32
  215.6 1.2 pad_maximum_fusion.2
  216.8 7.3 %collective-permute-done.34 = f32[1024,128]{1,0:T(8,128)} collective-permute-done((f32[1024,128]{1,0:T(8,128)}, f32[1024,128]{1,0:T(8,128)}, u32[]{:S(2)}, u32[]{:S(2)}) %collective-permute-start.34) | collective-permute-done | bytes 524320 | tf_op jit(solution)/shard_map/ppermute | solution.py:624
  224.2 1.3 collective-permute-start.35
  225.5 1.3 collective-permute-start.26
  226.8 1.7 collective-permute-start.21
  228.5 6.4 %collective-permute-done.25.refs_9_ = f32[288,1024]{1,0:T(8,128)} collective-permute-done((f32[288,1024]{1,0:T(8,128)S(1)}, f32[288,1024]{1,0:T(8,128)}, u32[]{:S(2)}, u32[]{:S(2)}) %collective-permute-start.25) | collective-permute-done | bytes 1179680 | tf_op jit(solution)/shard_map/ppermute | solution.py:709
  234.9 1.7 collective-permute-start.22
  236.6 0.8 copy-done.16
  237.4 1.3 collective-permute-start.27
  238.8 1.1 broadcast_select_fusion.5
  240.0 2.2 collective-permute-start.36
  242.2 1.4 broadcast_select_fusion.1
  243.6 3.9 %collective-permute-done.26.refs_10_ = f32[288,1024]{1,0:T(8,128)} collective-permute-done((f32[288,1024]{1,0:T(8,128)}, f32[288,1024]{1,0:T(8,128)}, u32[]{:S(2)}, u32[]{:S(2)}) %collective-permute-start.26) | collective-permute-done | bytes 1179680 | tf_op jit(solution)/shard_map/ppermute | solution.py:709
  247.6 1.4 collective-permute-start.28
  248.9 0.7 collective-permute-start.23
  249.7 1.4 collective-permute-start.29
  251.1 9.1 %collective-permute-done.27.refs_11_ = f32[288,1024]{1,0:T(8,128)} collective-permute-done((f32[288,1024]{1,0:T(8,128)}, f32[288,1024]{1,0:T(8,128)}, u32[]{:S(2)}, u32[]{:S(2)}) %collective-permute-start.27) | collective-permute-done | bytes 1179680 | tf_op jit(solution)/shard_map/ppermute | solution.py:714
  260.2 1.4 collective-permute-start.30
  261.6 1.4 collective-permute-start.31
  263.7 1.8 fusion
  265.5 3.5 %fusion.3.refs_17_ = f32[1024,128]{1,0:T(8,128)S(1)} fusion(f32[1024,1024]{1,0:T(8,128)S(1)} %unpack.1, f32[1024,128]{1,0:T(8,128)S(1)} %fusion), kind=kOutput, calls=%fused_computation.42 | convolution fusion | flops 805306368 | bytes 5242880 | tf_op jit(solution)/shard_map/dot_general | solution.py:739
  269.0 9.2 %finish.1 = (f32[1152,256]{1,0:T(8,128)}, f32[1152,128]{1,0:T(8,128)}) custom-call(s32[2]{0:T(128)S(1)} %pad_add_fusion.where_ref, f32[288,1024]{1,0:T(8,128)S(1)} %copy-done.3, f32[288,1024]{1,0:T(8,128)S(1)} %copy-done.4, f32[288,1024]{1,0:T(8,128)} %get-tuple-element.33.refs_2_, f32[288,1024]{1,0:T(8,128)} %get-tuple-element.37.refs_3_, ...), custom_call_target="tpu_custom_call" | custom-call | tf_op jit(solution)/shard_map/finish/pallas_call | solution.py:576
  (97 shorter events, 7.2 us)
Async XLA Ops:
  0.6 1.6 copy-start.1
  2.2 0.7 copy-start.5
  2.9 0.7 copy-start.7
  3.5 21.7 %copy-start.2 = (f32[128,4096]{1,0:T(8,128)S(1)}, f32[128,4096]{1,0:T(8,128)}, u32[]{:S(2)}) copy-start(f32[128,4096]{1,0:T(8,128)} %tiles_ref.3) | copy-start | bytes 6291460
  3.5 21.7 %copy-start.6 = (s32[128]{0:T(128)S(1)}, s32[128]{0:T(128)}, u32[]{:S(2)}) copy-start(s32[128]{0:T(128)} %target_ref.2) | copy-start | bytes 1540
  3.5 21.7 %copy-start.8 = (s32[4]{0:T(128)S(1)}, s32[4]{0:T(128)}, u32[]{:S(2)}) copy-start(s32[4]{0:T(128)} %tally_ref.1) | copy-start | bytes 52
  7.2 6.5 %collective-permute-start = (f32[136,128]{1,0:T(8,128)S(1)}, f32[136,128]{1,0:T(8,128)S(1)}, u32[]{:S(2)}, u32[]{:S(2)}) collective-permute-start(f32[136,128]{1,0:T(8,128)S(1)} %pick.1), channel_id=1, source_target_pairs={{1,0},{3,2},{5,4},{7,6}} | collective-permute-start | bytes 208904 | tf_op jit(solution)/shard_map/ppermute | solution.py:632
  8.5 6.5 %collective-permute-start.1 = (f32[136,128]{1,0:T(8,128)S(1)}, f32[136,128]{1,0:T(8,128)S(1)}, u32[]{:S(2)}, u32[]{:S(2)}) collective-permute-start(f32[136,128]{1,0:T(8,128)S(1)} %pick.1), channel_id=1, source_target_pairs={{8,0},{10,2},{12,4},{14,6}} | collective-permute-start | bytes 208904 | tf_op jit(solution)/shard_map/ppermute | solution.py:632
  9.8 6.6 %collective-permute-start.2 = (f32[136,128]{1,0:T(8,128)S(1)}, f32[136,128]{1,0:T(8,128)S(1)}, u32[]{:S(2)}, u32[]{:S(2)}) collective-permute-start(f32[136,128]{1,0:T(8,128)S(1)} %pick.1), channel_id=1, source_target_pairs={{9,0},{11,2},{13,4},{15,6}} | collective-permute-start | bytes 208904 | tf_op jit(solution)/shard_map/ppermute | solution.py:632
  11.1 7.2 %collective-permute-start.3 = (f32[136,128]{1,0:T(8,128)S(1)}, f32[136,128]{1,0:T(8,128)S(1)}, u32[]{:S(2)}, u32[]{:S(2)}) collective-permute-start(f32[136,128]{1,0:T(8,128)S(1)} %pick.1), channel_id=1, source_target_pairs={{16,0},{18,2},{20,4},{22,6}} | collective-permute-start | bytes 208904 | tf_op jit(solution)/shard_map/ppermute | solution.py:632
  12.4 6.5 %collective-permute-start.4 = (f32[136,128]{1,0:T(8,128)S(1)}, f32[136,128]{1,0:T(8,128)S(1)}, u32[]{:S(2)}, u32[]{:S(2)}) collective-permute-start(f32[136,128]{1,0:T(8,128)S(1)} %pick.1), channel_id=1, source_target_pairs={{17,0},{19,2},{21,4},{23,6}} | collective-permute-start | bytes 208904 | tf_op jit(solution)/shard_map/ppermute | solution.py:632
  13.7 8.0 %collective-permute-start.5 = (f32[136,128]{1,0:T(8,128)S(1)}, f32[136,128]{1,0:T(8,128)S(1)}, u32[]{:S(2)}, u32[]{:S(2)}) collective-permute-start(f32[136,128]{1,0:T(8,128)S(1)} %pick.1), channel_id=1, source_target_pairs={{24,0},{26,2},{28,4},{30,6}} | collective-permute-start | bytes 208904 | tf_op jit(solution)/shard_map/ppermute | solution.py:632
  15.0 7.4 %collective-permute-start.6 = (f32[136,128]{1,0:T(8,128)S(1)}, f32[136,128]{1,0:T(8,128)S(1)}, u32[]{:S(2)}, u32[]{:S(2)}) collective-permute-start(f32[136,128]{1,0:T(8,128)S(1)} %pick.1), channel_id=1, source_target_pairs={{25,0},{27,2},{29,4},{31,6}} | collective-permute-start | bytes 208904 | tf_op jit(solution)/shard_map/ppermute | solution.py:632
  22.5 16.0 %collective-permute-start.7 = (f32[1088,128]{1,0:T(8,128)S(1)}, f32[1088,128]{1,0:T(8,128)S(1)}, u32[]{:S(2)}, u32[]{:S(2)}) collective-permute-start(f32[1088,128]{1,0:T(8,128)S(1)} %constant_dynamic-update-slice_fusion), channel_id=1, source_target_pairs={{2,0}} | collective-permute-start | bytes 1671176 | tf_op jit(solution)/shard_map/ppermute | solution.py:636
  23.8 14.7 %collective-permute-start.8 = (f32[1088,128]{1,0:T(8,128)S(1)}, f32[1088,128]{1,0:T(8,128)S(1)}, u32[]{:S(2)}, u32[]{:S(2)}) collective-permute-start(f32[1088,128]{1,0:T(8,128)S(1)} %constant_dynamic-update-slice_fusion), channel_id=1, source_target_pairs={{4,0}} | collective-permute-start | bytes 1671176 | tf_op jit(solution)/shard_map/ppermute | solution.py:636
  24.5 13.9 %collective-permute-start.9 = (f32[1088,128]{1,0:T(8,128)S(1)}, f32[1088,128]{1,0:T(8,128)S(1)}, u32[]{:S(2)}, u32[]{:S(2)}) collective-permute-start(f32[1088,128]{1,0:T(8,128)S(1)} %constant_dynamic-update-slice_fusion), channel_id=1, source_target_pairs={{6,0}} | collective-permute-start | bytes 1671176 | tf_op jit(solution)/shard_map/ppermute | solution.py:636
  36.4 2.1 copy-start
  38.6 4.1 %copy-start.12 = (f32[4352,128]{1,0:T(8,128)}, f32[4352,128]{1,0:T(8,128)S(1)}, u32[]{:S(2)}) copy-start(f32[4352,128]{1,0:T(8,128)S(1)} %pad_maximum_fusion.1.tiles_ref) | copy-start | bytes 6684676
  38.6 100.4 %all-to-all-start = ((f32[32,264,128]{2,1,0:T(8,128)}), f32[32,264,128]{2,1,0:T(8,128)}, u32[]{:S(2)}, u32[]{:S(2)}) async-start(f32[32,264,128]{2,1,0:T(8,128)} %bitcast.16), calls=%async_computation | async-start | bytes 8650752 | tf_op jit(solution)/shard_map/all_to_all | solution.py:684
  46.4 3.2 %copy-start.11 = (f32[4608,128]{1,0:T(8,128)S(1)}, f32[4608,128]{1,0:T(8,128)}, u32[]{:S(2)}) copy-start(f32[4608,128]{1,0:T(8,128)} %factor.1) | copy-start | bytes 7077892
  47.9 1.7 collective-permute-start.10
  49.8 0.7 collective-permute-start.11
  50.6 0.7 collective-permute-start.12
  51.4 0.7 collective-permute-start.13
  52.1 85.8 %collective-permute-start.14 = (f32[144,128]{1,0:T(8,128)S(1)}, f32[144,128]{1,0:T(8,128)S(1)}, u32[]{:S(2)}, u32[]{:S(2)}) collective-permute-start(f32[144,128]{1,0:T(8,128)S(1)} %slice.83), channel_id=1, source_target_pairs={{0,2},{1,3},{4,6},{5,7},{8,10},{9,11},{12,14},{13,15},{16,18},{17,... | collective-permute-start | bytes 221192 | tf_op jit(solution)/shard_map/ppermute | solution.py:644
  166.5 4.8 %collective-permute-start.15 = (f32[2304,128]{1,0:T(8,128)S(1)}, f32[2304,128]{1,0:T(8,128)S(1)}, u32[]{:S(2)}, u32[]{:S(2)}) collective-permute-start(f32[2304,128]{1,0:T(8,128)S(1)} %bitcast.18), channel_id=1, source_target_pairs={{0,1},{1,0},{2,3},{3,2},{4,5},{5,4},{6,7},{7,6},{8,9},{9,8},{10,11... | collective-permute-start | bytes 3538952 | tf_op jit(solution)/shard_map/ppermute | solution.py:595
  166.6 4.7 %collective-permute-start.16 = (f32[144,128]{1,0:T(8,128)S(1)}, f32[144,128]{1,0:T(8,128)S(1)}, u32[]{:S(2)}, u32[]{:S(2)}) collective-permute-start(f32[144,128]{1,0:T(8,128)S(1)} %slice_select_fusion.7), channel_id=1, source_target_pairs={{0,2},{1,3},{2,0},{3,1},{4,6},{5,7},{6,4},{7,5},{8,10},{9,11},{10,... | collective-permute-start | bytes 221192 | tf_op jit(solution)/shard_map/ppermute | solution.py:595
  171.4 16.7 %copy-start.9 = (f32[2304,128]{1,0:T(8,128)}, f32[2304,128]{1,0:T(8,128)S(1)}, u32[]{:S(2)}) copy-start(f32[2304,128]{1,0:T(8,128)S(1)} %bitcast_add_fusion) | copy-start | bytes 3538948
  171.4 6.4 %collective-permute-start.18 = (f32[288,128]{1,0:T(8,128)S(1)}, f32[288,128]{1,0:T(8,128)S(1)}, u32[]{:S(2)}, u32[]{:S(2)}) collective-permute-start(f32[288,128]{1,0:T(8,128)S(1)} %pad_maximum_fusion.5), channel_id=1, source_target_pairs={{0,16},{1,17},{2,18},{3,19},{4,20},{5,21},{6,22},{7,23},{8,24},{9,... | collective-permute-start | bytes 442376 | tf_op jit(solution)/shard_map/ppermute | solution.py:595
  177.9 16.4 %collective-permute-start.19 = (f32[576,128]{1,0:T(8,128)S(1)}, f32[576,128]{1,0:T(8,128)S(1)}, u32[]{:S(2)}, u32[]{:S(2)}) collective-permute-start(f32[576,128]{1,0:T(8,128)S(1)} %pad_maximum_fusion.4), channel_id=1, source_target_pairs={{0,8},{1,9},{2,10},{3,11},{4,12},{5,13},{6,14},{7,15},{8,0},{9,1},... | collective-permute-start | bytes 884744 | tf_op jit(solution)/shard_map/ppermute | solution.py:595
  188.1 14.1 %collective-permute-start.17 = (f32[1152,128]{1,0:T(8,128)S(1)}, f32[1152,128]{1,0:T(8,128)S(1)}, u32[]{:S(2)}, u32[]{:S(2)}) collective-permute-start(f32[1152,128]{1,0:T(8,128)S(1)} %slice_select_fusion.4), channel_id=1, source_target_pairs={{0,2},{1,3},{2,0},{3,1},{4,6},{5,7},{6,4},{7,5},{8,10},{9,11},{10,... | collective-permute-start | bytes 1769480 | tf_op jit(solution)/shard_map/ppermute | solution.py:595
  188.6 13.6 %copy-start.10 = (f32[2304,128]{1,0:T(8,128)S(1)}, f32[2304,128]{1,0:T(8,128)}, u32[]{:S(2)}) copy-start(f32[2304,128]{1,0:T(8,128)} %copy-done.9) | copy-start | bytes 3538948
  194.4 9.7 %copy-start.3 = (f32[288,1024]{1,0:T(8,128)S(1)}, f32[288,1024]{1,0:T(8,128)}, u32[]{:S(2)}) copy-start(f32[288,1024]{1,0:T(8,128)} %get-tuple-element.26.refs_0_) | copy-start | bytes 3538948
  194.4 12.7 %copy-start.4 = (f32[288,1024]{1,0:T(8,128)S(1)}, f32[288,1024]{1,0:T(8,128)}, u32[]{:S(2)}) copy-start(f32[288,1024]{1,0:T(8,128)} %get-tuple-element.32.refs_1_) | copy-start | bytes 3538948
  202.3 13.2 %collective-permute-start.32 = (f32[1152,128]{1,0:T(8,128)S(1)}, f32[1152,128]{1,0:T(8,128)S(1)}, u32[]{:S(2)}, u32[]{:S(2)}) collective-permute-start(f32[1152,128]{1,0:T(8,128)S(1)} %pad_maximum_fusion.3), channel_id=1, source_target_pairs={{0,4},{1,5},{2,6},{3,7},{4,0},{5,1},{6,2},{7,3},{8,12},{9,13},{10,... | collective-permute-start | bytes 1769480 | tf_op jit(solution)/shard_map/ppermute | solution.py:595
  204.1 21.4 %collective-permute-start.24 = (f32[288,1024]{1,0:T(8,128)S(1)}, f32[288,1024]{1,0:T(8,128)}, u32[]{:S(2)}, u32[]{:S(2)}) collective-permute-start(f32[288,1024]{1,0:T(8,128)S(1)} %copy-done.3), channel_id=1, source_target_pairs={{0,2},{4,6},{8,10},{12,14},{16,18},{20,22},{24,26},{28,30}} | collective-permute-start | bytes 3538952 | tf_op jit(solution)/shard_map/ppermute | solution.py:704
  205.4 21.4 %collective-permute-start.20 = (f32[288,1024]{1,0:T(8,128)S(1)}, f32[288,1024]{1,0:T(8,128)}, u32[]{:S(2)}, u32[]{:S(2)}) collective-permute-start(f32[288,1024]{1,0:T(8,128)S(1)} %copy-done.3), channel_id=1, source_target_pairs={{0,1},{4,5},{8,9},{12,13},{16,17},{20,21},{24,25},{28,29}} | collective-permute-start | bytes 3538952 | tf_op jit(solution)/shard_map/ppermute | solution.py:735
  207.1 27.8 %collective-permute-start.25 = (f32[288,1024]{1,0:T(8,128)S(1)}, f32[288,1024]{1,0:T(8,128)}, u32[]{:S(2)}, u32[]{:S(2)}) collective-permute-start(f32[288,1024]{1,0:T(8,128)S(1)} %copy-done.4), channel_id=1, source_target_pairs={{0,2},{4,6},{8,10},{12,14},{16,18},{20,22},{24,26},{28,30}} | collective-permute-start | bytes 3538952 | tf_op jit(solution)/shard_map/ppermute | solution.py:709
  209.2 14.9 %collective-permute-start.34 = (f32[1024,128]{1,0:T(8,128)}, f32[1024,128]{1,0:T(8,128)}, u32[]{:S(2)}, u32[]{:S(2)}) collective-permute-start(f32[1024,128]{1,0:T(8,128)} %slice.73), channel_id=1, source_target_pairs={{0,16},{1,17},{2,18},{3,19}} | collective-permute-start | bytes 1572872 | tf_op jit(solution)/shard_map/ppermute | solution.py:624
  215.6 1.2 copy-start.13
  216.8 23.2 %collective-permute-start.33 = (f32[2304,128]{1,0:T(8,128)}, f32[2304,128]{1,0:T(8,128)}, u32[]{:S(2)}, u32[]{:S(2)}) collective-permute-start(f32[2304,128]{1,0:T(8,128)} %pad_maximum_fusion.2), channel_id=1, source_target_pairs={{0,1},{1,0},{2,3},{3,2},{4,5},{5,4},{6,7},{7,6},{8,9},{9,8},{10,11... | collective-permute-start | bytes 3538952 | tf_op jit(solution)/shard_map/ppermute | solution.py:595
  224.1 10.8 %copy-start.15 = (f32[1024,128]{1,0:T(8,128)}, f32[1024,128]{1,0:T(8,128)S(1)}, u32[]{:S(2)}) copy-start(f32[1024,128]{1,0:T(8,128)S(1)} %broadcast_select_fusion.4) | copy-start | bytes 1572868
  224.2 12.5 %collective-permute-start.35 = (f32[1024,128]{1,0:T(8,128)S(1)}, f32[1024,128]{1,0:T(8,128)S(1)}, u32[]{:S(2)}, u32[]{:S(2)}) collective-permute-start(f32[1024,128]{1,0:T(8,128)S(1)} %broadcast_select_fusion.4), channel_id=1, source_target_pairs={{0,8},{16,24},{1,9},{17,25},{2,10},{18,26},{3,11},{19,27}} | collective-permute-start | bytes 1572872 | tf_op jit(solution)/shard_map/ppermute | solution.py:624
  225.5 22.1 %collective-permute-start.26 = (f32[288,1024]{1,0:T(8,128)}, f32[288,1024]{1,0:T(8,128)}, u32[]{:S(2)}, u32[]{:S(2)}) collective-permute-start(f32[288,1024]{1,0:T(8,128)} %get-tuple-element.33.refs_2_), channel_id=1, source_target_pairs={{0,2},{4,6},{8,10},{12,14},{16,18},{20,22},{24,26},{28,30}} | collective-permute-start | bytes 3538952 | tf_op jit(solution)/shard_map/ppermute | solution.py:709
  226.8 22.1 %collective-permute-start.21 = (f32[288,1024]{1,0:T(8,128)S(1)}, f32[288,1024]{1,0:T(8,128)}, u32[]{:S(2)}, u32[]{:S(2)}) collective-permute-start(f32[288,1024]{1,0:T(8,128)S(1)} %copy-done.4), channel_id=1, source_target_pairs={{0,1},{4,5},{8,9},{12,13},{16,17},{20,21},{24,25},{28,29}} | collective-permute-start | bytes 3538952 | tf_op jit(solution)/shard_map/ppermute | solution.py:735
  234.9 14.8 %collective-permute-start.22 = (f32[288,1024]{1,0:T(8,128)}, f32[288,1024]{1,0:T(8,128)}, u32[]{:S(2)}, u32[]{:S(2)}) collective-permute-start(f32[288,1024]{1,0:T(8,128)} %get-tuple-element.33.refs_2_), channel_id=1, source_target_pairs={{0,1},{4,5},{8,9},{12,13},{16,17},{20,21},{24,25},{28,29}} | collective-permute-start | bytes 3538952 | tf_op jit(solution)/shard_map/ppermute | solution.py:735
  236.6 0.8 copy-start.16
  237.4 22.8 %collective-permute-start.27 = (f32[288,1024]{1,0:T(8,128)}, f32[288,1024]{1,0:T(8,128)}, u32[]{:S(2)}, u32[]{:S(2)}) collective-permute-start(f32[288,1024]{1,0:T(8,128)} %get-tuple-element.37.refs_3_), channel_id=1, source_target_pairs={{0,2},{4,6},{8,10},{12,14},{16,18},{20,22},{24,26},{28,30}} | collective-permute-start | bytes 3538952 | tf_op jit(solution)/shard_map/ppermute | solution.py:714
  238.7 3.5 %copy-start.14 = (f32[1152,128]{1,0:T(8,128)S(1)}, f32[1152,128]{1,0:T(8,128)}, u32[]{:S(2)}) copy-start(f32[1152,128]{1,0:T(8,128)} %copy-done.13) | copy-start | bytes 1769476
  240.0 21.6 %collective-permute-start.36 = (f32[1024,128]{1,0:T(8,128)S(1)}, f32[1024,128]{1,0:T(8,128)S(1)}, u32[]{:S(2)}, u32[]{:S(2)}) collective-permute-start(f32[1024,128]{1,0:T(8,128)S(1)} %broadcast_select_fusion.5), channel_id=1, source_target_pairs={{0,4},{8,12},{16,20},{24,28},{1,5},{9,13},{17,21},{25,29},{2,6},{1... | collective-permute-start | bytes 1572872 | tf_op jit(solution)/shard_map/ppermute | solution.py:624
  247.6 21.4 %collective-permute-start.28 = (f32[288,1024]{1,0:T(8,128)}, f32[288,1024]{1,0:T(8,128)S(1)}, u32[]{:S(2)}, u32[]{:S(2)}) collective-permute-start(f32[288,1024]{1,0:T(8,128)} %collective-permute-done.24.refs_8_), channel_id=1, source_target_pairs={{2,3},{6,7},{10,11},{14,15},{18,19},{22,23},{26,27},{30,31}} | collective-permute-start | bytes 3538952 | tf_op jit(solution)/shard_map/ppermute | solution.py:735
  248.9 20.0 %collective-permute-start.23 = (f32[288,1024]{1,0:T(8,128)}, f32[288,1024]{1,0:T(8,128)S(1)}, u32[]{:S(2)}, u32[]{:S(2)}) collective-permute-start(f32[288,1024]{1,0:T(8,128)} %get-tuple-element.37.refs_3_), channel_id=1, source_target_pairs={{0,1},{4,5},{8,9},{12,13},{16,17},{20,21},{24,25},{28,29}} | collective-permute-start | bytes 3538952 | tf_op jit(solution)/shard_map/ppermute | solution.py:735
  249.7 19.3 %collective-permute-start.29 = (f32[288,1024]{1,0:T(8,128)}, f32[288,1024]{1,0:T(8,128)S(1)}, u32[]{:S(2)}, u32[]{:S(2)}) collective-permute-start(f32[288,1024]{1,0:T(8,128)} %collective-permute-done.25.refs_9_), channel_id=1, source_target_pairs={{2,3},{6,7},{10,11},{14,15},{18,19},{22,23},{26,27},{30,31}} | collective-permute-start | bytes 3538952 | tf_op jit(solution)/shard_map/ppermute | solution.py:735
  260.2 8.8 %collective-permute-start.30 = (f32[288,1024]{1,0:T(8,128)}, f32[288,1024]{1,0:T(8,128)S(1)}, u32[]{:S(2)}, u32[]{:S(2)}) collective-permute-start(f32[288,1024]{1,0:T(8,128)} %collective-permute-done.26.refs_10_), channel_id=1, source_target_pairs={{2,3},{6,7},{10,11},{14,15},{18,19},{22,23},{26,27},{30,31}} | collective-permute-start | bytes 3538952 | tf_op jit(solution)/shard_map/ppermute | solution.py:735
  261.6 7.4 %collective-permute-start.31 = (f32[288,1024]{1,0:T(8,128)}, f32[288,1024]{1,0:T(8,128)S(1)}, u32[]{:S(2)}, u32[]{:S(2)}) collective-permute-start(f32[288,1024]{1,0:T(8,128)} %collective-permute-done.27.refs_11_), channel_id=1, source_target_pairs={{2,3},{6,7},{10,11},{14,15},{18,19},{22,23},{26,27},{30,31}} | collective-permute-start | bytes 3538952 | tf_op jit(solution)/shard_map/ppermute | solution.py:735

commit v5 on v4

--- a/solution.py
+++ b/solution.py
@@ -460,7 +460,7 @@
     lax.fori_loop(0, probe_ref.shape[0] // step, cut, 0)
     copy.wait()
     block = capacity * half + 8
-    group = 8 if slots % 8 == 0 else 2
+    group = 16 if slots % 16 == 0 else 2
     left = left_half((half, LANES))
 
     def place(g, carry):
@@ -509,7 +509,7 @@
     width = columns // len(order)
     smem = pl.BlockSpec(memory_space=pltpu.SMEM)
     vmem = pl.BlockSpec(memory_space=pltpu.VMEM)
-    row_chunk = 192 if local_rows % 192 == 0 else 64
+    row_chunk = next(n for n in (384, 192, 64) if local_rows % n == 0)
     return pl.pallas_call(
         functools.partial(
             assemble_kernel, landing.shape[0], capacity, tile_cols, tile_rows * tile_cols, row_chunk, width, order
@@ -552,7 +552,7 @@
 
     right_high, right_low = split(jnp.concatenate([inverse_ref[...].T, weights_ref[...]], axis=1))
     dot = functools.partial(jnp.dot, preferred_element_type=jnp.float32)
-    step = 192 if panel_ref.shape[0] % 192 == 0 else 64
+    step = next(n for n in (384, 192, 64) if panel_ref.shape[0] % n == 0)
 
     def body(b, carry):
         rows = pl.ds(pl.multiple_of(b * step, step), step)

time: 279 us -> 278 us (level)
  no operation moved by 1% of the time
where the time goes in v5:
time: 278 us; the launch traced here: 277 us
  waiting for transfers between devices  140 us (50%)
  starting transfers between devices  62.6 us (23%)
  Pallas kernels  50.1 us (18%)
  local copies, waits for them, and re-layouts  9.65 us (3%)
  other arithmetic  7.68 us (3%)
  matrix products  5.29 us (2%)
    ppermute x5, waiting for transfers between devices, scatter(): x = jnp.where(index & mask != 0, lax.ppermute(x[h:], axis, pairs), x[:h])  84.3 us
    pallas_call x1, Pallas kernels, assemble(): pl.pallas_call(functools.partial(assemble_kernel, landing.shape[0], capac...  23.2 us
    ppermute x7, waiting for transfers between devices, exchange(): return lax.ppermute(x, axis, [(d, d ^ mask) for d in range(count)])  21.8 us
    ppermute x7, starting transfers between devices, exchange(): return lax.ppermute(x, axis, [(d, d ^ mask) for d in range(count)])  16.5 us
    ppermute x8, starting transfers between devices, per_device(): lax.ppermute(piece, 'col', [(d, d + mask)])  11.3 us
    pallas_call x1, Pallas kernels, stage(): pl.pallas_call(functools.partial(stage_kernel, held, devices, capacity, g...  11.1 us
    ppermute x2, waiting for transfers between devices, per_device(): sent += [lax.ppermute(piece, 'col', far) for piece in panel[1:MIDDLE]]  10.3 us
    ppermute x1, waiting for transfers between devices, per_device(): sent += [lax.ppermute(piece, 'col', far) for piece in panel[MIDDLE:]]  9.14 us
  transfers between devices with their start and end apart: 38, of which 15 were waited for; matrix products, arithmetic and copies ran while one was open for 5% of the time, Pallas kernels for 5%

profile of v5, /device:TPU:4, one launch (start us, length us, event | category | flops | bytes accessed | tf_op | source)
XLA Modules:
  0.0 277.0 jit_solution(3909375431925608884)
XLA Ops:
  0.6 1.6 copy-done.1
  3.5 3.6 %pick.1 = f32[136,128]{1,0:T(8,128)S(1)} custom-call(s32[128]{0:T(128)S(1)} %copy-done.5, s32[4]{0:T(128)S(1)} %copy-done.7, f32[128,4096]{1,0:T(8,128)S(1)} %copy-done.1), custom_call_target="tpu_custom_call" | custom-call | tf_op jit(solution)/shard_map/pick/pallas_call | solution.py:105
  7.2 1.3 collective-permute-start
  8.5 1.3 collective-permute-start.1
  9.8 1.3 collective-permute-start.2
  11.1 1.3 collective-permute-start.3
  12.4 1.3 collective-permute-start.4
  13.7 1.3 collective-permute-start.5
  15.0 1.3 collective-permute-start.6
  16.4 1.9 collective-permute-done.3
  18.9 2.8 %collective-permute-done.5 = f32[136,128]{1,0:T(8,128)S(1)} collective-permute-done((f32[136,128]{1,0:T(8,128)S(1)}, f32[136,128]{1,0:T(8,128)S(1)}, u32[]{:S(2)}, u32[]{:S(2)}) %collective-permute-start.5) | collective-permute-done | bytes 69664 | tf_op jit(solution)/shard_map/ppermute | solution.py:632
  21.7 0.7 collective-permute-done.6
  22.5 1.3 collective-permute-start.7
  23.8 0.7 collective-permute-start.8
  24.5 0.7 collective-permute-start.9
  25.2 11.1 %stage.1 = f32[8448,128]{1,0:T(8,128)S(1)} custom-call(s32[128]{0:T(128)S(1)} %copy-done.6, s32[4]{0:T(128)S(1)} %copy-done.8, f32[128,4096]{1,0:T(8,128)S(1)} %copy-done.2), custom_call_target="tpu_custom_call" | custom-call | tf_op jit(solution)/shard_map/stage/pallas_call | solution.py:209
  36.4 2.1 copy-done
  38.6 4.1 %all-to-all-start = ((f32[32,264,128]{2,1,0:T(8,128)}), f32[32,264,128]{2,1,0:T(8,128)}, u32[]{:S(2)}, u32[]{:S(2)}) async-start(f32[32,264,128]{2,1,0:T(8,128)} %bitcast.16), calls=%async_computation | async-start | bytes 8650752 | tf_op jit(solution)/shard_map/all_to_all | solution.py:684
  43.3 3.0 %factor.1 = f32[4608,128]{1,0:T(8,128)} custom-call(s32[128]{0:T(128)} %convert_element_type.15.label_ref, s32[1]{0:T(128)} %bitcast.3.me_ref, f32[1152,2304]{1,0:T(8,128)} %front_ref.3, f32[4352,128]{1,0:T(8,128)} %copy-done.12), custom_call_target="tpu_custom_call" | custom-call | tf_op jit(solution)/shard_map/factor/pallas_call | solution.py:397
  46.4 1.5 slice.75
  47.9 1.7 collective-permute-start.10
  49.8 0.7 collective-permute-start.11
  52.1 1.5 collective-permute-start.14
  53.6 84.3 %collective-permute-done.14 = f32[144,128]{1,0:T(8,128)S(1)} collective-permute-done((f32[144,128]{1,0:T(8,128)S(1)}, f32[144,128]{1,0:T(8,128)S(1)}, u32[]{:S(2)}, u32[]{:S(2)}) %collective-permute-start.14) | collective-permute-done | bytes 73760 | tf_op jit(solution)/shard_map/ppermute | solution.py:644
  137.9 1.1 all-to-all-done
  139.0 1.0 convert_reduce_fusion
  140.7 23.2 %assemble.1 = (f32[4,1152,128]{2,1,0:T(8,128)}, f32[288,1024]{1,0:T(8,128)}, f32[288,1024]{1,0:T(8,128)}, f32[288,1024]{1,0:T(8,128)}, f32[288,1024]{1,0:T(8,128)}) custom-call(s32[256]{0:T(256)} %convert_element_type.17.landing_ref, s32[1]{0:T(128)} %bitcast.5.first_ref, f32[1152,2304]{1,0:T(8,128)} %front_ref.3, f32[8448,128]{1,0:T(8,128)} %bitcast.6.incoming_ref, ...), custom_call_target="tpu_custom_call" | custom-call | tf_op jit(solution)/shard_map/assemble/pallas_call | solution.py:513
  163.8 1.8 slice_select_fusion.2
  165.7 1.5 collective-permute-start.16
  167.2 3.1 %collective-permute-done.16 = f32[144,128]{1,0:T(8,128)S(1)} collective-permute-done((f32[144,128]{1,0:T(8,128)S(1)}, f32[144,128]{1,0:T(8,128)S(1)}, u32[]{:S(2)}, u32[]{:S(2)}) %collective-permute-start.16) | collective-permute-done | bytes 73760 | tf_op jit(solution)/shard_map/ppermute | solution.py:595
  170.6 2.4 collective-permute-start.18
  173.0 3.9 %collective-permute-done.18 = f32[288,128]{1,0:T(8,128)S(1)} collective-permute-done((f32[288,128]{1,0:T(8,128)S(1)}, f32[288,128]{1,0:T(8,128)S(1)}, u32[]{:S(2)}, u32[]{:S(2)}) %collective-permute-start.18) | collective-permute-done | bytes 147488 | tf_op jit(solution)/shard_map/ppermute | solution.py:595
  177.0 10.1 %collective-permute-start.19 = (f32[576,128]{1,0:T(8,128)S(1)}, f32[576,128]{1,0:T(8,128)S(1)}, u32[]{:S(2)}, u32[]{:S(2)}) collective-permute-start(f32[576,128]{1,0:T(8,128)S(1)} %pad_maximum_fusion.4), channel_id=1, source_target_pairs={{0,8},{1,9},{2,10},{3,11},{4,12},{5,13},{6,14},{7,15},{8,0},{9,1},... | collective-permute-start | bytes 884744 | tf_op jit(solution)/shard_map/ppermute | solution.py:595
  187.7 5.7 %collective-permute-done.19 = f32[576,128]{1,0:T(8,128)S(1)} collective-permute-done((f32[576,128]{1,0:T(8,128)S(1)}, f32[576,128]{1,0:T(8,128)S(1)}, u32[]{:S(2)}, u32[]{:S(2)}) %collective-permute-start.19) | collective-permute-done | bytes 294944 | tf_op jit(solution)/shard_map/ppermute | solution.py:595
  193.5 7.8 %collective-permute-done.17 = f32[1152,128]{1,0:T(8,128)S(1)} collective-permute-done((f32[1152,128]{1,0:T(8,128)S(1)}, f32[1152,128]{1,0:T(8,128)S(1)}, u32[]{:S(2)}, u32[]{:S(2)}) %collective-permute-start.17) | collective-permute-done | bytes 589856 | tf_op jit(solution)/shard_map/ppermute | solution.py:595
  201.4 1.8 collective-permute-start.32
  203.2 1.3 collective-permute-start.24
  204.5 1.7 collective-permute-start.20
  206.2 1.3 collective-permute-start.25
  207.5 0.8 slice.73
  208.3 5.0 %collective-permute-start.34 = (f32[1024,128]{1,0:T(8,128)}, f32[1024,128]{1,0:T(8,128)}, u32[]{:S(2)}, u32[]{:S(2)}) collective-permute-start(f32[1024,128]{1,0:T(8,128)} %slice.73), channel_id=1, source_target_pairs={{0,16},{1,17},{2,18},{3,19}} | collective-permute-start | bytes 1572872 | tf_op jit(solution)/shard_map/ppermute | solution.py:624
  213.3 1.2 collective-permute-done.32
  214.7 1.2 pad_maximum_fusion.2
  215.9 7.3 %collective-permute-done.34 = f32[1024,128]{1,0:T(8,128)} collective-permute-done((f32[1024,128]{1,0:T(8,128)}, f32[1024,128]{1,0:T(8,128)}, u32[]{:S(2)}, u32[]{:S(2)}) %collective-permute-start.34) | collective-permute-done | bytes 524320 | tf_op jit(solution)/shard_map/ppermute | solution.py:624
  223.3 1.3 collective-permute-start.35
  224.6 1.3 collective-permute-start.26
  225.9 1.7 collective-permute-start.21
  227.6 6.4 %collective-permute-done.25.refs_9_ = f32[288,1024]{1,0:T(8,128)} collective-permute-done((f32[288,1024]{1,0:T(8,128)S(1)}, f32[288,1024]{1,0:T(8,128)}, u32[]{:S(2)}, u32[]{:S(2)}) %collective-permute-start.25) | collective-permute-done | bytes 1179680 | tf_op jit(solution)/shard_map/ppermute | solution.py:709
  234.0 1.7 collective-permute-start.22
  235.7 0.8 copy-done.16
  236.5 1.3 collective-permute-start.27
  237.9 1.1 broadcast_select_fusion.5
  239.1 2.2 collective-permute-start.36
  241.3 1.4 broadcast_select_fusion.1
  242.7 3.9 %collective-permute-done.26.refs_10_ = f32[288,1024]{1,0:T(8,128)} collective-permute-done((f32[288,1024]{1,0:T(8,128)}, f32[288,1024]{1,0:T(8,128)}, u32[]{:S(2)}, u32[]{:S(2)}) %collective-permute-start.26) | collective-permute-done | bytes 1179680 | tf_op jit(solution)/shard_map/ppermute | solution.py:709
  246.7 1.4 collective-permute-start.28
  248.0 0.7 collective-permute-start.23
  248.8 1.4 collective-permute-start.29
  250.2 9.1 %collective-permute-done.27.refs_11_ = f32[288,1024]{1,0:T(8,128)} collective-permute-done((f32[288,1024]{1,0:T(8,128)}, f32[288,1024]{1,0:T(8,128)}, u32[]{:S(2)}, u32[]{:S(2)}) %collective-permute-start.27) | collective-permute-done | bytes 1179680 | tf_op jit(solution)/shard_map/ppermute | solution.py:714
  259.3 1.4 collective-permute-start.30
  260.7 1.4 collective-permute-start.31
  262.8 1.8 fusion
  264.6 3.5 %fusion.3.refs_17_ = f32[1024,128]{1,0:T(8,128)S(1)} fusion(f32[1024,1024]{1,0:T(8,128)S(1)} %unpack.1, f32[1024,128]{1,0:T(8,128)S(1)} %fusion), kind=kOutput, calls=%fused_computation.42 | convolution fusion | flops 805306368 | bytes 5242880 | tf_op jit(solution)/shard_map/dot_general | solution.py:739
  268.1 8.7 %finish.1 = (f32[1152,256]{1,0:T(8,128)}, f32[1152,128]{1,0:T(8,128)}) custom-call(s32[2]{0:T(128)S(1)} %pad_add_fusion.where_ref, f32[288,1024]{1,0:T(8,128)S(1)} %copy-done.3, f32[288,1024]{1,0:T(8,128)S(1)} %copy-done.4, f32[288,1024]{1,0:T(8,128)} %get-tuple-element.33.refs_2_, f32[288,1024]{1,0:T(8,128)} %get-tuple-element.37.refs_3_, ...), custom_call_target="tpu_custom_call" | custom-call | tf_op jit(solution)/shard_map/finish/pallas_call | solution.py:576
  (97 shorter events, 7.2 us)
Async XLA Ops:
  0.6 1.6 copy-start.1
  2.2 0.7 copy-start.5
  2.9 0.7 copy-start.7
  3.5 21.7 %copy-start.2 = (f32[128,4096]{1,0:T(8,128)S(1)}, f32[128,4096]{1,0:T(8,128)}, u32[]{:S(2)}) copy-start(f32[128,4096]{1,0:T(8,128)} %tiles_ref.3) | copy-start | bytes 6291460
  3.5 21.7 %copy-start.6 = (s32[128]{0:T(128)S(1)}, s32[128]{0:T(128)}, u32[]{:S(2)}) copy-start(s32[128]{0:T(128)} %target_ref.2) | copy-start | bytes 1540
  3.5 21.7 %copy-start.8 = (s32[4]{0:T(128)S(1)}, s32[4]{0:T(128)}, u32[]{:S(2)}) copy-start(s32[4]{0:T(128)} %tally_ref.1) | copy-start | bytes 52
  7.2 6.5 %collective-permute-start = (f32[136,128]{1,0:T(8,128)S(1)}, f32[136,128]{1,0:T(8,128)S(1)}, u32[]{:S(2)}, u32[]{:S(2)}) collective-permute-start(f32[136,128]{1,0:T(8,128)S(1)} %pick.1), channel_id=1, source_target_pairs={{1,0},{3,2},{5,4},{7,6}} | collective-permute-start | bytes 208904 | tf_op jit(solution)/shard_map/ppermute | solution.py:632
  8.5 6.5 %collective-permute-start.1 = (f32[136,128]{1,0:T(8,128)S(1)}, f32[136,128]{1,0:T(8,128)S(1)}, u32[]{:S(2)}, u32[]{:S(2)}) collective-permute-start(f32[136,128]{1,0:T(8,128)S(1)} %pick.1), channel_id=1, source_target_pairs={{8,0},{10,2},{12,4},{14,6}} | collective-permute-start | bytes 208904 | tf_op jit(solution)/shard_map/ppermute | solution.py:632
  9.8 6.6 %collective-permute-start.2 = (f32[136,128]{1,0:T(8,128)S(1)}, f32[136,128]{1,0:T(8,128)S(1)}, u32[]{:S(2)}, u32[]{:S(2)}) collective-permute-start(f32[136,128]{1,0:T(8,128)S(1)} %pick.1), channel_id=1, source_target_pairs={{9,0},{11,2},{13,4},{15,6}} | collective-permute-start | bytes 208904 | tf_op jit(solution)/shard_map/ppermute | solution.py:632
  11.1 7.2 %collective-permute-start.3 = (f32[136,128]{1,0:T(8,128)S(1)}, f32[136,128]{1,0:T(8,128)S(1)}, u32[]{:S(2)}, u32[]{:S(2)}) collective-permute-start(f32[136,128]{1,0:T(8,128)S(1)} %pick.1), channel_id=1, source_target_pairs={{16,0},{18,2},{20,4},{22,6}} | collective-permute-start | bytes 208904 | tf_op jit(solution)/shard_map/ppermute | solution.py:632
  12.4 6.5 %collective-permute-start.4 = (f32[136,128]{1,0:T(8,128)S(1)}, f32[136,128]{1,0:T(8,128)S(1)}, u32[]{:S(2)}, u32[]{:S(2)}) collective-permute-start(f32[136,128]{1,0:T(8,128)S(1)} %pick.1), channel_id=1, source_target_pairs={{17,0},{19,2},{21,4},{23,6}} | collective-permute-start | bytes 208904 | tf_op jit(solution)/shard_map/ppermute | solution.py:632
  13.7 8.0 %collective-permute-start.5 = (f32[136,128]{1,0:T(8,128)S(1)}, f32[136,128]{1,0:T(8,128)S(1)}, u32[]{:S(2)}, u32[]{:S(2)}) collective-permute-start(f32[136,128]{1,0:T(8,128)S(1)} %pick.1), channel_id=1, source_target_pairs={{24,0},{26,2},{28,4},{30,6}} | collective-permute-start | bytes 208904 | tf_op jit(solution)/shard_map/ppermute | solution.py:632
  15.0 7.4 %collective-permute-start.6 = (f32[136,128]{1,0:T(8,128)S(1)}, f32[136,128]{1,0:T(8,128)S(1)}, u32[]{:S(2)}, u32[]{:S(2)}) collective-permute-start(f32[136,128]{1,0:T(8,128)S(1)} %pick.1), channel_id=1, source_target_pairs={{25,0},{27,2},{29,4},{31,6}} | collective-permute-start | bytes 208904 | tf_op jit(solution)/shard_map/ppermute | solution.py:632
  22.5 16.0 %collective-permute-start.7 = (f32[1088,128]{1,0:T(8,128)S(1)}, f32[1088,128]{1,0:T(8,128)S(1)}, u32[]{:S(2)}, u32[]{:S(2)}) collective-permute-start(f32[1088,128]{1,0:T(8,128)S(1)} %constant_dynamic-update-slice_fusion), channel_id=1, source_target_pairs={{2,0}} | collective-permute-start | bytes 1671176 | tf_op jit(solution)/shard_map/ppermute | solution.py:636
  23.8 14.7 %collective-permute-start.8 = (f32[1088,128]{1,0:T(8,128)S(1)}, f32[1088,128]{1,0:T(8,128)S(1)}, u32[]{:S(2)}, u32[]{:S(2)}) collective-permute-start(f32[1088,128]{1,0:T(8,128)S(1)} %constant_dynamic-update-slice_fusion), channel_id=1, source_target_pairs={{4,0}} | collective-permute-start | bytes 1671176 | tf_op jit(solution)/shard_map/ppermute | solution.py:636
  24.5 13.9 %collective-permute-start.9 = (f32[1088,128]{1,0:T(8,128)S(1)}, f32[1088,128]{1,0:T(8,128)S(1)}, u32[]{:S(2)}, u32[]{:S(2)}) collective-permute-start(f32[1088,128]{1,0:T(8,128)S(1)} %constant_dynamic-update-slice_fusion), channel_id=1, source_target_pairs={{6,0}} | collective-permute-start | bytes 1671176 | tf_op jit(solution)/shard_map/ppermute | solution.py:636
  36.4 2.1 copy-start
  38.6 4.1 %copy-start.12 = (f32[4352,128]{1,0:T(8,128)}, f32[4352,128]{1,0:T(8,128)S(1)}, u32[]{:S(2)}) copy-start(f32[4352,128]{1,0:T(8,128)S(1)} %pad_maximum_fusion.1.tiles_ref) | copy-start | bytes 6684676
  38.6 100.4 %all-to-all-start = ((f32[32,264,128]{2,1,0:T(8,128)}), f32[32,264,128]{2,1,0:T(8,128)}, u32[]{:S(2)}, u32[]{:S(2)}) async-start(f32[32,264,128]{2,1,0:T(8,128)} %bitcast.16), calls=%async_computation | async-start | bytes 8650752 | tf_op jit(solution)/shard_map/all_to_all | solution.py:684
  46.4 3.2 %copy-start.11 = (f32[4608,128]{1,0:T(8,128)S(1)}, f32[4608,128]{1,0:T(8,128)}, u32[]{:S(2)}) copy-start(f32[4608,128]{1,0:T(8,128)} %factor.1) | copy-start | bytes 7077892
  47.9 1.7 collective-permute-start.10
  49.8 0.7 collective-permute-start.11
  50.6 0.7 collective-permute-start.12
  51.4 0.7 collective-permute-start.13
  52.1 85.8 %collective-permute-start.14 = (f32[144,128]{1,0:T(8,128)S(1)}, f32[144,128]{1,0:T(8,128)S(1)}, u32[]{:S(2)}, u32[]{:S(2)}) collective-permute-start(f32[144,128]{1,0:T(8,128)S(1)} %slice.83), channel_id=1, source_target_pairs={{0,2},{1,3},{4,6},{5,7},{8,10},{9,11},{12,14},{13,15},{16,18},{17,... | collective-permute-start | bytes 221192 | tf_op jit(solution)/shard_map/ppermute | solution.py:644
  165.6 4.8 %collective-permute-start.15 = (f32[2304,128]{1,0:T(8,128)S(1)}, f32[2304,128]{1,0:T(8,128)S(1)}, u32[]{:S(2)}, u32[]{:S(2)}) collective-permute-start(f32[2304,128]{1,0:T(8,128)S(1)} %bitcast.18), channel_id=1, source_target_pairs={{0,1},{1,0},{2,3},{3,2},{4,5},{5,4},{6,7},{7,6},{8,9},{9,8},{10,11... | collective-permute-start | bytes 3538952 | tf_op jit(solution)/shard_map/ppermute | solution.py:595
  165.7 4.7 %collective-permute-start.16 = (f32[144,128]{1,0:T(8,128)S(1)}, f32[144,128]{1,0:T(8,128)S(1)}, u32[]{:S(2)}, u32[]{:S(2)}) collective-permute-start(f32[144,128]{1,0:T(8,128)S(1)} %slice_select_fusion.7), channel_id=1, source_target_pairs={{0,2},{1,3},{2,0},{3,1},{4,6},{5,7},{6,4},{7,5},{8,10},{9,11},{10,... | collective-permute-start | bytes 221192 | tf_op jit(solution)/shard_map/ppermute | solution.py:595
  170.6 16.6 %copy-start.9 = (f32[2304,128]{1,0:T(8,128)}, f32[2304,128]{1,0:T(8,128)S(1)}, u32[]{:S(2)}) copy-start(f32[2304,128]{1,0:T(8,128)S(1)} %bitcast_add_fusion) | copy-start | bytes 3538948
  170.6 6.4 %collective-permute-start.18 = (f32[288,128]{1,0:T(8,128)S(1)}, f32[288,128]{1,0:T(8,128)S(1)}, u32[]{:S(2)}, u32[]{:S(2)}) collective-permute-start(f32[288,128]{1,0:T(8,128)S(1)} %pad_maximum_fusion.5), channel_id=1, source_target_pairs={{0,16},{1,17},{2,18},{3,19},{4,20},{5,21},{6,22},{7,23},{8,24},{9,... | collective-permute-start | bytes 442376 | tf_op jit(solution)/shard_map/ppermute | solution.py:595
  177.0 16.4 %collective-permute-start.19 = (f32[576,128]{1,0:T(8,128)S(1)}, f32[576,128]{1,0:T(8,128)S(1)}, u32[]{:S(2)}, u32[]{:S(2)}) collective-permute-start(f32[576,128]{1,0:T(8,128)S(1)} %pad_maximum_fusion.4), channel_id=1, source_target_pairs={{0,8},{1,9},{2,10},{3,11},{4,12},{5,13},{6,14},{7,15},{8,0},{9,1},... | collective-permute-start | bytes 884744 | tf_op jit(solution)/shard_map/ppermute | solution.py:595
  187.2 14.1 %collective-permute-start.17 = (f32[1152,128]{1,0:T(8,128)S(1)}, f32[1152,128]{1,0:T(8,128)S(1)}, u32[]{:S(2)}, u32[]{:S(2)}) collective-permute-start(f32[1152,128]{1,0:T(8,128)S(1)} %slice_select_fusion.4), channel_id=1, source_target_pairs={{0,2},{1,3},{2,0},{3,1},{4,6},{5,7},{6,4},{7,5},{8,10},{9,11},{10,... | collective-permute-start | bytes 1769480 | tf_op jit(solution)/shard_map/ppermute | solution.py:595
  187.7 13.6 %copy-start.10 = (f32[2304,128]{1,0:T(8,128)S(1)}, f32[2304,128]{1,0:T(8,128)}, u32[]{:S(2)}) copy-start(f32[2304,128]{1,0:T(8,128)} %copy-done.9) | copy-start | bytes 3538948
  193.5 9.7 %copy-start.3 = (f32[288,1024]{1,0:T(8,128)S(1)}, f32[288,1024]{1,0:T(8,128)}, u32[]{:S(2)}) copy-start(f32[288,1024]{1,0:T(8,128)} %get-tuple-element.26.refs_0_) | copy-start | bytes 3538948
  193.5 12.7 %copy-start.4 = (f32[288,1024]{1,0:T(8,128)S(1)}, f32[288,1024]{1,0:T(8,128)}, u32[]{:S(2)}) copy-start(f32[288,1024]{1,0:T(8,128)} %get-tuple-element.32.refs_1_) | copy-start | bytes 3538948
  201.4 13.2 %collective-permute-start.32 = (f32[1152,128]{1,0:T(8,128)S(1)}, f32[1152,128]{1,0:T(8,128)S(1)}, u32[]{:S(2)}, u32[]{:S(2)}) collective-permute-start(f32[1152,128]{1,0:T(8,128)S(1)} %pad_maximum_fusion.3), channel_id=1, source_target_pairs={{0,4},{1,5},{2,6},{3,7},{4,0},{5,1},{6,2},{7,3},{8,12},{9,13},{10,... | collective-permute-start | bytes 1769480 | tf_op jit(solution)/shard_map/ppermute | solution.py:595
  203.2 21.4 %collective-permute-start.24 = (f32[288,1024]{1,0:T(8,128)S(1)}, f32[288,1024]{1,0:T(8,128)}, u32[]{:S(2)}, u32[]{:S(2)}) collective-permute-start(f32[288,1024]{1,0:T(8,128)S(1)} %copy-done.3), channel_id=1, source_target_pairs={{0,2},{4,6},{8,10},{12,14},{16,18},{20,22},{24,26},{28,30}} | collective-permute-start | bytes 3538952 | tf_op jit(solution)/shard_map/ppermute | solution.py:704
  204.5 21.4 %collective-permute-start.20 = (f32[288,1024]{1,0:T(8,128)S(1)}, f32[288,1024]{1,0:T(8,128)}, u32[]{:S(2)}, u32[]{:S(2)}) collective-permute-start(f32[288,1024]{1,0:T(8,128)S(1)} %copy-done.3), channel_id=1, source_target_pairs={{0,1},{4,5},{8,9},{12,13},{16,17},{20,21},{24,25},{28,29}} | collective-permute-start | bytes 3538952 | tf_op jit(solution)/shard_map/ppermute | solution.py:735
  206.2 27.8 %collective-permute-start.25 = (f32[288,1024]{1,0:T(8,128)S(1)}, f32[288,1024]{1,0:T(8,128)}, u32[]{:S(2)}, u32[]{:S(2)}) collective-permute-start(f32[288,1024]{1,0:T(8,128)S(1)} %copy-done.4), channel_id=1, source_target_pairs={{0,2},{4,6},{8,10},{12,14},{16,18},{20,22},{24,26},{28,30}} | collective-permute-start | bytes 3538952 | tf_op jit(solution)/shard_map/ppermute | solution.py:709
  208.3 14.9 %collective-permute-start.34 = (f32[1024,128]{1,0:T(8,128)}, f32[1024,128]{1,0:T(8,128)}, u32[]{:S(2)}, u32[]{:S(2)}) collective-permute-start(f32[1024,128]{1,0:T(8,128)} %slice.73), channel_id=1, source_target_pairs={{0,16},{1,17},{2,18},{3,19}} | collective-permute-start | bytes 1572872 | tf_op jit(solution)/shard_map/ppermute | solution.py:624
  214.7 1.2 copy-start.13
  215.9 23.2 %collective-permute-start.33 = (f32[2304,128]{1,0:T(8,128)}, f32[2304,128]{1,0:T(8,128)}, u32[]{:S(2)}, u32[]{:S(2)}) collective-permute-start(f32[2304,128]{1,0:T(8,128)} %pad_maximum_fusion.2), channel_id=1, source_target_pairs={{0,1},{1,0},{2,3},{3,2},{4,5},{5,4},{6,7},{7,6},{8,9},{9,8},{10,11... | collective-permute-start | bytes 3538952 | tf_op jit(solution)/shard_map/ppermute | solution.py:595
  223.2 10.8 %copy-start.15 = (f32[1024,128]{1,0:T(8,128)}, f32[1024,128]{1,0:T(8,128)S(1)}, u32[]{:S(2)}) copy-start(f32[1024,128]{1,0:T(8,128)S(1)} %broadcast_select_fusion.4) | copy-start | bytes 1572868
  223.3 12.5 %collective-permute-start.35 = (f32[1024,128]{1,0:T(8,128)S(1)}, f32[1024,128]{1,0:T(8,128)S(1)}, u32[]{:S(2)}, u32[]{:S(2)}) collective-permute-start(f32[1024,128]{1,0:T(8,128)S(1)} %broadcast_select_fusion.4), channel_id=1, source_target_pairs={{0,8},{16,24},{1,9},{17,25},{2,10},{18,26},{3,11},{19,27}} | collective-permute-start | bytes 1572872 | tf_op jit(solution)/shard_map/ppermute | solution.py:624
  224.6 22.1 %collective-permute-start.26 = (f32[288,1024]{1,0:T(8,128)}, f32[288,1024]{1,0:T(8,128)}, u32[]{:S(2)}, u32[]{:S(2)}) collective-permute-start(f32[288,1024]{1,0:T(8,128)} %get-tuple-element.33.refs_2_), channel_id=1, source_target_pairs={{0,2},{4,6},{8,10},{12,14},{16,18},{20,22},{24,26},{28,30}} | collective-permute-start | bytes 3538952 | tf_op jit(solution)/shard_map/ppermute | solution.py:709
  225.9 22.1 %collective-permute-start.21 = (f32[288,1024]{1,0:T(8,128)S(1)}, f32[288,1024]{1,0:T(8,128)}, u32[]{:S(2)}, u32[]{:S(2)}) collective-permute-start(f32[288,1024]{1,0:T(8,128)S(1)} %copy-done.4), channel_id=1, source_target_pairs={{0,1},{4,5},{8,9},{12,13},{16,17},{20,21},{24,25},{28,29}} | collective-permute-start | bytes 3538952 | tf_op jit(solution)/shard_map/ppermute | solution.py:735
  234.0 14.8 %collective-permute-start.22 = (f32[288,1024]{1,0:T(8,128)}, f32[288,1024]{1,0:T(8,128)}, u32[]{:S(2)}, u32[]{:S(2)}) collective-permute-start(f32[288,1024]{1,0:T(8,128)} %get-tuple-element.33.refs_2_), channel_id=1, source_target_pairs={{0,1},{4,5},{8,9},{12,13},{16,17},{20,21},{24,25},{28,29}} | collective-permute-start | bytes 3538952 | tf_op jit(solution)/shard_map/ppermute | solution.py:735
  235.7 0.8 copy-start.16
  236.5 22.8 %collective-permute-start.27 = (f32[288,1024]{1,0:T(8,128)}, f32[288,1024]{1,0:T(8,128)}, u32[]{:S(2)}, u32[]{:S(2)}) collective-permute-start(f32[288,1024]{1,0:T(8,128)} %get-tuple-element.37.refs_3_), channel_id=1, source_target_pairs={{0,2},{4,6},{8,10},{12,14},{16,18},{20,22},{24,26},{28,30}} | collective-permute-start | bytes 3538952 | tf_op jit(solution)/shard_map/ppermute | solution.py:714
  237.8 3.5 %copy-start.14 = (f32[1152,128]{1,0:T(8,128)S(1)}, f32[1152,128]{1,0:T(8,128)}, u32[]{:S(2)}) copy-start(f32[1152,128]{1,0:T(8,128)} %copy-done.13) | copy-start | bytes 1769476
  239.1 21.6 %collective-permute-start.36 = (f32[1024,128]{1,0:T(8,128)S(1)}, f32[1024,128]{1,0:T(8,128)S(1)}, u32[]{:S(2)}, u32[]{:S(2)}) collective-permute-start(f32[1024,128]{1,0:T(8,128)S(1)} %broadcast_select_fusion.5), channel_id=1, source_target_pairs={{0,4},{8,12},{16,20},{24,28},{1,5},{9,13},{17,21},{25,29},{2,6},{1... | collective-permute-start | bytes 1572872 | tf_op jit(solution)/shard_map/ppermute | solution.py:624
  246.7 21.4 %collective-permute-start.28 = (f32[288,1024]{1,0:T(8,128)}, f32[288,1024]{1,0:T(8,128)S(1)}, u32[]{:S(2)}, u32[]{:S(2)}) collective-permute-start(f32[288,1024]{1,0:T(8,128)} %collective-permute-done.24.refs_8_), channel_id=1, source_target_pairs={{2,3},{6,7},{10,11},{14,15},{18,19},{22,23},{26,27},{30,31}} | collective-permute-start | bytes 3538952 | tf_op jit(solution)/shard_map/ppermute | solution.py:735
  248.0 20.0 %collective-permute-start.23 = (f32[288,1024]{1,0:T(8,128)}, f32[288,1024]{1,0:T(8,128)S(1)}, u32[]{:S(2)}, u32[]{:S(2)}) collective-permute-start(f32[288,1024]{1,0:T(8,128)} %get-tuple-element.37.refs_3_), channel_id=1, source_target_pairs={{0,1},{4,5},{8,9},{12,13},{16,17},{20,21},{24,25},{28,29}} | collective-permute-start | bytes 3538952 | tf_op jit(solution)/shard_map/ppermute | solution.py:735
  248.8 19.3 %collective-permute-start.29 = (f32[288,1024]{1,0:T(8,128)}, f32[288,1024]{1,0:T(8,128)S(1)}, u32[]{:S(2)}, u32[]{:S(2)}) collective-permute-start(f32[288,1024]{1,0:T(8,128)} %collective-permute-done.25.refs_9_), channel_id=1, source_target_pairs={{2,3},{6,7},{10,11},{14,15},{18,19},{22,23},{26,27},{30,31}} | collective-permute-start | bytes 3538952 | tf_op jit(solution)/shard_map/ppermute | solution.py:735
  259.3 8.8 %collective-permute-start.30 = (f32[288,1024]{1,0:T(8,128)}, f32[288,1024]{1,0:T(8,128)S(1)}, u32[]{:S(2)}, u32[]{:S(2)}) collective-permute-start(f32[288,1024]{1,0:T(8,128)} %collective-permute-done.26.refs_10_), channel_id=1, source_target_pairs={{2,3},{6,7},{10,11},{14,15},{18,19},{22,23},{26,27},{30,31}} | collective-permute-start | bytes 3538952 | tf_op jit(solution)/shard_map/ppermute | solution.py:735
  260.7 7.4 %collective-permute-start.31 = (f32[288,1024]{1,0:T(8,128)}, f32[288,1024]{1,0:T(8,128)S(1)}, u32[]{:S(2)}, u32[]{:S(2)}) collective-permute-start(f32[288,1024]{1,0:T(8,128)} %collective-permute-done.27.refs_11_), channel_id=1, source_target_pairs={{2,3},{6,7},{10,11},{14,15},{18,19},{22,23},{26,27},{30,31}} | collective-permute-start | bytes 3538952 | tf_op jit(solution)/shard_map/ppermute | solution.py:735
